TPU v7x, 256 devices: a whole 4x4x8 slice. The times are simulated.
256 devices in a mesh: dp: 32 (over z, x), passage: 8 (over y, core).
Axes of the slice: x: 4, y: 4, z: 8, core: 2. Of those that a mesh axis runs over, the one named last changes fastest.
Arguments:
- queries: bfloat16 [32, 256, 1024], P('dp'), may hold values from -300 to 300
- key_rows: bfloat16 [32, 4096, 1024], P('dp', 'passage'), may hold values from -20 to 20
- value_rows: bfloat16 [32, 4096, 1024], P('dp', 'passage'), may hold values from -6 to 6
- encoded: bfloat16 [32, 4096, 2048], P('dp', 'passage'), may hold values from -6 to 6
- key_weight: bfloat16 [2048, 1024], P('dp'), may hold values from -0.125 to 0.125
- value_weight: bfloat16 [2048, 1024], P('dp'), may hold values from -0.125 to 0.125
- grad_out: bfloat16 [32, 256, 1024], P('dp'), may hold values from -6 to 6
- lengths: int32 [32], P('dp'), may hold values from 64 to 256, as said below
Outputs:
- query_grad: bfloat16 [32, 256, 1024], P('dp', None, 'passage')
- encoded_grad: bfloat16 [32, 4096, 2048], P('dp', 'passage')
- key_weight_grad: float32 [2048, 1024], P(('dp', 'passage'))
- value_weight_grad: float32 [2048, 1024], P(('dp', 'passage'))
Inputs may be any that keep to these rules, and one draw needn't show every extreme that they name: `lengths`: the first question's answer has all 256 tokens.
All inputs are finite; a program needn't handle non-finite values.
Results may differ from a plain program's by a relative error of at most 0.0065.
Values may be sent and summed in bfloat16 or wider, within the bound.
No kernel may reach another device: no remote copies, remote signals or barrier semaphores. Data moves between devices by JAX's collectives and lax.ppermute only.
A program may use at most 128 MiB of HBM per device.

v0:
```python
import math

import jax
import jax.numpy as jnp
from jax import lax
from jax.sharding import PartitionSpec as P

HEADS = 16
HEAD_DIM = 64


def on_device(queries, key_rows, value_rows, encoded, key_weight, value_weight, grad_out, lengths):
    questions, answer, features = queries.shape
    local_keys = key_rows.shape[1]
    width = encoded.shape[2]
    score_scale = 1.0 / math.sqrt(HEAD_DIM)
    positions = lax.broadcasted_iota(jnp.int32, (questions, answer), 1)
    live_rows = (positions < lengths[:, None]).astype(jnp.bfloat16)
    masked = grad_out * live_rows[:, :, None]
    query_heads = queries.reshape(questions, answer, HEADS, HEAD_DIM)
    key_heads = key_rows.reshape(questions, local_keys, HEADS, HEAD_DIM)
    value_heads = value_rows.reshape(questions, local_keys, HEADS, HEAD_DIM)
    grad_heads = masked.reshape(questions, answer, HEADS, HEAD_DIM)
    scores = (
        jnp.einsum("bihe,bjhe->bhij", query_heads, key_heads, preferred_element_type=jnp.float32)
        * score_scale
    )
    prob_grad = jnp.einsum(
        "bihe,bjhe->bhij", grad_heads, value_heads, preferred_element_type=jnp.float32
    )
    local_max = jnp.max(scores, axis=-1)
    row_max = lax.pmax(local_max, "passage")
    expo = jnp.exp(scores - row_max[..., None])
    row_total = lax.psum(jnp.sum(expo, axis=-1), "passage")
    prob = expo / row_total[..., None]
    row_delta = lax.psum(jnp.sum(prob * prob_grad, axis=-1), "passage")
    prob_low = prob.astype(jnp.bfloat16)
    score_grad = (prob * (prob_grad - row_delta[..., None]) * score_scale).astype(jnp.bfloat16)
    query_terms = jnp.einsum(
        "bhij,bjhe->bihe", score_grad, key_heads, preferred_element_type=jnp.float32
    )
    query_terms = query_terms.reshape(questions, answer, features)
    query_grad = lax.psum_scatter(query_terms, "passage", scatter_dimension=2, tiled=True).astype(
        jnp.bfloat16
    )
    key_grad = jnp.einsum(
        "bhij,bihe->bjhe", score_grad, query_heads, preferred_element_type=jnp.float32
    ).astype(jnp.bfloat16)
    value_grad = jnp.einsum(
        "bhij,bihe->bjhe", prob_low, grad_heads, preferred_element_type=jnp.float32
    ).astype(jnp.bfloat16)
    both_grads = jnp.stack(
        [key_grad.reshape(-1, features), value_grad.reshape(-1, features)], axis=1
    )
    stacked = jnp.stack([key_weight, value_weight], axis=0)
    encoded_grad = jnp.einsum(
        "ksf,sdf->kd",
        both_grads,
        lax.all_gather(stacked, "dp", axis=1, tiled=True),
        preferred_element_type=jnp.float32,
    )
    encoded_grad = encoded_grad.astype(jnp.bfloat16).reshape(questions, local_keys, width)
    encoder_flat = encoded.reshape(-1, width)
    joined = both_grads.reshape(-1, 2 * features)
    reduced = lax.psum_scatter(
        jnp.einsum("kd,kf->df", encoder_flat, joined, preferred_element_type=jnp.float32),
        ("dp", "passage"),
        scatter_dimension=0,
        tiled=True,
    )
    return (query_grad, encoded_grad, reduced[:, :features], reduced[:, features:])


def solution(mesh):
    return jax.shard_map(
        on_device,
        mesh=mesh,
        in_specs=(
            P("dp", None, None),
            P("dp", "passage", None),
            P("dp", "passage", None),
            P("dp", "passage", None),
            P("dp", None),
            P("dp", None),
            P("dp", None, None),
            P("dp"),
        ),
        out_specs=(
            P("dp", None, "passage"),
            P("dp", "passage", None),
            P(("dp", "passage"), None),
            P(("dp", "passage"), None),
        ),
        check_vma=False,
    )
```

profile of v0, /device:TPU:1, one launch (start us, length us, event | category | flops | bytes accessed | tf_op | source)
XLA Modules:
  0.0 1483.0 jit_solution(15641762026467439810)
XLA Ops:
  8.0 0.0 copy-start
  8.0 0.0 reduce-scatter.5.cloned.1.call-start
  8.9 2.0 copy.34
  10.9 2.1 copy.36
  13.0 1.5 copy.35
  14.5 2.3 copy.37
  16.8 5.6 multiply_reduce_fusion.1
  22.3 23.8 %pmax.7 = f32[16,256]{1,0:T(8,128)S(1)} all-reduce(f32[16,256]{1,0:T(8,128)S(1)} %get-tuple-element.18), channel_id=1, replica_groups=mesh['dp'=32,'passage'=8] {'passage'}, use_global_device_ids=true, to_apply=%region_1.0 | all-reduce | flops 4096 | bytes 32768 | tf_op jit(solution)/shard_map/pmax | solution.py:32
  46.1 4.4 fusion.1
  50.6 23.6 %psum.14 = f32[16,256]{1,0:T(8,128)S(1)} all-reduce(f32[16,256]{1,0:T(8,128)S(1)} %fusion.1), channel_id=1, replica_groups=mesh['dp'=32,'passage'=8] {'passage'}, use_global_device_ids=true, to_apply=%region_3.0 | all-reduce | flops 4096 | bytes 32768 | tf_op jit(solution)/shard_map/psum | solution.py:34
  74.1 1.1 broadcast_multiply_fusion
  75.2 0.0 copy-start.5
  75.2 7.7 multiply_reduce_fusion
  83.0 0.0 copy-done.5
  83.0 23.5 %psum.15 = f32[16,256]{1,0:T(8,128)S(1)} all-reduce(f32[16,256]{1,0:T(8,128)S(1)} %get-tuple-element.20), channel_id=1, replica_groups=mesh['dp'=32,'passage'=8] {'passage'}, use_global_device_ids=true, to_apply=%region_5.0 | all-reduce | flops 4096 | bytes 32768 | tf_op jit(solution)/shard_map/psum | solution.py:36
  106.5 7.2 multiply_convert_fusion
  113.8 0.0 copy-start.1
  113.8 2.0 copy-done.1
  115.7 0.0 copy-start.6
  115.8 0.0 copy-start.7
  115.8 2.4 fusion.11
  118.1 2.5 copy.38
  120.7 0.0 reduce-scatter.5.cloned.1.call-update
  120.7 0.0 all-gather.2.cloned.1.call-start
  120.7 0.0 copy-done.6
  120.8 0.0 copy-done.7
  120.8 0.7 pad_maximum_fusion.1
  121.5 0.0 all-gather.2.cloned.1.call-update
  121.5 0.0 copy-start.2
  121.5 0.2 reduce-scatter.7.cloned.1.call-start
  121.7 5.9 fusion.6
  127.7 2.3 copy.40
  130.0 0.0 copy-done.2
  130.0 4.0 convolution_convert_fusion
  134.0 1.5 copy.39
  135.5 0.0 copy-start.4
  135.5 3.1 pad_maximum_fusion
  138.6 4.0 copy.41
  142.6 0.0 copy-done
  142.6 9.8 convolution_bitcast_fusion
  152.4 0.0 copy-done.4
  152.4 17.7 %copy.44 = f32[2048,2048]{1,0:T(8,128)} copy(f32[2048,2048]{0,1:T(8,128)} %convolution_bitcast_fusion) | data formatting | bytes 33554432
  170.0 0.0 copy-start.3
  170.0 0.0 reduce-scatter.7.cloned.1.call-update
  170.1 0.0 reduce-scatter.5.cloned.1.call-done
  170.1 1.6 convert_element_type.46
  171.7 53.0 %all-gather.2.cloned.1.call-done = bf16[2,2048,1024]{2,1,0:T(8,128)(2,1)} async-done(((bf16[2,64,1024]{2,1,0:T(8,128)(2,1)}), bf16[2,2048,1024]{2,1,0:T(8,128)(2,1)}) %all-gather.2.cloned.1.call-update) | async-done | bytes 8388624 | tf_op jit(solution)/shard_map/all_gather | solution.py:59
  224.7 0.0 copy-done.3
  224.7 9.6 fusion.4
  234.3 1239.9 %reduce-scatter.7.cloned.1.call-done = f32[8,2048]{1,0:T(8,128)} async-done(((f32[2048,2048]{1,0:T(8,128)}), f32[8,2048]{1,0:T(8,128)}) %reduce-scatter.7.cloned.1.call-update) | async-done | bytes 65552
  1474.2 1.4 fusion.10
  (1 shorter events, 0.0 us)
Async XLA Ops:
  8.0 134.6 %copy-start = (bf16[1,512,2048]{2,1,0:T(8,128)(2,1)S(1)}, bf16[1,512,2048]{2,1,0:T(8,128)(2,1)}, u32[]{:S(2)}) copy-start(bf16[1,512,2048]{2,1,0:T(8,128)(2,1)} %param.11) | copy-start | bytes 6291460
  8.0 162.1 %reduce-scatter.5.cloned.1.call-start = ((), (), s32[]{:S(2)}) async-start(), calls=%async_computation.2 | async-start | bytes 1179648 | tf_op jit(solution)/shard_map/reduce_scatter | solution.py:43
  75.2 7.8 copy-start.5
  113.8 2.0 copy-start.1
  115.7 5.0 copy-start.6
  115.8 5.0 copy-start.7
  120.7 104.0 %all-gather.2.cloned.1.call-start = ((), (), s32[]{:S(2)}) async-start(), calls=%async_computation.3 | async-start | bytes 8650752 | tf_op jit(solution)/shard_map/all_gather | solution.py:59
  121.5 8.5 copy-start.2
  121.5 1352.7 %reduce-scatter.7.cloned.1.call-start = ((), (), s32[]{:S(2)}) async-start(), calls=%async_computation.4 | async-start | bytes 16842752
  135.5 16.9 %copy-start.4 = (bf16[512,1,1024]{2,0,1:T(8,128)(2,1)}, bf16[512,1,1024]{2,0,1:T(8,128)(2,1)S(1)}, u32[]{:S(2)}) copy-start(bf16[512,1,1024]{2,0,1:T(8,128)(2,1)S(1)} %copy.39) | copy-start | bytes 3145732
  170.0 54.6 %copy-start.3 = (bf16[512,1,1024]{2,0,1:T(8,128)(2,1)S(1)}, bf16[512,1,1024]{2,0,1:T(8,128)(2,1)}, u32[]{:S(2)}) copy-start(bf16[512,1,1024]{2,0,1:T(8,128)(2,1)} %copy.40) | copy-start | bytes 3145732
Sparse Core Ops, SparseCore 0:
  120.8 35.6 reduce-scatter.4
  170.2 1303.9 reduce-scatter.6
Sparse Core Ops, SparseCore 1:
  123.8 100.9 all-gather.1
where the time goes:
time: 1490 us; the launch traced here: 1480 us
  waiting for transfers between devices  1290 us (87%)
  blocking collectives  70.9 us (5%)
  matrix products  44.9 us (3%)
  local copies, waits for them, and re-layouts  39.3 us (3%)
  other arithmetic  18.2 us (1%)
  between operations  16.4 us (1%)
    unnamed x4, waiting for transfers between devices  1240 us
    all_gather x1, waiting for transfers between devices, on_device(): lax.all_gather(stacked, 'dp', axis=1, tiled=True)  53 us
  transfers between devices with their start and end apart: 3, of which 2 were waited for; matrix products, arithmetic and copies ran while one was open for 4% of the time, Pallas kernels for 0%

commit v1 on v0

v1 whole, which is shorter than its diff:
```python
import functools
import math

import jax
import jax.numpy as jnp
from jax import lax
from jax.experimental import pallas as pl
from jax.experimental.pallas import tpu as pltpu
from jax.sharding import PartitionSpec as P

HEADS = 16
HEAD_DIM = 64
PAIR = 2 * HEAD_DIM
SCALE = 1.0 / math.sqrt(HEAD_DIM)
EXP2_SCALE = SCALE * math.log2(math.e)
NZ, NX, NY, NC = 8, 4, 4, 2
AXES = ("dp", "passage")
VMEM_LIMIT = 40 * 1024 * 1024


def device_index(z, x, y, c):
    return ((z % NZ) * NX + x % NX) * (NY * NC) + (y % NY) * NC + c % NC


def permutation(target):
    return [
        (device_index(z, x, y, c), device_index(*target(z, x, y, c)))
        for z in range(NZ)
        for x in range(NX)
        for y in range(NY)
        for c in range(NC)
    ]


def groups(key):
    found = {}
    for z in range(NZ):
        for x in range(NX):
            for y in range(NY):
                for c in range(NC):
                    found.setdefault(key(z, x, y, c), []).append(device_index(z, x, y, c))
    return list(found.values())


def swap_cores(value):
    return lax.ppermute(value, AXES, permutation(lambda z, x, y, c: (z, x, y, 1 - c)))


def two_heads(rows):
    lane = lax.broadcasted_iota(jnp.int32, rows.shape, 1)
    wide = rows.astype(jnp.float32)
    first = jnp.where(lane < HEAD_DIM, wide, 0.0)
    second = jnp.where(lane < HEAD_DIM, 0.0, wide)
    return jnp.concatenate([first, second], axis=0).astype(jnp.bfloat16)


def live_grads(length_ref, grad_ref):
    rows = grad_ref[...].astype(jnp.float32)
    position = lax.broadcasted_iota(jnp.int32, rows.shape, 0)
    return two_heads(jnp.where(position < length_ref[0], rows, 0.0))


def dot_last(left, right):
    return lax.dot_general(left, right, (((1,), (1,)), ((), ())), preferred_element_type=jnp.float32)


def stats_kernel(length_ref, query_ref, key_ref, value_ref, grad_ref, out_ref):
    pair = pl.program_id(0)
    scores = dot_last(key_ref[...], two_heads(query_ref[...]))
    prob_grad = dot_last(value_ref[...], live_grads(length_ref, grad_ref))
    peak = jnp.max(scores, axis=0, keepdims=True)
    expo = jnp.exp2((scores - peak) * EXP2_SCALE)
    out_ref[pl.ds(pair, 1), :] = peak
    out_ref[pl.ds(8 + pair, 1), :] = jnp.sum(expo, axis=0, keepdims=True)
    out_ref[pl.ds(16 + pair, 1), :] = jnp.sum(expo * prob_grad, axis=0, keepdims=True)


def grads_kernel(
    length_ref, query_ref, key_ref, value_ref, grad_ref, stats_ref, key_grad_ref, value_grad_ref, query_grad_ref
):
    pair = pl.program_id(0)
    peaks = stats_ref[:, pl.ds(pair, 1), :]
    sums = stats_ref[:, pl.ds(8 + pair, 1), :]
    deltas = stats_ref[:, pl.ds(16 + pair, 1), :]
    peak = jnp.max(peaks, axis=0)
    weight = jnp.exp2((peaks - peak[None]) * EXP2_SCALE)
    total = jnp.sum(sums * weight, axis=0)
    row_delta = jnp.sum(deltas * weight, axis=0) / total
    inverse = 1.0 / total
    key = key_ref[...]
    queries = two_heads(query_ref[...])
    grads = live_grads(length_ref, grad_ref)
    scores = dot_last(key, queries)
    prob_grad = dot_last(value_ref[...], grads)
    prob = jnp.exp2((scores - peak) * EXP2_SCALE) * inverse
    prob_low = prob.astype(jnp.bfloat16)
    score_grad = (prob * (prob_grad - row_delta)).astype(jnp.bfloat16)
    value_grad = jnp.dot(prob_low, grads, preferred_element_type=jnp.float32)
    key_grad = jnp.dot(score_grad, queries, preferred_element_type=jnp.float32)
    key_grad_ref[...] = (key_grad * SCALE).astype(jnp.bfloat16)
    value_grad_ref[...] = value_grad.astype(jnp.bfloat16)
    flipped = key.T
    answer = queries.shape[0] // 2
    query_grad_ref[:HEAD_DIM, :] = SCALE * jnp.dot(
        flipped[:HEAD_DIM], score_grad[:, :answer], preferred_element_type=jnp.float32
    )
    query_grad_ref[HEAD_DIM:, :] = SCALE * jnp.dot(
        flipped[HEAD_DIM:], score_grad[:, answer:], preferred_element_type=jnp.float32
    )


def transpose_kernel(in_ref, out_ref):
    out_ref[...] = in_ref[...].T


def weights_kernel(place_ref, own_ref, other_ref, grad_own_ref, grad_other_ref, *refs):
    outs, total = refs[:-1], refs[-1]
    total[...] = jnp.dot(own_ref[...], grad_own_ref[...], preferred_element_type=jnp.float32) + jnp.dot(
        other_ref[...], grad_other_ref[...], preferred_element_type=jnp.float32
    )
    half = total.shape[1] // 2
    for step in range(NX):
        chosen = lax.rem(place_ref[0] + step, NX)
        rows = total[pl.ds(pl.multiple_of(chosen * 64, 64), 64), :half]
        outs[step][0] = rows.astype(outs[step].dtype)
    for step in range(NY):
        chosen = lax.rem(place_ref[1] + step, NY)
        for x in range(NX):
            rows = total[pl.ds(pl.multiple_of(x * 64 + chosen * 16, 16), 16), half:]
            outs[NX + step][0, x] = rows.astype(outs[NX + step].dtype)


def encoded_kernel(key_ref, value_ref, weight_ref, out_ref):
    half = key_ref.shape[1]
    total = dot_last(key_ref[...], weight_ref[:, :half]) + dot_last(value_ref[...], weight_ref[:, half:])
    out_ref[...] = total.astype(jnp.bfloat16)


def params():
    return pltpu.CompilerParams(vmem_limit_bytes=VMEM_LIMIT)


def cost(flops, moved, exps=0):
    return pl.CostEstimate(flops=flops, bytes_accessed=moved, transcendentals=exps)


def on_device(queries, key_rows, value_rows, encoded, key_weight, value_weight, grad_out, lengths):
    _, answer, features = queries.shape
    keys = key_rows.shape[1]
    width = encoded.shape[2]
    pairs = features // PAIR
    dp, passage = lax.axis_index("dp"), lax.axis_index("passage")
    core = passage % NC
    queries, grad_out = queries[0], grad_out[0]
    key_rows, value_rows, encoded = key_rows[0], value_rows[0], encoded[0]

    weights = lax.all_gather(jnp.concatenate([key_weight, value_weight], axis=1), "dp", axis=0, tiled=True)

    smem = pl.BlockSpec(memory_space=pltpu.SMEM)
    row_spec = pl.BlockSpec((answer, PAIR), lambda p: (0, p))
    key_spec = pl.BlockSpec((keys, PAIR), lambda p: (0, p))
    stats = pl.pallas_call(
        stats_kernel,
        grid=(pairs,),
        in_specs=[smem, row_spec, key_spec, key_spec, row_spec],
        out_specs=pl.BlockSpec((3 * pairs, 2 * answer), lambda p: (0, 0)),
        out_shape=jax.ShapeDtypeStruct((3 * pairs, 2 * answer), jnp.float32),
        compiler_params=params(),
        cost_estimate=cost(4 * answer * keys * features, 4 * 2**20, answer * keys * HEADS),
        name="stats",
    )(lengths, queries, key_rows, value_rows, grad_out)
    others = [
        lax.ppermute(stats, AXES, permutation(lambda z, x, y, c: (z, x, y + dy, c + dc)))
        for dy in range(NY)
        for dc in range(NC)
        if dy or dc
    ]

    flipped = pl.pallas_call(
        transpose_kernel,
        grid=(width // 256,),
        in_specs=[pl.BlockSpec((keys, 256), lambda i: (0, i))],
        out_specs=pl.BlockSpec((256, keys), lambda i: (i, 0)),
        out_shape=jax.ShapeDtypeStruct((width, keys), jnp.bfloat16),
        compiler_params=params(),
        cost_estimate=cost(0, 4 * 2**20),
        name="flip",
    )(encoded)
    flipped_other = swap_cores(flipped)

    all_stats = jnp.stack([stats, *others])
    key_grad, value_grad, query_terms = pl.pallas_call(
        grads_kernel,
        grid=(pairs,),
        in_specs=[
            smem,
            row_spec,
            key_spec,
            key_spec,
            row_spec,
            pl.BlockSpec(all_stats.shape, lambda p: (0, 0, 0)),
        ],
        out_specs=[key_spec, key_spec, pl.BlockSpec((PAIR, answer), lambda p: (p, 0))],
        out_shape=[
            jax.ShapeDtypeStruct((keys, features), jnp.bfloat16),
            jax.ShapeDtypeStruct((keys, features), jnp.bfloat16),
            jax.ShapeDtypeStruct((features, answer), jnp.float32),
        ],
        compiler_params=params(),
        cost_estimate=cost(10 * answer * keys * features, 8 * 2**20, answer * keys * HEADS),
        name="grads",
    )(lengths, queries, key_rows, value_rows, grad_out, all_stats)

    query_grad = lax.psum_scatter(query_terms, "passage", scatter_dimension=0, tiled=True)
    query_grad = query_grad.T.astype(jnp.bfloat16)[None]

    first = core == 0
    mine = jnp.where(first, key_grad, value_grad)
    received = swap_cores(jnp.where(first, value_grad, key_grad))
    place = jnp.stack([dp % NX, passage // NC]).astype(jnp.int32)
    half = features // 2
    x_shape, y_shape = (NZ, 64, half), (NZ, NX, 16, half)
    x_spec = pl.BlockSpec((1, 64, half), lambda i: (i, 0, 0))
    y_spec = pl.BlockSpec((1, NX, 16, half), lambda i: (i, 0, 0, 0))
    whole = pl.BlockSpec((keys, features), lambda i: (0, 0))
    rows = pl.BlockSpec((width // NZ, keys), lambda i: (i, 0))
    kinds = [jnp.float32] + [jnp.bfloat16] * 3
    terms = pl.pallas_call(
        weights_kernel,
        grid=(NZ,),
        in_specs=[smem, rows, rows, whole, whole],
        out_specs=[x_spec] * NX + [y_spec] * NY,
        out_shape=[jax.ShapeDtypeStruct(x_shape, kind) for kind in kinds]
        + [jax.ShapeDtypeStruct(y_shape, kind) for kind in kinds],
        scratch_shapes=[pltpu.VMEM((width // NZ, features), jnp.float32)],
        compiler_params=params(),
        cost_estimate=cost(4 * keys * width * features, 12 * 2**20),
        name="weights",
    )(place, flipped, flipped_other, mine, received)
    x_terms, y_terms = terms[:NX], terms[NX:]
    x_got = [
        lax.ppermute(x_terms[k], AXES, permutation(lambda z, x, y, c: (z, x + k, y, c))) for k in range(1, NX)
    ]
    y_got = [
        lax.ppermute(y_terms[k], AXES, permutation(lambda z, x, y, c: (z, x, y + k, c))) for k in range(1, NY)
    ]
    x_sum = x_terms[0] + sum(t.astype(jnp.float32) for t in x_got)
    y_sum = y_terms[0] + sum(t.astype(jnp.float32) for t in y_got)
    x_sum = x_sum.astype(jnp.bfloat16).reshape(NZ * NY * NC, 8, half)
    y_sum = y_sum.astype(jnp.bfloat16).reshape(NZ * NX * NC, 8, half)
    x_all = lax.all_to_all(
        x_sum, AXES, 0, 0, tiled=True, axis_index_groups=groups(lambda z, x, y, c: x)
    )
    y_all = lax.all_to_all(
        y_sum, AXES, 0, 0, tiled=True, axis_index_groups=groups(lambda z, x, y, c: y)
    )
    x_all = x_all.reshape(NZ * NY, NC, 8, half).astype(jnp.float32).sum(0)
    y_all = y_all.reshape(NZ * NX, NC, 8, half).astype(jnp.float32).sum(0)
    summed = jnp.concatenate([x_all, y_all], axis=2)

    encoded_grad = pl.pallas_call(
        encoded_kernel,
        grid=(width // 256,),
        in_specs=[
            pl.BlockSpec((keys, features), lambda i: (0, 0)),
            pl.BlockSpec((keys, features), lambda i: (0, 0)),
            pl.BlockSpec((256, 2 * features), lambda i: (i, 0)),
        ],
        out_specs=pl.BlockSpec((keys, 256), lambda i: (0, i)),
        out_shape=jax.ShapeDtypeStruct((keys, width), jnp.bfloat16),
        compiler_params=params(),
        cost_estimate=cost(4 * keys * width * features, 12 * 2**20),
        name="encoded",
    )(key_grad, value_grad, weights)
    return query_grad, encoded_grad[None], summed[0], summed[1]


def solution(mesh):
    return jax.shard_map(
        on_device,
        mesh=mesh,
        in_specs=(
            P("dp", None, None),
            P("dp", "passage", None),
            P("dp", "passage", None),
            P("dp", "passage", None),
            P("dp", None),
            P("dp", None),
            P("dp", None, None),
            P("dp"),
        ),
        out_specs=(
            P("dp", None, "passage"),
            P("dp", "passage", None),
            P(("dp", "passage"), None),
            P(("dp", "passage"), None),
        ),
        check_vma=False,
    )
```

time: 1490 us -> 206 us (0.14)
  waiting for transfers between devices: 1290 us -> 95.4 us
  blocking collectives: 70.9 us -> 0 us
  matrix products: 44.9 us -> 0 us
  starting transfers between devices: 0.3 us -> 39.6 us
  Pallas kernels: 0 us -> 31.7 us
  local copies, waits for them, and re-layouts: 39.3 us -> 12.9 us
    unnamed x4 -> x2, waiting for transfers between devices: 1240 us -> 0.03 us
    ppermute x0 -> x15, waiting for transfers between devices: none -> 80.4 us  [the longest x3 48.5 us: on_device(): lax.ppermute(x_terms[k], AXES, permutation(lambda z, x, y, c: (z, x + k,...]
    all_gather x1, waiting for transfers between devices: 53 us -> 0.01 us  [on_device(): lax.all_gather(jnp.concatenate([key_weight, value_weight], axis=1), 'dp',...]
    psum x2 -> x0, blocking collectives: 47.1 us -> none  [the longest x1 23.6 us: on_device(): row_total = lax.psum(jnp.sum(expo, axis=-1), 'passage')]
    dot_general x7 -> x0, matrix products: 44.9 us -> none  [the longest x1 9.76 us: on_device(): jnp.einsum('kd,kf->df', encoder_flat, joined, preferred_element_type=jnp....]
    pallas_call x0 -> x5, Pallas kernels: none -> 31.7 us  [the longest x1 8.51 us: on_device(): pl.pallas_call(weights_kernel, grid=(NZ,), in_specs=[smem, rows, rows, wh...]
    pmax x1 -> x0, blocking collectives: 23.8 us -> none  [on_device(): row_max = lax.pmax(local_max, 'passage')]
    all_to_all x0 -> x2, starting transfers between devices: none -> 20.2 us  [the longest x1 11.8 us: on_device(): lax.all_to_all(y_sum, AXES, 0, 0, tiled=True, axis_index_groups=groups(la...]
  transfers between devices with their start and end apart: 3 -> 19, of which waited for: 2 -> 10; matrix products, arithmetic and copies ran while one was open for 4% -> 4% of each run, Pallas kernels for 0% -> 6%
where the time goes in v1:
time: 206 us; the launch traced here: 204 us
  waiting for transfers between devices  95.4 us (46%)
  starting transfers between devices  39.6 us (19%)
  Pallas kernels  31.7 us (15%)
  between operations  16.3 us (8%)
  local copies, waits for them, and re-layouts  12.9 us (6%)
  other arithmetic  8.15 us (4%)
    ppermute x3, waiting for transfers between devices, on_device(): lax.ppermute(x_terms[k], AXES, permutation(lambda z, x, y, c: (z, x + k,...  48.5 us
    ppermute x3, waiting for transfers between devices, on_device(): lax.ppermute(y_terms[k], AXES, permutation(lambda z, x, y, c: (z, x, y +...  27.2 us
    all_to_all x1, waiting for transfers between devices, on_device(): lax.all_to_all(x_sum, AXES, 0, 0, tiled=True, axis_index_groups=groups(la...  14.9 us
    unnamed x42, local copies, waits for them, and re-layouts  12.9 us
    all_to_all x1, starting transfers between devices, on_device(): lax.all_to_all(y_sum, AXES, 0, 0, tiled=True, axis_index_groups=groups(la...  11.8 us
    ppermute x7, starting transfers between devices, on_device(): lax.ppermute(stats, AXES, permutation(lambda z, x, y, c: (z, x, y + dy, c...  11.4 us
    pallas_call x1, Pallas kernels, on_device(): pl.pallas_call(weights_kernel, grid=(NZ,), in_specs=[smem, rows, rows, wh...  8.51 us
    all_to_all x1, starting transfers between devices, on_device(): lax.all_to_all(x_sum, AXES, 0, 0, tiled=True, axis_index_groups=groups(la...  8.39 us
  transfers between devices with their start and end apart: 19, of which 10 were waited for; matrix products, arithmetic and copies ran while one was open for 4% of the time, Pallas kernels for 6%

profile of v1, /device:TPU:1, one launch (start us, length us, event | category | flops | bytes accessed | tf_op | source)
XLA Modules:
  0.0 204.1 jit_solution(17202905026742777528)
XLA Ops:
  8.0 0.0 reduce-scatter.2.cloned.1.call-start
  8.7 1.2 copy-done.5
  9.9 1.2 copy-done.7
  11.1 1.0 copy-done.10
  12.2 1.0 copy-done.11
  13.2 5.2 %stats.1 = f32[24,512]{1,0:T(8,128)S(1)} custom-call(s32[1]{0:T(128)S(6)} %copy.20.length_ref, bf16[256,1024]{1,0:T(8,128)(2,1)S(1)} %bitcast.43, bf16[512,1024]{1,0:T(8,128)(2,1)S(1)} %bitcast.39, bf16[512,1024]{1,0:T(8,128)(2,1)S(1)} %bitcast.41, bf16[256,1024]{1,0:T(8,128)(2,1)S(1)} %bitcast.45), custom_call_target="tpu_custom_call" | custom-call | flops 536870912 | bytes 4194304 | tf_op jit(solution)/shard_map/stats/pallas_call | solution.py:162
  18.4 3.3 %collective-permute-start = (f32[24,512]{1,0:T(8,128)S(1)}, f32[24,512]{1,0:T(8,128)S(1)}, u32[]{:S(2)}, u32[]{:S(2)}) collective-permute-start(f32[24,512]{1,0:T(8,128)S(1)} %stats.1), channel_id=1, source_target_pairs={{0,1},{1,0},{2,3},{3,2},{4,5},{5,4},{6,7},{7,6},{8,9},{9,8},{10,11... | collective-permute-start | bytes 147464 | tf_op jit(solution)/shard_map/ppermute | solution.py:173
  21.7 0.0 collective-permute-start.1
  21.7 1.1 collective-permute-start.2
  22.8 3.0 %collective-permute-start.3 = (f32[24,512]{1,0:T(8,128)S(1)}, f32[24,512]{1,0:T(8,128)S(1)}, u32[]{:S(2)}, u32[]{:S(2)}) collective-permute-start(f32[24,512]{1,0:T(8,128)S(1)} %stats.1), channel_id=1, source_target_pairs={{0,4},{1,5},{2,6},{3,7},{4,0},{5,1},{6,2},{7,3},{8,12},{9,13},{10,... | collective-permute-start | bytes 147464 | tf_op jit(solution)/shard_map/ppermute | solution.py:173
  25.8 0.3 collective-permute-start.4
  26.2 0.0 collective-permute-done
  26.2 1.9 collective-permute-start.5
  28.1 0.0 collective-permute-done.1
  28.1 1.8 collective-permute-start.6
  29.8 0.0 collective-permute-done.2
  29.9 0.0 collective-permute-done.3
  29.9 1.3 collective-permute-done.4
  31.2 0.4 collective-permute-done.6
  31.7 0.0 copy-start.15
  31.7 0.0 copy-start.16
  31.7 0.0 copy-start
  31.7 7.7 %grads.1 = (bf16[512,1024]{1,0:T(8,128)(2,1)S(1)}, bf16[512,1024]{1,0:T(8,128)(2,1)S(1)}, f32[1024,256]{1,0:T(8,128)S(1)}) custom-call(s32[1]{0:T(128)S(6)} %copy.20.length_ref, bf16[256,1024]{1,0:T(8,128)(2,1)S(1)} %bitcast.44, bf16[512,1024]{1,0:T(8,128)(2,1)S(1)} %bitcast.40, bf16[512,1024]{1,0:T(8,128)(2,1)S(1)} %bitcast.42, ...), custom_call_target="tpu_custom_call" | custom-call | flops 1342177280 | bytes 8388608 | tf_op jit(solution)/shard_map/grads/pallas_call | solution.py:192
  39.4 1.0 copy-done.1
  40.4 1.0 copy-done.3
  41.4 0.0 reduce-scatter.2.cloned.1.call-update
  41.4 0.0 all-gather.2.cloned.1.call-start
  41.5 0.7 pad_maximum_fusion
  42.2 0.0 all-gather.2.cloned.1.call-update
  42.2 3.6 %flip.1.own_ref = bf16[2048,512]{1,0:T(8,128)(2,1)} custom-call(bf16[512,2048]{1,0:T(8,128)(2,1)S(1)} %bitcast.38), custom_call_target="tpu_custom_call" | custom-call | bytes 4194304 | tf_op jit(solution)/shard_map/flip/pallas_call | solution.py:179
  45.8 0.2 collective-permute-start.7
  46.0 2.3 %broadcast_select_fusion = (bf16[512,1024]{1,0:T(8,128)(2,1)}, bf16[512,1024]{1,0:T(8,128)(2,1)S(1)}) fusion(bf16[512,1024]{1,0:T(8,128)(2,1)} %copy-done.1, bf16[512,1024]{1,0:T(8,128)(2,1)S(1)} %get-tuple-element.16.key_ref, pred[]{:T(512)S(6)} %eq.6), kind=kLoop, calls=%fused_computation.4 | loop fusion | flops 1048576 | bytes 4194305 | tf_op jit(solution)/shard_map/jit(_where)/select_n | solution.py:219
  48.4 0.3 collective-permute-start.8
  48.7 0.1 pad_add_fusion.place_ref
  48.8 2.9 %collective-permute-done.8.grad_other_ref = bf16[512,1024]{1,0:T(8,128)(2,1)S(1)} collective-permute-done((bf16[512,1024]{1,0:T(8,128)(2,1)}, bf16[512,1024]{1,0:T(8,128)(2,1)S(1)}, u32[]{:S(2)}, u32[]{:S(2)}) %collective-permute-start.8) | collective-permute-done | bytes 1048608 | tf_op jit(solution)/shard_map/ppermute | solution.py:46
  51.7 1.0 copy-done.8
  52.7 1.2 copy-done.9
  53.9 8.5 %weights.1 = (f32[8,64,512]{2,1,0:T(8,128)S(1)}, bf16[8,64,512]{2,1,0:T(8,128)(2,1)S(1)}, bf16[8,64,512]{2,1,0:T(8,128)(2,1)S(1)}, bf16[8,64,512]{2,1,0:T(8,128)...) custom-call(s32[2]{0:T(128)S(1)} %pad_add_fusion.place_ref, ...), custom_call_target="tpu_custom_call" | custom-call | flops 4294967296 | bytes 12582912 | tf_op jit(solution)/shard_map/weights/pallas_call | solution.py:228
  62.5 2.9 %collective-permute-start.14 = (bf16[8,4,16,512]{3,2,1,0:T(8,128)(2,1)S(1)}, bf16[8,4,16,512]{3,2,1,0:T(8,128)(2,1)S(1)}, u32[]{:S(2)}, u32[]{:S(2)}) collective-permute-start(bf16[8,4,16,512]{3,2,1,0:T(8,128)(2,1)S(1)} %get-tuple-element.25), channel_id=1, source_target_pairs={{0,6},{1,7},{2,0},{3,1},{4,2},{5,3},{6,4},{7,5},{8,14},{9,15},{10,... | collective-permute-start | bytes 1572872 | tf_op jit(solution)/shard_map/ppermute | solution.py:245
  65.4 0.2 collective-permute-start.13
  65.6 0.5 collective-permute-start.12
  66.1 12.3 %collective-permute-done.14 = bf16[8,4,16,512]{3,2,1,0:T(8,128)(2,1)S(1)} collective-permute-done((bf16[8,4,16,512]{3,2,1,0:T(8,128)(2,1)S(1)}, bf16[8,4,16,512]{3,2,1,0:T(8,128)(2,1)S(1)}, u32[]{:S(2)}, u32[]{:S(2)}) %collective-permute-start.14) | collective-permute-done | bytes 524320 | tf_op jit(solution)/shard_map/ppermute | solution.py:245
  78.4 2.8 %collective-permute-done.13 = bf16[8,4,16,512]{3,2,1,0:T(8,128)(2,1)S(1)} collective-permute-done((bf16[8,4,16,512]{3,2,1,0:T(8,128)(2,1)S(1)}, bf16[8,4,16,512]{3,2,1,0:T(8,128)(2,1)S(1)}, u32[]{:S(2)}, u32[]{:S(2)}) %collective-permute-start.13) | collective-permute-done | bytes 524320 | tf_op jit(solution)/shard_map/ppermute | solution.py:245
  81.2 12.1 %collective-permute-done.12 = bf16[8,4,16,512]{3,2,1,0:T(8,128)(2,1)S(1)} collective-permute-done((bf16[8,4,16,512]{3,2,1,0:T(8,128)(2,1)S(1)}, bf16[8,4,16,512]{3,2,1,0:T(8,128)(2,1)S(1)}, u32[]{:S(2)}, u32[]{:S(2)}) %collective-permute-start.12) | collective-permute-done | bytes 524320 | tf_op jit(solution)/shard_map/ppermute | solution.py:245
  93.3 1.1 add_convert_fusion
  94.5 11.8 %all-to-all-start.1 = ((bf16[64,8,512]{2,1,0:T(8,128)(2,1)}), bf16[64,8,512]{2,1,0:T(8,128)(2,1)}, u32[]{:S(2)}, u32[]{:S(2)}) async-start(bf16[64,8,512]{2,1,0:T(8,128)(2,1)} %bitcast.20), calls=%async_computation.2 | async-start | bytes 1048576 | tf_op jit(solution)/shard_map/all_to_all | solution.py:254
  106.3 2.7 %collective-permute-start.11 = (bf16[8,64,512]{2,1,0:T(8,128)(2,1)}, bf16[8,64,512]{2,1,0:T(8,128)(2,1)S(1)}, u32[]{:S(2)}, u32[]{:S(2)}) collective-permute-start(bf16[8,64,512]{2,1,0:T(8,128)(2,1)} %copy-done.14), channel_id=1, source_target_pairs={{0,24},{1,25},{2,26},{3,27},{4,28},{5,29},{6,30},{7,31},{8,0},{9,1... | collective-permute-start | bytes 1572872 | tf_op jit(solution)/shard_map/ppermute | solution.py:242
  108.9 0.6 collective-permute-start.10
  109.5 0.6 collective-permute-start.9
  110.1 27.1 %collective-permute-done.11 = bf16[8,64,512]{2,1,0:T(8,128)(2,1)S(1)} collective-permute-done((bf16[8,64,512]{2,1,0:T(8,128)(2,1)}, bf16[8,64,512]{2,1,0:T(8,128)(2,1)S(1)}, u32[]{:S(2)}, u32[]{:S(2)}) %collective-permute-start.11) | collective-permute-done | bytes 524320 | tf_op jit(solution)/shard_map/ppermute | solution.py:242
  137.2 2.8 %collective-permute-done.10 = bf16[8,64,512]{2,1,0:T(8,128)(2,1)S(1)} collective-permute-done((bf16[8,64,512]{2,1,0:T(8,128)(2,1)}, bf16[8,64,512]{2,1,0:T(8,128)(2,1)S(1)}, u32[]{:S(2)}, u32[]{:S(2)}) %collective-permute-start.10) | collective-permute-done | bytes 524320 | tf_op jit(solution)/shard_map/ppermute | solution.py:242
  140.1 18.5 %collective-permute-done.9 = bf16[8,64,512]{2,1,0:T(8,128)(2,1)S(1)} collective-permute-done((bf16[8,64,512]{2,1,0:T(8,128)(2,1)}, bf16[8,64,512]{2,1,0:T(8,128)(2,1)S(1)}, u32[]{:S(2)}, u32[]{:S(2)}) %collective-permute-start.9) | collective-permute-done | bytes 524320 | tf_op jit(solution)/shard_map/ppermute | solution.py:242
  158.6 1.1 add_convert_fusion.1
  159.7 0.0 all-to-all-done.1
  159.7 8.4 %all-to-all-start = ((bf16[64,8,512]{2,1,0:T(8,128)(2,1)}), bf16[64,8,512]{2,1,0:T(8,128)(2,1)S(1)}, u32[]{:S(2)}, u32[]{:S(2)}) async-start(bf16[64,8,512]{2,1,0:T(8,128)(2,1)} %bitcast.48), calls=%async_computation.1 | async-start | bytes 1048576 | tf_op jit(solution)/shard_map/all_to_all | solution.py:251
  168.1 0.0 reduce-scatter.2.cloned.1.call-done
  168.1 0.9 convert_bitcast_fusion
  169.1 0.7 copy.12
  169.8 1.1 convert_reduce_fusion
  170.9 14.9 %all-to-all-done = bf16[64,8,512]{2,1,0:T(8,128)(2,1)S(1)} async-done(((bf16[64,8,512]{2,1,0:T(8,128)(2,1)}), bf16[64,8,512]{2,1,0:T(8,128)(2,1)S(1)}, u32[]{:S(2)}, u32[]{:S(2)}) %all-to-all-start) | async-done | bytes 524320 | tf_op jit(solution)/shard_map/all_to_all | solution.py:251
  185.8 0.1 convert_reduce_fusion.1
  185.9 0.6 fusion.2
  186.6 3.4 %copy-done.4 = bf16[2048,2048]{1,0:T(8,128)(2,1)S(1)} copy-done((bf16[2048,2048]{1,0:T(8,128)(2,1)S(1)}, bf16[2048,2048]{1,0:T(8,128)(2,1)}, u32[]{:S(2)}) %copy-start.4) | copy-done | bytes 8388632
  189.9 6.8 %encoded.1 = bf16[512,2048]{1,0:T(8,128)(2,1)} custom-call(bf16[512,1024]{1,0:T(8,128)(2,1)S(1)} %get-tuple-element.16.key_ref, bf16[512,1024]{1,0:T(8,128)(2,1)S(1)} %copy-done.2, bf16[2048,2048]{1,0:T(8,128)(2,1)S(1)} %copy-done.4), custom_call_target="tpu_custom_call" | custom-call | flops 4294967296 | bytes 12582912 | tf_op jit(solution)/shard_map/encoded/pallas_call | solution.py:261
  (33 shorter events, 0.1 us)
Async XLA Ops:
  8.0 160.1 %reduce-scatter.2.cloned.1.call-start = ((), (), s32[]{:S(2)}) async-start(), calls=%async_computation.3 | async-start | bytes 1179648 | tf_op jit(solution)/shard_map/reduce_scatter | solution.py:214
  8.7 1.2 copy-start.5
  9.9 1.2 copy-start.7
  11.1 1.0 copy-start.10
  12.2 1.0 copy-start.11
  13.2 18.4 %copy-start.6 = (bf16[1,512,1024]{2,1,0:T(8,128)(2,1)S(1)}, bf16[1,512,1024]{2,1,0:T(8,128)(2,1)}, u32[]{:S(2)}) copy-start(bf16[1,512,1024]{2,1,0:T(8,128)(2,1)} %param.9) | copy-start | bytes 3145732
  18.4 7.8 %collective-permute-start = (f32[24,512]{1,0:T(8,128)S(1)}, f32[24,512]{1,0:T(8,128)S(1)}, u32[]{:S(2)}, u32[]{:S(2)}) collective-permute-start(f32[24,512]{1,0:T(8,128)S(1)} %stats.1), channel_id=1, source_target_pairs={{0,1},{1,0},{2,3},{3,2},{4,5},{5,4},{6,7},{7,6},{8,9},{9,8},{10,11... | collective-permute-start | bytes 147464 | tf_op jit(solution)/shard_map/ppermute | solution.py:173
  21.7 6.3 %collective-permute-start.1 = (f32[24,512]{1,0:T(8,128)S(1)}, f32[24,512]{1,0:T(8,128)S(1)}, u32[]{:S(2)}, u32[]{:S(2)}) collective-permute-start(f32[24,512]{1,0:T(8,128)S(1)} %stats.1), channel_id=1, source_target_pairs={{0,2},{1,3},{2,4},{3,5},{4,6},{5,7},{6,0},{7,1},{8,10},{9,11},{10,... | collective-permute-start | bytes 147464 | tf_op jit(solution)/shard_map/ppermute | solution.py:173
  21.7 8.1 %collective-permute-start.2 = (f32[24,512]{1,0:T(8,128)S(1)}, f32[24,512]{1,0:T(8,128)S(1)}, u32[]{:S(2)}, u32[]{:S(2)}) collective-permute-start(f32[24,512]{1,0:T(8,128)S(1)} %stats.1), channel_id=1, source_target_pairs={{0,3},{1,2},{2,5},{3,4},{4,7},{5,6},{6,1},{7,0},{8,11},{9,10},{10,... | collective-permute-start | bytes 147464 | tf_op jit(solution)/shard_map/ppermute | solution.py:173
  22.8 7.0 %collective-permute-start.3 = (f32[24,512]{1,0:T(8,128)S(1)}, f32[24,512]{1,0:T(8,128)S(1)}, u32[]{:S(2)}, u32[]{:S(2)}) collective-permute-start(f32[24,512]{1,0:T(8,128)S(1)} %stats.1), channel_id=1, source_target_pairs={{0,4},{1,5},{2,6},{3,7},{4,0},{5,1},{6,2},{7,3},{8,12},{9,13},{10,... | collective-permute-start | bytes 147464 | tf_op jit(solution)/shard_map/ppermute | solution.py:173
  25.8 5.4 %collective-permute-start.4 = (f32[24,512]{1,0:T(8,128)S(1)}, f32[24,512]{1,0:T(8,128)S(1)}, u32[]{:S(2)}, u32[]{:S(2)}) collective-permute-start(f32[24,512]{1,0:T(8,128)S(1)} %stats.1), channel_id=1, source_target_pairs={{0,5},{1,4},{2,7},{3,6},{4,1},{5,0},{6,3},{7,2},{8,13},{9,12},{10,... | collective-permute-start | bytes 147464 | tf_op jit(solution)/shard_map/ppermute | solution.py:173
  26.2 5.0 %collective-permute-start.5 = (f32[24,512]{1,0:T(8,128)S(1)}, f32[24,512]{1,0:T(8,128)S(1)}, u32[]{:S(2)}, u32[]{:S(2)}) collective-permute-start(f32[24,512]{1,0:T(8,128)S(1)} %stats.1), channel_id=1, source_target_pairs={{0,6},{1,7},{2,0},{3,1},{4,2},{5,3},{6,4},{7,5},{8,14},{9,15},{10,... | collective-permute-start | bytes 147464 | tf_op jit(solution)/shard_map/ppermute | solution.py:173
  28.1 3.6 %collective-permute-start.6 = (f32[24,512]{1,0:T(8,128)S(1)}, f32[24,512]{1,0:T(8,128)S(1)}, u32[]{:S(2)}, u32[]{:S(2)}) collective-permute-start(f32[24,512]{1,0:T(8,128)S(1)} %stats.1), channel_id=1, source_target_pairs={{0,7},{1,6},{2,1},{3,0},{4,3},{5,2},{6,5},{7,4},{8,15},{9,14},{10,... | collective-permute-start | bytes 147464 | tf_op jit(solution)/shard_map/ppermute | solution.py:173
  31.7 9.8 %copy-start.15 = (bf16[64,1024]{1,0:T(8,128)(2,1)S(1)}, bf16[64,1024]{1,0:T(8,128)(2,1)}, u32[]{:S(2)}) copy-start(bf16[64,1024]{1,0:T(8,128)(2,1)} %param.13) | copy-start | bytes 393220
  31.7 9.8 %copy-start.16 = (bf16[64,1024]{1,0:T(8,128)(2,1)S(1)}, bf16[64,1024]{1,0:T(8,128)(2,1)}, u32[]{:S(2)}) copy-start(bf16[64,1024]{1,0:T(8,128)(2,1)} %param.12) | copy-start | bytes 393220
  31.7 10.5 %copy-start = (bf16[1,512,2048]{2,1,0:T(8,128)(2,1)S(1)}, bf16[1,512,2048]{2,1,0:T(8,128)(2,1)}, u32[]{:S(2)}) copy-start(bf16[1,512,2048]{2,1,0:T(8,128)(2,1)} %param.11) | copy-start | bytes 6291460
  39.4 1.0 copy-start.1
  40.4 1.0 copy-start.3
  41.4 145.2 %all-gather.2.cloned.1.call-start = ((), (), s32[]{:S(2)}) async-start(), calls=%async_computation.4 | async-start | bytes 8650752 | tf_op jit(solution)/shard_map/all_gather | solution.py:157
  45.8 6.9 %collective-permute-start.7 = (bf16[2048,512]{1,0:T(8,128)(2,1)}, bf16[2048,512]{1,0:T(8,128)(2,1)}, u32[]{:S(2)}, u32[]{:S(2)}) collective-permute-start(bf16[2048,512]{1,0:T(8,128)(2,1)} %flip.1.own_ref), channel_id=1, source_target_pairs={{0,1},{1,0},{2,3},{3,2},{4,5},{5,4},{6,7},{7,6},{8,9},{9,8},{10,11... | collective-permute-start | bytes 6291464 | tf_op jit(solution)/shard_map/ppermute | solution.py:46
  48.4 3.4 %collective-permute-start.8 = (bf16[512,1024]{1,0:T(8,128)(2,1)}, bf16[512,1024]{1,0:T(8,128)(2,1)S(1)}, u32[]{:S(2)}, u32[]{:S(2)}) collective-permute-start(bf16[512,1024]{1,0:T(8,128)(2,1)} %get-tuple-element.30), channel_id=1, source_target_pairs={{0,1},{1,0},{2,3},{3,2},{4,5},{5,4},{6,7},{7,6},{8,9},{9,8},{10,11... | collective-permute-start | bytes 3145736 | tf_op jit(solution)/shard_map/ppermute | solution.py:46
  51.7 1.0 copy-start.8
  52.7 1.2 copy-start.9
  62.4 32.0 %copy-start.12 = (bf16[8,64,512]{2,1,0:T(8,128)(2,1)}, bf16[8,64,512]{2,1,0:T(8,128)(2,1)S(1)}, u32[]{:S(2)}) copy-start(bf16[8,64,512]{2,1,0:T(8,128)(2,1)S(1)} %get-tuple-element.19) | copy-start | bytes 1572868
  62.4 32.0 %copy-start.13 = (bf16[8,64,512]{2,1,0:T(8,128)(2,1)}, bf16[8,64,512]{2,1,0:T(8,128)(2,1)S(1)}, u32[]{:S(2)}) copy-start(bf16[8,64,512]{2,1,0:T(8,128)(2,1)S(1)} %get-tuple-element.20) | copy-start | bytes 1572868
  62.5 32.0 %copy-start.14 = (bf16[8,64,512]{2,1,0:T(8,128)(2,1)}, bf16[8,64,512]{2,1,0:T(8,128)(2,1)S(1)}, u32[]{:S(2)}) copy-start(bf16[8,64,512]{2,1,0:T(8,128)(2,1)S(1)} %get-tuple-element.21) | copy-start | bytes 1572868
  62.5 16.0 %collective-permute-start.14 = (bf16[8,4,16,512]{3,2,1,0:T(8,128)(2,1)S(1)}, bf16[8,4,16,512]{3,2,1,0:T(8,128)(2,1)S(1)}, u32[]{:S(2)}, u32[]{:S(2)}) collective-permute-start(bf16[8,4,16,512]{3,2,1,0:T(8,128)(2,1)S(1)} %get-tuple-element.25), channel_id=1, source_target_pairs={{0,6},{1,7},{2,0},{3,1},{4,2},{5,3},{6,4},{7,5},{8,14},{9,15},{10,... | collective-permute-start | bytes 1572872 | tf_op jit(solution)/shard_map/ppermute | solution.py:245
  65.4 15.8 %collective-permute-start.13 = (bf16[8,4,16,512]{3,2,1,0:T(8,128)(2,1)S(1)}, bf16[8,4,16,512]{3,2,1,0:T(8,128)(2,1)S(1)}, u32[]{:S(2)}, u32[]{:S(2)}) collective-permute-start(bf16[8,4,16,512]{3,2,1,0:T(8,128)(2,1)S(1)} %get-tuple-element.24), channel_id=1, source_target_pairs={{0,4},{1,5},{2,6},{3,7},{4,0},{5,1},{6,2},{7,3},{8,12},{9,13},{10,... | collective-permute-start | bytes 1572872 | tf_op jit(solution)/shard_map/ppermute | solution.py:245
  65.6 27.7 %collective-permute-start.12 = (bf16[8,4,16,512]{3,2,1,0:T(8,128)(2,1)S(1)}, bf16[8,4,16,512]{3,2,1,0:T(8,128)(2,1)S(1)}, u32[]{:S(2)}, u32[]{:S(2)}) collective-permute-start(bf16[8,4,16,512]{3,2,1,0:T(8,128)(2,1)S(1)} %get-tuple-element.23), channel_id=1, source_target_pairs={{0,2},{1,3},{2,4},{3,5},{4,6},{5,7},{6,0},{7,1},{8,10},{9,11},{10,... | collective-permute-start | bytes 1572872 | tf_op jit(solution)/shard_map/ppermute | solution.py:245
  94.5 65.2 %all-to-all-start.1 = ((bf16[64,8,512]{2,1,0:T(8,128)(2,1)}), bf16[64,8,512]{2,1,0:T(8,128)(2,1)}, u32[]{:S(2)}, u32[]{:S(2)}) async-start(bf16[64,8,512]{2,1,0:T(8,128)(2,1)} %bitcast.20), calls=%async_computation.2 | async-start | bytes 1048576 | tf_op jit(solution)/shard_map/all_to_all | solution.py:254
  106.3 31.0 %collective-permute-start.11 = (bf16[8,64,512]{2,1,0:T(8,128)(2,1)}, bf16[8,64,512]{2,1,0:T(8,128)(2,1)S(1)}, u32[]{:S(2)}, u32[]{:S(2)}) collective-permute-start(bf16[8,64,512]{2,1,0:T(8,128)(2,1)} %copy-done.14), channel_id=1, source_target_pairs={{0,24},{1,25},{2,26},{3,27},{4,28},{5,29},{6,30},{7,31},{8,0},{9,1... | collective-permute-start | bytes 1572872 | tf_op jit(solution)/shard_map/ppermute | solution.py:242
  108.9 31.1 %collective-permute-start.10 = (bf16[8,64,512]{2,1,0:T(8,128)(2,1)}, bf16[8,64,512]{2,1,0:T(8,128)(2,1)S(1)}, u32[]{:S(2)}, u32[]{:S(2)}) collective-permute-start(bf16[8,64,512]{2,1,0:T(8,128)(2,1)} %copy-done.13), channel_id=1, source_target_pairs={{0,16},{1,17},{2,18},{3,19},{4,20},{5,21},{6,22},{7,23},{8,24},{9,... | collective-permute-start | bytes 1572872 | tf_op jit(solution)/shard_map/ppermute | solution.py:242
  109.5 49.1 %collective-permute-start.9 = (bf16[8,64,512]{2,1,0:T(8,128)(2,1)}, bf16[8,64,512]{2,1,0:T(8,128)(2,1)S(1)}, u32[]{:S(2)}, u32[]{:S(2)}) collective-permute-start(bf16[8,64,512]{2,1,0:T(8,128)(2,1)} %copy-done.12), channel_id=1, source_target_pairs={{0,8},{1,9},{2,10},{3,11},{4,12},{5,13},{6,14},{7,15},{8,16},{9,17... | collective-permute-start | bytes 1572872 | tf_op jit(solution)/shard_map/ppermute | solution.py:242
  159.7 26.8 %copy-start.2 = (bf16[512,1024]{1,0:T(8,128)(2,1)S(1)}, bf16[512,1024]{1,0:T(8,128)(2,1)}, u32[]{:S(2)}) copy-start(bf16[512,1024]{1,0:T(8,128)(2,1)} %copy-done.1) | copy-start | bytes 3145732
  159.7 26.1 %all-to-all-start = ((bf16[64,8,512]{2,1,0:T(8,128)(2,1)}), bf16[64,8,512]{2,1,0:T(8,128)(2,1)S(1)}, u32[]{:S(2)}, u32[]{:S(2)}) async-start(bf16[64,8,512]{2,1,0:T(8,128)(2,1)} %bitcast.48), calls=%async_computation.1 | async-start | bytes 1048576 | tf_op jit(solution)/shard_map/all_to_all | solution.py:251
  186.6 3.4 %copy-start.4 = (bf16[2048,2048]{1,0:T(8,128)(2,1)S(1)}, bf16[2048,2048]{1,0:T(8,128)(2,1)}, u32[]{:S(2)}) copy-start(bf16[2048,2048]{1,0:T(8,128)(2,1)} %all-gather.2.cloned.1.call-done.weight_ref) | copy-start | bytes 25165828
Sparse Core Ops, SparseCore 0:
  41.5 50.4 reduce-scatter.1
Sparse Core Ops, SparseCore 1:
  44.4 127.6 all-gather.1

commit v2 on v0

v2 whole, which is shorter than its diff:
```python
import functools
import math

import jax
import jax.numpy as jnp
from jax import lax
from jax.experimental import pallas as pl
from jax.experimental.pallas import tpu as pltpu
from jax.sharding import PartitionSpec as P

HEADS = 16
HEAD_DIM = 64
PAIR = 2 * HEAD_DIM
SCALE = 1.0 / math.sqrt(HEAD_DIM)
EXP2_SCALE = SCALE * math.log2(math.e)
NZ, NX, NY, NC = 8, 4, 4, 2
AXES = ("dp", "passage")
MIB = 1024 * 1024


def device_index(z, x, y, c):
    return ((z % NZ) * NX + x % NX) * (NY * NC) + (y % NY) * NC + c % NC


def permutation(target):
    return [
        (device_index(z, x, y, c), device_index(*target(z, x, y, c)))
        for z in range(NZ)
        for x in range(NX)
        for y in range(NY)
        for c in range(NC)
    ]


def groups(key):
    found = {}
    for z in range(NZ):
        for x in range(NX):
            for y in range(NY):
                for c in range(NC):
                    found.setdefault(key(z, x, y, c), []).append(device_index(z, x, y, c))
    return list(found.values())


def swap_cores(value):
    return lax.ppermute(value, AXES, permutation(lambda z, x, y, c: (z, x, y, 1 - c)))


def two_heads(rows):
    lane = lax.broadcasted_iota(jnp.int32, rows.shape, 1)
    wide = rows.astype(jnp.float32)
    first = jnp.where(lane < HEAD_DIM, wide, 0.0)
    second = jnp.where(lane < HEAD_DIM, 0.0, wide)
    return jnp.concatenate([first, second], axis=0).astype(jnp.bfloat16)


def live_grads(length_ref, grad):
    rows = grad.astype(jnp.float32)
    position = lax.broadcasted_iota(jnp.int32, rows.shape, 0)
    return two_heads(jnp.where(position < length_ref[0], rows, 0.0))


def dot_last(left, right):
    return lax.dot_general(left, right, (((1,), (1,)), ((), ())), preferred_element_type=jnp.float32)


def merged(rows, pairs):
    peak = jnp.max(rows[:, :pairs], axis=0)
    weight = jnp.exp2((rows[:, :pairs] - peak[None]) * EXP2_SCALE)
    total = jnp.sum(rows[:, pairs : 2 * pairs] * weight, axis=0)
    delta = jnp.sum(rows[:, 2 * pairs :] * weight, axis=0)
    return peak, total, delta


def stats_kernel(length_ref, query_ref, key_ref, value_ref, grad_ref, out_ref):
    for part in range(2):
        lanes = slice(part * PAIR, part * PAIR + PAIR)
        pair = 2 * pl.program_id(0) + part
        scores = dot_last(key_ref[:, lanes], two_heads(query_ref[:, lanes]))
        prob_grad = dot_last(value_ref[:, lanes], live_grads(length_ref, grad_ref[:, lanes]))
        peak = jnp.max(scores, axis=0, keepdims=True)
        expo = jnp.exp2((scores - peak) * EXP2_SCALE)
        out_ref[pl.ds(pair, 1), :] = peak
        out_ref[pl.ds(8 + pair, 1), :] = jnp.sum(expo, axis=0, keepdims=True)
        out_ref[pl.ds(16 + pair, 1), :] = jnp.sum(expo * prob_grad, axis=0, keepdims=True)


def merge_kernel(left_ref, right_ref, out_ref):
    pairs = out_ref.shape[0] // 3
    peak, total, delta = merged(jnp.stack([left_ref[...], right_ref[...]]), pairs)
    out_ref[:pairs] = peak
    out_ref[pairs : 2 * pairs] = total
    out_ref[2 * pairs :] = delta


def grads_kernel(first_pair, core_ref, length_ref, query_ref, key_ref, value_ref, grad_ref, *refs):
    stats_refs = refs[:NY]
    mine_ref, sent_ref, query_kept_ref, query_sent_ref = refs[NY:]
    keeps_key = core_ref[0] == 0
    query_grads = []
    for part in range(2):
        lanes = slice(part * PAIR, part * PAIR + PAIR)
        pair = first_pair + 2 * pl.program_id(0) + part
        rows = jnp.stack([
            jnp.concatenate([ref[pl.ds(start + pair, 1), :] for start in (0, 8, 16)], axis=0)
            for ref in stats_refs
        ])
        peak, total, delta = merged(rows, 1)
        row_delta = delta / total
        inverse = 1.0 / total
        key = key_ref[:, lanes]
        queries = two_heads(query_ref[:, lanes])
        grads = live_grads(length_ref, grad_ref[:, lanes])
        scores = dot_last(key, queries)
        prob_grad = dot_last(value_ref[:, lanes], grads)
        prob = jnp.exp2((scores - peak) * EXP2_SCALE) * inverse
        prob_low = prob.astype(jnp.bfloat16)
        score_grad = (prob * (prob_grad - row_delta)).astype(jnp.bfloat16)
        value_grad = jnp.dot(prob_low, grads, preferred_element_type=jnp.float32)
        key_grad = jnp.dot(score_grad, queries, preferred_element_type=jnp.float32) * SCALE
        mine_ref[:, lanes] = jnp.where(keeps_key, key_grad, value_grad).astype(jnp.bfloat16)
        sent_ref[:, lanes] = jnp.where(keeps_key, value_grad, key_grad).astype(jnp.bfloat16)
        flipped = key.T
        answer = queries.shape[0] // 2
        query_grads.append(
            SCALE
            * jnp.concatenate(
                [
                    jnp.dot(flipped[:HEAD_DIM], score_grad[:, :answer], preferred_element_type=jnp.float32),
                    jnp.dot(flipped[HEAD_DIM:], score_grad[:, answer:], preferred_element_type=jnp.float32),
                ],
                axis=0,
            )
        )
    even, odd = query_grads
    query_kept_ref[0] = jnp.where(keeps_key, even, odd)
    query_sent_ref[0] = jnp.where(keeps_key, odd, even).astype(jnp.bfloat16)


def arrange_kernel(place_ref, *refs):
    shards, out_ref = refs[:-1], refs[-1]
    rows = shards[0].shape[0]
    for k, shard in enumerate(shards):
        first = lax.rem(place_ref[0] + NX - k, NX) * rows
        out_ref[pl.ds(pl.multiple_of(first, rows), rows), :] = shard[...]


def split(place_ref, first, rows_of, refs):
    kept_left, sent_left, kept_right, sent_right = refs
    for kept, sent, near, far, side in ((kept_left, sent_left, 1, 3, 0), (kept_right, sent_right, 3, 1, 1)):
        for out, order in ((kept, (0, far)), (sent, (near, 2))):
            for index, flip in enumerate(order):
                rows_of(out.at[index], place_ref[first + flip], side)


def side_of(ref, index, rows, side):
    half = ref.shape[-1] // 2
    return ref[index, rows, side * half : side * half + half]


def weights_kernel(place_ref, own_ref, other_ref, *refs):
    own_grads, other_grads, query_refs = refs[:2], refs[2:4], refs[4:8]
    x_outs, y_outs = refs[8:12], refs[12:16]
    x_total, y_total, query_total = refs[16:]
    own, other = own_ref[...].T, other_ref[...].T
    for total, own_grad, other_grad in zip((x_total, y_total), own_grads, other_grads):
        total[0] = jnp.dot(own, own_grad[...], preferred_element_type=jnp.float32) + jnp.dot(
            other, other_grad[...], preferred_element_type=jnp.float32
        )
    for y in range(NY):
        kept, received = query_refs[y // 2], query_refs[2 + y // 2]
        for side in range(2):
            first = pl.multiple_of(side * 64 + pl.program_id(0) * 16, 16)
            rows = kept[y % 2, pl.ds(first, 16), :] + received[y % 2, pl.ds(first, 16), :].astype(jnp.float32)
            query_total[y, side] = rows

    def x_rows(out, chosen, side):
        for z in range(out.shape[0]):
            rows = pl.ds(pl.multiple_of(z * 256 + chosen * 64, 64), 64)
            out[z] = side_of(x_total, 0, rows, side).astype(out.dtype)

    def y_rows(out, chosen, side):
        for z in range(NZ // 4):
            for x in range(NX):
                rows = pl.ds(pl.multiple_of(z * 256 + x * 64 + chosen * 16, 16), 16)
                row = (z * NX + x) * 16
                out[0, row : row + 16] = side_of(y_total, 0, rows, side).astype(out.dtype)
        out[0, NZ // 4 * NX * 16 :] = query_total[chosen, side].astype(out.dtype)

    split(place_ref, 0, x_rows, x_outs)
    split(place_ref, 4, y_rows, y_outs)


def middle_kernel(*refs):
    parts = len(refs) // 3
    for kept, received, out in zip(refs[:parts], refs[parts : 2 * parts], refs[2 * parts :]):
        out[...] = (kept[0] + received[0].astype(jnp.float32)).astype(out.dtype)


def add_parts(refs, total):
    half = total.shape[-1] // 2
    for side in range(2):
        kept, first, last = refs[side], refs[2 + side], refs[4 + side]
        rows = kept[0] + first[0].astype(jnp.float32) + last[...].astype(jnp.float32)
        total[:, :, side * half : side * half + half] = rows


def second_kernel(place_ref, *refs):
    add_parts(refs[:6], refs[-2])
    add_parts(refs[6:12], refs[-1])
    x_outs, y_outs = refs[12:16], refs[16:20]
    query_out, x_total, y_total = refs[20:]
    query_out[...] = y_total[:, NZ // 4 * NX * 16 :]

    def x_rows(out, chosen, side):
        for z in range(NZ // 4):
            rows = pl.ds(pl.multiple_of(chosen * 16, 16), 16)
            out[z] = side_of(x_total, z, rows, side).astype(out.dtype)

    def y_rows(out, chosen, side):
        for z in range(NZ // 4):
            rows = pl.ds(pl.multiple_of(z * NX * 16 + chosen * 16, 16), 16)
            out[z] = side_of(y_total, 0, rows, side).astype(out.dtype)

    split(place_ref, 4, x_rows, x_outs)
    split(place_ref, 0, y_rows, y_outs)


def last_kernel(*refs):
    out, x_total, y_total = refs[12:]
    half = x_total.shape[2]
    add_parts(refs[:6], x_total)
    add_parts(refs[6:12], y_total)
    out[:, :, :half] = x_total[...].astype(out.dtype)
    out[:, :, half:] = y_total[...].astype(out.dtype)


def encoded_kernel(*refs):
    grads, weights, out_ref = refs[:4], refs[4:-1], refs[-1]
    half = grads[0].shape[1]
    total = None
    for index, grad in enumerate(grads):
        part = index % 2
        term = dot_last(grad[...], weights[index // 2][:, part * half : part * half + half])
        total = term if total is None else total + term
    out_ref[...] = total.astype(jnp.bfloat16)


def kernel_call(kernel, name, out_shape, mebibytes=24, flops=0, moved=0, **options):
    return pl.pallas_call(
        kernel,
        out_shape=out_shape,
        compiler_params=pltpu.CompilerParams(vmem_limit_bytes=mebibytes * MIB),
        cost_estimate=pl.CostEstimate(flops=flops, bytes_accessed=moved, transcendentals=0),
        name=name,
        **options,
    )


def like(shape, dtype):
    return jax.ShapeDtypeStruct(shape, dtype)


def along(axis, step):
    def target(z, x, y, c):
        return (
            z + step * (axis == "z"),
            x + step * (axis == "x"),
            y + step * (axis == "y"),
            c + step * (axis == "core"),
        )

    return permutation(target)


def send(value, links):
    return lax.ppermute(value, AXES, links)


def tie(value, *after):
    return lax.optimization_barrier((value, *after))[0]


def flipped(axis, bits):
    return permutation(lambda z, x, y, c: (z, x ^ bits if axis == "x" else x, y ^ bits if axis == "y" else y, c))


def halving(outs, axes, steps):
    kept, sent = outs[0::2], outs[1::2]
    ways = [(axis, *bits) for axis in axes for bits in ((1, 3), (3, 1))]
    first = [send(value, flipped(axis, near)) for value, (axis, near, _) in zip(sent, ways)]
    first = lax.optimization_barrier(first)

    def block(shape):
        return pl.BlockSpec((1, shape[1] // steps, *shape[2:]), lambda i: (1, i, 0, 0))

    shapes = [value.shape for value in kept]
    middle = kernel_call(
        middle_kernel,
        "middle",
        [like(shape[1:], jnp.bfloat16) for shape in shapes],
        grid=(steps,),
        in_specs=[block(shape) for shape in shapes] * 2,
        out_specs=[pl.BlockSpec((shape[1] // steps, *shape[2:]), lambda i: (i, 0, 0)) for shape in shapes],
    )(*kept, *first)
    last = [send(value, flipped(axis, far)) for value, (axis, _, far) in zip(middle, ways)]
    last = lax.optimization_barrier(last)
    operands, specs = [], []
    for start in (0, 2):
        for values in (kept, first, last):
            for value in values[start : start + 2]:
                operands.append(value)
                inner = value.shape[-3:]
                shape = (1,) * (value.ndim - 3) + (inner[0] // steps, *inner[1:])
                leading = (0,) * (value.ndim - 3)
                specs.append(pl.BlockSpec(shape, lambda i, leading=leading: (*leading, i, 0, 0)))
    return operands, specs


def on_device(queries, key_rows, value_rows, encoded, key_weight, value_weight, grad_out, lengths):
    _, answer, features = queries.shape
    keys = key_rows.shape[1]
    width = encoded.shape[2]
    pairs = features // PAIR
    half = features // 2
    dp, passage = lax.axis_index("dp").astype(jnp.int32), lax.axis_index("passage").astype(jnp.int32)
    x_place, y_place, core = dp % NX, passage // NC, passage % NC
    place = jnp.stack([p ^ bits for p in (x_place, y_place) for bits in range(4)])
    queries, grad_out = queries[0], grad_out[0]
    key_rows, value_rows, encoded = key_rows[0], value_rows[0], encoded[0]
    f32, bf16 = jnp.float32, jnp.bfloat16
    encoded_other = swap_cores(encoded)
    smem = pl.BlockSpec(memory_space=pltpu.SMEM)

    shard = jnp.where(core == 0, key_weight, value_weight)
    shards = [shard] + [send(shard, along("x", k)) for k in range(1, NX)]

    stats_shape = like((3 * pairs, 2 * answer), f32)
    row_spec = pl.BlockSpec((answer, 2 * PAIR), lambda p: (0, p))
    key_spec = pl.BlockSpec((keys, 2 * PAIR), lambda p: (0, p))
    stats = kernel_call(
        stats_kernel,
        "stats",
        stats_shape,
        62,
        grid=(pairs // 2,),
        in_specs=[smem, row_spec, key_spec, key_spec, row_spec],
        out_specs=pl.BlockSpec(stats_shape.shape, lambda p: (0, 0)),
    )(lengths, queries, key_rows, value_rows, grad_out)

    whole_vmem = pl.BlockSpec(memory_space=pltpu.VMEM)
    shards = lax.optimization_barrier((*shards, stats))[:-1]
    ordered = kernel_call(
        arrange_kernel,
        "arrange",
        like((NX * shard.shape[0], features), bf16),
        in_specs=[smem] + [whole_vmem] * NX,
        out_specs=whole_vmem,
    )(place, *shards)
    gathered = lax.all_gather(
        ordered, AXES, axis=0, tiled=True, axis_index_groups=groups(lambda z, x, y, c: (x, y, c))
    )

    chip_stats = kernel_call(merge_kernel, "merge", stats_shape)(tie(stats, ordered), swap_cores(stats))
    all_stats = [chip_stats] + [send(chip_stats, along("y", k)) for k in range(1, NY)]

    def grads(first_pair):
        def rows(p):
            return (0, first_pair // 2 + p)

        row_spec = pl.BlockSpec((answer, 2 * PAIR), rows)
        key_spec = pl.BlockSpec((keys, 2 * PAIR), rows)
        out_spec = pl.BlockSpec((keys, 2 * PAIR), lambda p: (0, p))
        stats_spec = pl.BlockSpec(stats_shape.shape, lambda p: (0, 0))
        query_spec = pl.BlockSpec((1, PAIR, answer), lambda p: (p, 0, 0))
        return kernel_call(
            functools.partial(grads_kernel, first_pair),
            "grads",
            [
                like((keys, half), bf16),
                like((keys, half), bf16),
                like((NY // 2, PAIR, answer), f32),
                like((NY // 2, PAIR, answer), bf16),
            ],
            grid=(pairs // 4,),
            in_specs=[smem, smem, row_spec, key_spec, key_spec, row_spec] + [stats_spec] * NY,
            out_specs=[out_spec, out_spec, query_spec, query_spec],
        )(core[None], lengths, queries, key_rows, value_rows, grad_out, *all_stats)

    mine_a, sent_a, query_kept_a, query_sent_a = grads(0)
    received_a = swap_cores(sent_a)
    mine_b, sent_b, query_kept_b, query_sent_b = grads(pairs // 2)
    received_b = swap_cores(sent_b)
    query_received = [swap_cores(query_sent_a), swap_cores(query_sent_b)]

    def blocks(shape):
        return pl.BlockSpec((shape[0] // 4, *shape[1:]), lambda i: (i, 0, 0))

    whole = pl.BlockSpec((keys, half), lambda i: (0, 0))
    encoded_spec = pl.BlockSpec((keys, width // 4), lambda i: (0, i))
    query_spec = pl.BlockSpec(query_kept_a.shape, lambda i: (0, 0, 0))
    query_rows = PAIR * answer // half // 4
    x_shape = (2, NZ, 64, half // 2)
    y_shape = (2, 4, NZ // 4 * NX * 16 + query_rows, half // 2)

    def split_outs(shape):
        spec = pl.BlockSpec((2, shape[1] // 4, *shape[2:]), lambda i: (0, i, 0, 0))
        return [like(shape, f32), like(shape, bf16)] * 2, [spec] * 4

    def total(shape):
        return pltpu.VMEM((shape[1] // 4, shape[2], 2 * shape[3]), f32)

    x_outs, x_specs = split_outs(x_shape)
    y_outs, y_specs = split_outs(y_shape)
    terms = kernel_call(
        weights_kernel,
        "weights",
        x_outs + y_outs,
        grid=(4,),
        in_specs=[smem, encoded_spec, encoded_spec] + [whole] * 4 + [query_spec] * 4,
        out_specs=x_specs + y_specs,
        scratch_shapes=[pltpu.VMEM((1, width // 4, half), f32)] * 2
        + [pltpu.VMEM((NY, 2, query_rows, answer), f32)],
    )(
        place,
        encoded,
        encoded_other,
        mine_a,
        mine_b,
        received_a,
        received_b,
        query_kept_a,
        query_kept_b,
        *query_received,
    )

    operands, specs = halving(terms, "xy", 4)
    chunk, query_shape = (2, NZ, 16, half // 2), (4, query_rows, half)
    chunk_outs, chunk_specs = split_outs(chunk)
    *second, query_grad = kernel_call(
        second_kernel,
        "second",
        chunk_outs * 2 + [like(query_shape, f32)],
        grid=(4,),
        in_specs=[smem] + specs,
        out_specs=chunk_specs * 2 + [blocks(query_shape)],
        scratch_shapes=[total(x_shape), total(y_shape)],
    )(place, *operands)
    query_grad = query_grad.reshape(4, query_rows, 2, answer).transpose(2, 0, 1, 3)
    query_grad = query_grad.reshape(PAIR, answer).T.astype(bf16)[None]

    operands, specs = halving(second, "yx", 1)
    last = kernel_call(
        last_kernel,
        "last",
        like((NZ, 16, features), bf16),
        grid=(1,),
        in_specs=specs,
        out_specs=pl.BlockSpec((NZ, 16, features), lambda i: (0, 0, 0)),
        scratch_shapes=[pltpu.VMEM((NZ, 16, half), f32)] * 2,
    )(*operands)
    gathered = tie(gathered, last)
    gathered_other = swap_cores(gathered)
    last = lax.all_to_all(
        last.reshape(NZ * NC, 8, features),
        AXES,
        0,
        0,
        tiled=True,
        axis_index_groups=groups(lambda z, x, y, c: (x, y)),
    )

    weight_spec = pl.BlockSpec((width // 4, features), lambda i: (i, 0))
    encoded_grad = kernel_call(
        encoded_kernel,
        "encoded",
        like((keys, width), bf16),
        flops=4 * keys * width * features,
        moved=14 * MIB,
        grid=(4,),
        in_specs=[whole] * 4 + [weight_spec] * 2,
        out_specs=pl.BlockSpec((keys, width // 4), lambda i: (0, i)),
    )(mine_a, mine_b, sent_a, sent_b, gathered, gathered_other)
    summed = tie(last, encoded_grad).reshape(NZ, NC, 8, features).astype(f32).sum(0)
    key_weight_grad, value_weight_grad = summed[0], summed[1]
    return query_grad, encoded_grad[None], key_weight_grad, value_weight_grad


def solution(mesh):
    return jax.shard_map(
        on_device,
        mesh=mesh,
        in_specs=(
            P("dp", None, None),
            P("dp", "passage", None),
            P("dp", "passage", None),
            P("dp", "passage", None),
            P("dp", None),
            P("dp", None),
            P("dp", None, None),
            P("dp"),
        ),
        out_specs=(
            P("dp", None, "passage"),
            P("dp", "passage", None),
            P(("dp", "passage"), None),
            P(("dp", "passage"), None),
        ),
        check_vma=False,
    )
```

time: 1490 us -> 133 us (0.09)
  waiting for transfers between devices: 1290 us -> 36.9 us
  blocking collectives: 70.9 us -> 0 us
  matrix products: 44.9 us -> 0 us
  starting transfers between devices: 0.3 us -> 41.7 us
  local copies, waits for them, and re-layouts: 39.3 us -> 7.18 us
  Pallas kernels: 0 us -> 31 us
  other arithmetic: 18.2 us -> 0.98 us
    unnamed x4 -> x1, waiting for transfers between devices: 1240 us -> 0.02 us
    all_gather x1, waiting for transfers between devices: 53 us -> 0.01 us  [on_device(): lax.all_gather(ordered, AXES, axis=0, tiled=True, axis_index_groups=group...]
    psum x2 -> x0, blocking collectives: 47.1 us -> none  [the longest x1 23.6 us: on_device(): row_total = lax.psum(jnp.sum(expo, axis=-1), 'passage')]
    dot_general x7 -> x0, matrix products: 44.9 us -> none  [the longest x1 9.76 us: on_device(): jnp.einsum('kd,kf->df', encoder_flat, joined, preferred_element_type=jnp....]
    ppermute x0 -> x29, waiting for transfers between devices: none -> 35.5 us  [the longest x22 30.2 us: send(): return lax.ppermute(value, AXES, links)]
    ppermute x0 -> x29, starting transfers between devices: none -> 33.1 us  [the longest x22 23.1 us: send(): return lax.ppermute(value, AXES, links)]
    pallas_call x0 -> x11, Pallas kernels: none -> 31 us  [the longest x1 7.35 us: on_device(): kernel_call(encoded_kernel, 'encoded', like((keys, width), bf16), flops=4...]
    pmax x1 -> x0, blocking collectives: 23.8 us -> none  [on_device(): row_max = lax.pmax(local_max, 'passage')]
  transfers between devices with their start and end apart: 3 -> 31, of which waited for: 2 -> 16; matrix products, arithmetic and copies ran while one was open for 4% -> 1% of each run, Pallas kernels for 0% -> 23%
where the time goes in v2:
time: 133 us
  starting transfers between devices  41.7 us (31%)
  waiting for transfers between devices  36.9 us (28%)
  Pallas kernels  31 us (23%)
  between operations  15 us (11%)
  local copies, waits for them, and re-layouts  7.18 us (5%)
    ppermute x22, waiting for transfers between devices, send(): return lax.ppermute(value, AXES, links)  30.2 us
    ppermute x22, starting transfers between devices, send(): return lax.ppermute(value, AXES, links)  23.1 us
    ppermute x7, starting transfers between devices, swap_cores(): lax.ppermute(value, AXES, permutation(lambda z, x, y, c: (z, x, y, 1 - c)))  9.97 us
    all_to_all x1, starting transfers between devices, on_device(): lax.all_to_all(last.reshape(NZ * NC, 8, features), AXES, 0, 0, tiled=True...  8.58 us
    pallas_call x1, Pallas kernels, on_device(): kernel_call(encoded_kernel, 'encoded', like((keys, width), bf16), flops=4...  7.35 us
    pallas_call x1, Pallas kernels, on_device(): kernel_call(weights_kernel, 'weights', x_outs + y_outs, grid=(4,), in_spe...  7.08 us
    pallas_call x2, Pallas kernels, grads(): kernel_call(functools.partial(grads_kernel, first_pair), 'grads', [like((...  6.85 us
    unnamed x33, local copies, waits for them, and re-layouts  6.46 us
  transfers between devices with their start and end apart: 31, of which 16 were waited for; matrix products, arithmetic and copies ran while one was open for 1% of the time, Pallas kernels for 23%

profile of v2, /device:TPU:1, one launch (start us, length us, event | category | flops | bytes accessed | tf_op | source)
XLA Modules:
  0.0 132.7 jit_solution(570709829660244431)
XLA Ops:
  7.2 0.0 all-gather.2.cloned.1.call-start
  7.2 0.9 broadcast_select_fusion.refs_0_
  8.2 2.1 %collective-permute-start.1 = (bf16[64,1024]{1,0:T(8,128)(2,1)S(1)}, bf16[64,1024]{1,0:T(8,128)(2,1)S(1)}, u32[]{:S(2)}, u32[]{:S(2)}) collective-permute-start(bf16[64,1024]{1,0:T(8,128)(2,1)S(1)} %broadcast_select_fusion.refs_0_), channel_id=1, source_target_pairs={{0,8},{1,9},{2,10},{3,11},{4,12},{5,13},{6,14},{7,15},{8,16},{9,17... | collective-permute-start | bytes 393224 | tf_op jit(solution)/shard_map/ppermute | solution.py:277
  10.3 2.5 %collective-permute-start.2 = (bf16[64,1024]{1,0:T(8,128)(2,1)S(1)}, bf16[64,1024]{1,0:T(8,128)(2,1)S(1)}, u32[]{:S(2)}, u32[]{:S(2)}) collective-permute-start(bf16[64,1024]{1,0:T(8,128)(2,1)S(1)} %broadcast_select_fusion.refs_0_), channel_id=1, source_target_pairs={{0,16},{1,17},{2,18},{3,19},{4,20},{5,21},{6,22},{7,23},{8,24},{9,... | collective-permute-start | bytes 393224 | tf_op jit(solution)/shard_map/ppermute | solution.py:277
  12.7 1.2 collective-permute-start.3
  14.5 0.0 copy-start
  14.5 0.0 copy-start.2
  14.6 6.3 %stats.1.left_ref = f32[24,512]{1,0:T(8,128)} custom-call(s32[1]{0:T(128)S(6)} %copy.18.length_ref, bf16[256,1024]{1,0:T(8,128)(2,1)} %bitcast.39, bf16[512,1024]{1,0:T(8,128)(2,1)} %bitcast.33, bf16[512,1024]{1,0:T(8,128)(2,1)} %bitcast.36, bf16[256,1024]{1,0:T(8,128)(2,1)} %bitcast.42), custom_call_target="tpu_custom_call" | custom-call | tf_op jit(solution)/shard_map/stats/pallas_call | solution.py:341
  20.8 0.1 stack.35.place_ref
  21.0 1.0 arrange.1
  22.0 0.8 copy-done.5
  22.8 0.0 all-gather.2.cloned.1.call-update
  22.8 1.6 %collective-permute-start = (bf16[512,2048]{1,0:T(8,128)(2,1)}, bf16[512,2048]{1,0:T(8,128)(2,1)S(1)}, u32[]{:S(2)}, u32[]{:S(2)}) collective-permute-start(bf16[512,2048]{1,0:T(8,128)(2,1)} %bitcast.45), channel_id=1, source_target_pairs={{0,1},{1,0},{2,3},{3,2},{4,5},{5,4},{6,7},{7,6},{8,9},{9,8},{10,11... | collective-permute-start | bytes 6291464 | tf_op jit(solution)/shard_map/ppermute | solution.py:46
  24.4 0.1 collective-permute-start.4
  24.5 4.0 %collective-permute-done.4.right_ref = f32[24,512]{1,0:T(8,128)S(1)} collective-permute-done((f32[24,512]{1,0:T(8,128)}, f32[24,512]{1,0:T(8,128)S(1)}, u32[]{:S(2)}, u32[]{:S(2)}) %collective-permute-start.4) | collective-permute-done | bytes 49184 | tf_op jit(solution)/shard_map/ppermute | solution.py:46
  28.5 0.8 copy-done.10
  29.3 1.4 %collective-permute-start.5 = (f32[24,512]{1,0:T(8,128)S(1)}, f32[24,512]{1,0:T(8,128)S(1)}, u32[]{:S(2)}, u32[]{:S(2)}) collective-permute-start(f32[24,512]{1,0:T(8,128)S(1)} %merge.1.refs_0_), channel_id=1, source_target_pairs={{0,2},{1,3},{2,4},{3,5},{4,6},{5,7},{6,0},{7,1},{8,10},{9,11},{10,... | collective-permute-start | bytes 147464 | tf_op jit(solution)/shard_map/ppermute | solution.py:277
  30.7 2.6 %collective-permute-start.6 = (f32[24,512]{1,0:T(8,128)S(1)}, f32[24,512]{1,0:T(8,128)S(1)}, u32[]{:S(2)}, u32[]{:S(2)}) collective-permute-start(f32[24,512]{1,0:T(8,128)S(1)} %merge.1.refs_0_), channel_id=1, source_target_pairs={{0,4},{1,5},{2,6},{3,7},{4,0},{5,1},{6,2},{7,3},{8,12},{9,13},{10,... | collective-permute-start | bytes 147464 | tf_op jit(solution)/shard_map/ppermute | solution.py:277
  33.3 1.1 collective-permute-start.7
  34.4 1.2 collective-permute-done.6.refs_2_
  35.5 1.0 collective-permute-done.7.refs_3_
  36.5 1.0 copy-done.3
  37.6 3.4 %grads.3 = (bf16[512,512]{1,0:T(8,128)(2,1)S(1)}, bf16[512,512]{1,0:T(8,128)(2,1)S(1)}, f32[2,128,256]{2,1,0:T(8,128)S(1)}, bf16[2,128,256]{2,1,0:T(8,128)(2,1)S(1)}) custom-call(s32[1]{0:T(128)} %bitcast.9.core_ref, s32[1]{0:T(128)S(6)} %copy.18.length_ref, bf16[256,1024]{1,0:T(8,128)(2,1)S(1)} %bitcast.40, bf16[512,1024]{1,0:T(8,128)(2,1)S(1)} %bitcast.34, ...), custom_call_target="tpu_custom_call" | custom-call | tf_op jit(solution)/shard_map/grads/pallas_call | solution.py:376
  41.0 1.9 %collective-permute-start.9 = (bf16[512,512]{1,0:T(8,128)(2,1)S(1)}, bf16[512,512]{1,0:T(8,128)(2,1)S(1)}, u32[]{:S(2)}, u32[]{:S(2)}) collective-permute-start(bf16[512,512]{1,0:T(8,128)(2,1)S(1)} %get-tuple-element.68.refs_3_), channel_id=1, source_target_pairs={{0,1},{1,0},{2,3},{3,2},{4,5},{5,4},{6,7},{7,6},{8,9},{9,8},{10,11... | collective-permute-start | bytes 1572872 | tf_op jit(solution)/shard_map/ppermute | solution.py:46
  42.9 3.4 %grads.2 = (bf16[512,512]{1,0:T(8,128)(2,1)S(1)}, bf16[512,512]{1,0:T(8,128)(2,1)S(1)}, f32[2,128,256]{2,1,0:T(8,128)S(1)}, bf16[2,128,256]{2,1,0:T(8,128)(2,1)S(1)}) custom-call(s32[1]{0:T(128)} %bitcast.9.core_ref, s32[1]{0:T(128)S(6)} %copy.18.length_ref, bf16[256,1024]{1,0:T(8,128)(2,1)S(1)} %bitcast.41, bf16[512,1024]{1,0:T(8,128)(2,1)S(1)} %bitcast.35, ...), custom_call_target="tpu_custom_call" | custom-call | tf_op jit(solution)/shard_map/grads/pallas_call | solution.py:376
  46.4 0.1 collective-permute-start.8
  46.5 0.9 copy-done.14
  47.4 0.4 collective-permute-start.11
  47.8 0.1 collective-permute-start.10
  47.9 0.9 collective-permute-done.11.refs_7_
  48.8 0.4 collective-permute-done.10.refs_6_
  49.2 7.1 %weights.1 = (f32[2,8,64,256]{3,2,1,0:T(8,128)S(1)}, bf16[2,8,64,256]{3,2,1,0:T(8,128)(2,1)S(1)}, f32[2,8,64,256]{3,2,1,0:T(8,128)S(1)}, bf16[2,8,64,256]{3,2,1,...) custom-call(s32[8]{0:T(128)S(1)} %stack.35.place_ref, ...), custom_call_target="tpu_custom_call" | custom-call | tf_op jit(solution)/shard_map/weights/pallas_call | solution.py:415
  56.3 0.1 collective-permute-start.14
  56.4 2.3 %collective-permute-start.15 = (bf16[2,4,144,256]{3,2,1,0:T(8,128)(2,1)S(1)}, bf16[2,4,144,256]{3,2,1,0:T(8,128)(2,1)S(1)}, u32[]{:S(2)}, u32[]{:S(2)}) collective-permute-start(bf16[2,4,144,256]{3,2,1,0:T(8,128)(2,1)S(1)} %get-tuple-element.78), channel_id=1, source_target_pairs={{0,6},{1,7},{2,4},{3,5},{4,2},{5,3},{6,0},{7,1},{8,14},{9,15},{10,... | collective-permute-start | bytes 1769480 | tf_op jit(solution)/shard_map/ppermute | solution.py:277
  58.7 0.3 collective-permute-start.12
  59.0 0.3 collective-permute-start.13
  59.3 12.6 %collective-permute-done.12.refs_4_.refs_2_ = bf16[2,8,64,256]{3,2,1,0:T(8,128)(2,1)S(1)} collective-permute-done((bf16[2,8,64,256]{3,2,1,0:T(8,128)(2,1)S(1)}, bf16[2,8,64,256]{3,2,1,0:T(8,128)(2,1)S(1)}, u32[]{:S(2)}, u32[]{:S(2)}) %collective-permute-start.12) | collective-permute-done | bytes 524320 | tf_op jit(solution)/shard_map/ppermute | solution.py:277
  71.9 1.2 collective-permute-done.13.refs_5_.refs_3_
  73.1 0.3 middle.2
  73.3 1.8 %collective-permute-start.18 = (bf16[4,144,256]{2,1,0:T(8,128)(2,1)S(1)}, bf16[4,144,256]{2,1,0:T(8,128)(2,1)S(1)}, u32[]{:S(2)}, u32[]{:S(2)}) collective-permute-start(bf16[4,144,256]{2,1,0:T(8,128)(2,1)S(1)} %get-tuple-element.87), channel_id=1, source_target_pairs={{0,6},{1,7},{2,4},{3,5},{4,2},{5,3},{6,0},{7,1},{8,14},{9,15},{10,... | collective-permute-start | bytes 884744 | tf_op jit(solution)/shard_map/ppermute | solution.py:277
  75.2 0.3 collective-permute-start.17
  75.5 7.5 %collective-permute-done.16.refs_4_ = bf16[8,64,256]{2,1,0:T(8,128)(2,1)S(1)} collective-permute-done((bf16[8,64,256]{2,1,0:T(8,128)(2,1)S(1)}, bf16[8,64,256]{2,1,0:T(8,128)(2,1)S(1)}, u32[]{:S(2)}, u32[]{:S(2)}) %collective-permute-start.16) | collective-permute-done | bytes 262176 | tf_op jit(solution)/shard_map/ppermute | solution.py:277
  83.0 1.3 second.1
  84.3 1.3 collective-permute-start.20
  85.6 0.3 collective-permute-start.21
  85.9 1.4 %collective-permute-start.23 = (bf16[2,8,16,256]{3,2,1,0:T(8,128)(2,1)S(1)}, bf16[2,8,16,256]{3,2,1,0:T(8,128)(2,1)S(1)}, u32[]{:S(2)}, u32[]{:S(2)}) collective-permute-start(bf16[2,8,16,256]{3,2,1,0:T(8,128)(2,1)S(1)} %get-tuple-element.99), channel_id=1, source_target_pairs={{0,24},{1,25},{2,26},{3,27},{4,28},{5,29},{6,30},{7,31},{8,16},{9,... | collective-permute-start | bytes 393224 | tf_op jit(solution)/shard_map/ppermute | solution.py:277
  87.3 0.9 collective-permute-done.20.refs_4_.refs_2_
  88.2 2.4 %collective-permute-done.21.refs_5_.refs_3_ = bf16[2,8,16,256]{3,2,1,0:T(8,128)(2,1)S(1)} collective-permute-done((bf16[2,8,16,256]{3,2,1,0:T(8,128)(2,1)S(1)}, bf16[2,8,16,256]{3,2,1,0:T(8,128)(2,1)S(1)}, u32[]{:S(2)}, u32[]{:S(2)}) %collective-permute-start.21) | collective-permute-done | bytes 131104 | tf_op jit(solution)/shard_map/ppermute | solution.py:277
  90.6 0.3 collective-permute-done.23.refs_7_.refs_9_
  90.9 0.1 middle.3
  91.0 2.8 %collective-permute-start.24 = (bf16[8,16,256]{2,1,0:T(8,128)(2,1)S(1)}, bf16[8,16,256]{2,1,0:T(8,128)(2,1)S(1)}, u32[]{:S(2)}, u32[]{:S(2)}) collective-permute-start(bf16[8,16,256]{2,1,0:T(8,128)(2,1)S(1)} %get-tuple-element.106), channel_id=1, source_target_pairs={{0,6},{1,7},{2,4},{3,5},{4,2},{5,3},{6,0},{7,1},{8,14},{9,15},{10,... | collective-permute-start | bytes 196616 | tf_op jit(solution)/shard_map/ppermute | solution.py:277
  93.8 1.4 %collective-permute-start.26 = (bf16[8,16,256]{2,1,0:T(8,128)(2,1)S(1)}, bf16[8,16,256]{2,1,0:T(8,128)(2,1)S(1)}, u32[]{:S(2)}, u32[]{:S(2)}) collective-permute-start(bf16[8,16,256]{2,1,0:T(8,128)(2,1)S(1)} %get-tuple-element.108), channel_id=1, source_target_pairs={{0,24},{1,25},{2,26},{3,27},{4,28},{5,29},{6,30},{7,31},{8,16},{9,... | collective-permute-start | bytes 196616 | tf_op jit(solution)/shard_map/ppermute | solution.py:277
  95.2 0.2 collective-permute-done.24.refs_4_
  95.4 1.5 %collective-permute-done.25.refs_5_ = bf16[8,16,256]{2,1,0:T(8,128)(2,1)S(1)} collective-permute-done((bf16[8,16,256]{2,1,0:T(8,128)(2,1)S(1)}, bf16[8,16,256]{2,1,0:T(8,128)(2,1)S(1)}, u32[]{:S(2)}, u32[]{:S(2)}) %collective-permute-start.25) | collective-permute-done | bytes 65568 | tf_op jit(solution)/shard_map/ppermute | solution.py:277
  96.9 1.2 collective-permute-done.26.refs_10_
  98.1 0.2 collective-permute-done.27.refs_11_
  98.3 0.8 last.1
  99.1 5.8 %collective-permute-start.28 = (bf16[2048,1024]{1,0:T(8,128)(2,1)}, bf16[2048,1024]{1,0:T(8,128)(2,1)}, u32[]{:S(2)}, u32[]{:S(2)}) collective-permute-start(bf16[2048,1024]{1,0:T(8,128)(2,1)} %all-gather.2.cloned.1.call-done.refs_4_), channel_id=1, source_target_pairs={{0,1},{1,0},{2,3},{3,2},{4,5},{5,4},{6,7},{7,6},{8,9},{9,8},{10,11... | collective-permute-start | bytes 12582920 | tf_op jit(solution)/shard_map/ppermute | solution.py:46
  104.9 8.6 %all-to-all-start = ((bf16[16,8,1024]{2,1,0:T(8,128)(2,1)}), bf16[16,8,1024]{2,1,0:T(8,128)(2,1)S(1)}, u32[]{:S(2)}, u32[]{:S(2)}) async-start(bf16[16,8,1024]{2,1,0:T(8,128)(2,1)} %bitcast.19), calls=%async_computation | async-start | bytes 524288 | tf_op jit(solution)/shard_map/all_to_all | solution.py:464
  113.5 0.7 copy.14
  114.2 2.2 %copy-done.11 = bf16[2048,1024]{1,0:T(8,128)(2,1)S(1)} copy-done((bf16[2048,1024]{1,0:T(8,128)(2,1)S(1)}, bf16[2048,1024]{1,0:T(8,128)(2,1)}, u32[]{:S(2)}) %copy-start.11) | copy-done | bytes 4194328
  116.4 7.4 %encoded.1 = bf16[512,2048]{1,0:T(8,128)(2,1)} custom-call(bf16[512,512]{1,0:T(8,128)(2,1)S(1)} %copy-done.9, bf16[512,512]{1,0:T(8,128)(2,1)S(1)} %copy-done.7, bf16[512,512]{1,0:T(8,128)(2,1)S(1)} %copy-done.15, bf16[512,512]{1,0:T(8,128)(2,1)S(1)} %copy-done.13, bf16[2048,1024]{1,0:T(8,128)(2,1)S(1)} %copy-done.11, ...), custom_call_target="tpu_custom_call" | custom-call | flops 4294967296 | bytes 14680064 | tf_op jit(solution)/shard_map/encoded/pallas_call | solution.py:474
  123.8 1.4 %all-to-all-done = bf16[16,8,1024]{2,1,0:T(8,128)(2,1)S(1)} async-done(((bf16[16,8,1024]{2,1,0:T(8,128)(2,1)}), bf16[16,8,1024]{2,1,0:T(8,128)(2,1)S(1)}, u32[]{:S(2)}, u32[]{:S(2)}) %all-to-all-start) | async-done | bytes 262176 | tf_op jit(solution)/shard_map/all_to_all | solution.py:464
  125.2 0.6 slice_bitcast_fusion
  (49 shorter events, 0.2 us)
Async XLA Ops:
  7.2 91.9 %all-gather.2.cloned.1.call-start = ((), (), s32[]{:S(2)}) async-start(), calls=%async_computation.1 | async-start | bytes 4718592 | tf_op jit(solution)/shard_map/all_gather | solution.py:360
  8.2 12.8 %collective-permute-start.1 = (bf16[64,1024]{1,0:T(8,128)(2,1)S(1)}, bf16[64,1024]{1,0:T(8,128)(2,1)S(1)}, u32[]{:S(2)}, u32[]{:S(2)}) collective-permute-start(bf16[64,1024]{1,0:T(8,128)(2,1)S(1)} %broadcast_select_fusion.refs_0_), channel_id=1, source_target_pairs={{0,8},{1,9},{2,10},{3,11},{4,12},{5,13},{6,14},{7,15},{8,16},{9,17... | collective-permute-start | bytes 393224 | tf_op jit(solution)/shard_map/ppermute | solution.py:277
  10.3 10.7 %collective-permute-start.2 = (bf16[64,1024]{1,0:T(8,128)(2,1)S(1)}, bf16[64,1024]{1,0:T(8,128)(2,1)S(1)}, u32[]{:S(2)}, u32[]{:S(2)}) collective-permute-start(bf16[64,1024]{1,0:T(8,128)(2,1)S(1)} %broadcast_select_fusion.refs_0_), channel_id=1, source_target_pairs={{0,16},{1,17},{2,18},{3,19},{4,20},{5,21},{6,22},{7,23},{8,24},{9,... | collective-permute-start | bytes 393224 | tf_op jit(solution)/shard_map/ppermute | solution.py:277
  12.7 8.2 %collective-permute-start.3 = (bf16[64,1024]{1,0:T(8,128)(2,1)S(1)}, bf16[64,1024]{1,0:T(8,128)(2,1)}, u32[]{:S(2)}, u32[]{:S(2)}) collective-permute-start(bf16[64,1024]{1,0:T(8,128)(2,1)S(1)} %broadcast_select_fusion.refs_0_), channel_id=1, source_target_pairs={{0,24},{1,25},{2,26},{3,27},{4,28},{5,29},{6,30},{7,31},{8,0},{9,1... | collective-permute-start | bytes 393224 | tf_op jit(solution)/shard_map/ppermute | solution.py:277
  14.5 22.0 %copy-start = (bf16[1,512,1024]{2,1,0:T(8,128)(2,1)S(1)}, bf16[1,512,1024]{2,1,0:T(8,128)(2,1)}, u32[]{:S(2)}) copy-start(bf16[1,512,1024]{2,1,0:T(8,128)(2,1)} %param.9) | copy-start | bytes 3145732
  14.5 22.0 %copy-start.2 = (bf16[1,256,1024]{2,1,0:T(8,128)(2,1)S(1)}, bf16[1,256,1024]{2,1,0:T(8,128)(2,1)}, u32[]{:S(2)}) copy-start(bf16[1,256,1024]{2,1,0:T(8,128)(2,1)} %param.8) | copy-start | bytes 1572868
  20.8 15.7 %copy-start.1 = (bf16[1,512,1024]{2,1,0:T(8,128)(2,1)S(1)}, bf16[1,512,1024]{2,1,0:T(8,128)(2,1)}, u32[]{:S(2)}) copy-start(bf16[1,512,1024]{2,1,0:T(8,128)(2,1)} %param.10) | copy-start | bytes 3145732
  22.0 0.8 copy-start.5
  22.8 26.3 %collective-permute-start = (bf16[512,2048]{1,0:T(8,128)(2,1)}, bf16[512,2048]{1,0:T(8,128)(2,1)S(1)}, u32[]{:S(2)}, u32[]{:S(2)}) collective-permute-start(bf16[512,2048]{1,0:T(8,128)(2,1)} %bitcast.45), channel_id=1, source_target_pairs={{0,1},{1,0},{2,3},{3,2},{4,5},{5,4},{6,7},{7,6},{8,9},{9,8},{10,11... | collective-permute-start | bytes 6291464 | tf_op jit(solution)/shard_map/ppermute | solution.py:46
  24.4 4.1 %collective-permute-start.4 = (f32[24,512]{1,0:T(8,128)}, f32[24,512]{1,0:T(8,128)S(1)}, u32[]{:S(2)}, u32[]{:S(2)}) collective-permute-start(f32[24,512]{1,0:T(8,128)} %stats.1.left_ref), channel_id=1, source_target_pairs={{0,1},{1,0},{2,3},{3,2},{4,5},{5,4},{6,7},{7,6},{8,9},{9,8},{10,11... | collective-permute-start | bytes 147464 | tf_op jit(solution)/shard_map/ppermute | solution.py:46
  28.5 0.8 copy-start.10
  29.3 5.1 %collective-permute-start.5 = (f32[24,512]{1,0:T(8,128)S(1)}, f32[24,512]{1,0:T(8,128)S(1)}, u32[]{:S(2)}, u32[]{:S(2)}) collective-permute-start(f32[24,512]{1,0:T(8,128)S(1)} %merge.1.refs_0_), channel_id=1, source_target_pairs={{0,2},{1,3},{2,4},{3,5},{4,6},{5,7},{6,0},{7,1},{8,10},{9,11},{10,... | collective-permute-start | bytes 147464 | tf_op jit(solution)/shard_map/ppermute | solution.py:277
  30.7 4.9 %collective-permute-start.6 = (f32[24,512]{1,0:T(8,128)S(1)}, f32[24,512]{1,0:T(8,128)S(1)}, u32[]{:S(2)}, u32[]{:S(2)}) collective-permute-start(f32[24,512]{1,0:T(8,128)S(1)} %merge.1.refs_0_), channel_id=1, source_target_pairs={{0,4},{1,5},{2,6},{3,7},{4,0},{5,1},{6,2},{7,3},{8,12},{9,13},{10,... | collective-permute-start | bytes 147464 | tf_op jit(solution)/shard_map/ppermute | solution.py:277
  33.3 3.2 %collective-permute-start.7 = (f32[24,512]{1,0:T(8,128)S(1)}, f32[24,512]{1,0:T(8,128)S(1)}, u32[]{:S(2)}, u32[]{:S(2)}) collective-permute-start(f32[24,512]{1,0:T(8,128)S(1)} %merge.1.refs_0_), channel_id=1, source_target_pairs={{0,6},{1,7},{2,0},{3,1},{4,2},{5,3},{6,4},{7,5},{8,14},{9,15},{10,... | collective-permute-start | bytes 147464 | tf_op jit(solution)/shard_map/ppermute | solution.py:277
  36.5 1.0 copy-start.3
  41.0 8.2 %copy-start.12 = (bf16[512,512]{1,0:T(8,128)(2,1)}, bf16[512,512]{1,0:T(8,128)(2,1)S(1)}, u32[]{:S(2)}) copy-start(bf16[512,512]{1,0:T(8,128)(2,1)S(1)} %get-tuple-element.68.refs_3_) | copy-start | bytes 1572868
  41.0 15.3 %copy-start.6 = (bf16[512,512]{1,0:T(8,128)(2,1)}, bf16[512,512]{1,0:T(8,128)(2,1)S(1)}, u32[]{:S(2)}) copy-start(bf16[512,512]{1,0:T(8,128)(2,1)S(1)} %get-tuple-element.66.refs_1_) | copy-start | bytes 1572868
  41.0 8.2 %copy-start.4 = (bf16[1,512,2048]{2,1,0:T(8,128)(2,1)S(1)}, bf16[1,512,2048]{2,1,0:T(8,128)(2,1)}, u32[]{:S(2)}) copy-start(bf16[1,512,2048]{2,1,0:T(8,128)(2,1)} %param.11) | copy-start | bytes 6291460
  41.0 8.1 %collective-permute-start.9 = (bf16[512,512]{1,0:T(8,128)(2,1)S(1)}, bf16[512,512]{1,0:T(8,128)(2,1)S(1)}, u32[]{:S(2)}, u32[]{:S(2)}) collective-permute-start(bf16[512,512]{1,0:T(8,128)(2,1)S(1)} %get-tuple-element.68.refs_3_), channel_id=1, source_target_pairs={{0,1},{1,0},{2,3},{3,2},{4,5},{5,4},{6,7},{7,6},{8,9},{9,8},{10,11... | collective-permute-start | bytes 1572872 | tf_op jit(solution)/shard_map/ppermute | solution.py:46
  46.4 9.9 %copy-start.8 = (bf16[512,512]{1,0:T(8,128)(2,1)}, bf16[512,512]{1,0:T(8,128)(2,1)S(1)}, u32[]{:S(2)}) copy-start(bf16[512,512]{1,0:T(8,128)(2,1)S(1)} %get-tuple-element.65.refs_0_) | copy-start | bytes 1572868
  46.4 2.8 %collective-permute-start.8 = (bf16[512,512]{1,0:T(8,128)(2,1)S(1)}, bf16[512,512]{1,0:T(8,128)(2,1)S(1)}, u32[]{:S(2)}, u32[]{:S(2)}) collective-permute-start(bf16[512,512]{1,0:T(8,128)(2,1)S(1)} %get-tuple-element.67.refs_2_), channel_id=1, source_target_pairs={{0,1},{1,0},{2,3},{3,2},{4,5},{5,4},{6,7},{7,6},{8,9},{9,8},{10,11... | collective-permute-start | bytes 1572872 | tf_op jit(solution)/shard_map/ppermute | solution.py:46
  46.5 0.9 copy-start.14
  47.4 1.4 %collective-permute-start.11 = (bf16[2,128,256]{2,1,0:T(8,128)(2,1)S(1)}, bf16[2,128,256]{2,1,0:T(8,128)(2,1)S(1)}, u32[]{:S(2)}, u32[]{:S(2)}) collective-permute-start(bf16[2,128,256]{2,1,0:T(8,128)(2,1)S(1)} %get-tuple-element.72), channel_id=1, source_target_pairs={{0,1},{1,0},{2,3},{3,2},{4,5},{5,4},{6,7},{7,6},{8,9},{9,8},{10,11... | collective-permute-start | bytes 393224 | tf_op jit(solution)/shard_map/ppermute | solution.py:46
  47.8 1.3 %collective-permute-start.10 = (bf16[2,128,256]{2,1,0:T(8,128)(2,1)S(1)}, bf16[2,128,256]{2,1,0:T(8,128)(2,1)S(1)}, u32[]{:S(2)}, u32[]{:S(2)}) collective-permute-start(bf16[2,128,256]{2,1,0:T(8,128)(2,1)S(1)} %get-tuple-element.71), channel_id=1, source_target_pairs={{0,1},{1,0},{2,3},{3,2},{4,5},{5,4},{6,7},{7,6},{8,9},{9,8},{10,11... | collective-permute-start | bytes 393224 | tf_op jit(solution)/shard_map/ppermute | solution.py:46
  56.3 16.8 %collective-permute-start.14 = (bf16[2,4,144,256]{3,2,1,0:T(8,128)(2,1)S(1)}, bf16[2,4,144,256]{3,2,1,0:T(8,128)(2,1)S(1)}, u32[]{:S(2)}, u32[]{:S(2)}) collective-permute-start(bf16[2,4,144,256]{3,2,1,0:T(8,128)(2,1)S(1)} %get-tuple-element.77), channel_id=1, source_target_pairs={{0,2},{1,3},{2,0},{3,1},{4,6},{5,7},{6,4},{7,5},{8,10},{9,11},{10,... | collective-permute-start | bytes 1769480 | tf_op jit(solution)/shard_map/ppermute | solution.py:277
  56.4 16.7 %collective-permute-start.15 = (bf16[2,4,144,256]{3,2,1,0:T(8,128)(2,1)S(1)}, bf16[2,4,144,256]{3,2,1,0:T(8,128)(2,1)S(1)}, u32[]{:S(2)}, u32[]{:S(2)}) collective-permute-start(bf16[2,4,144,256]{3,2,1,0:T(8,128)(2,1)S(1)} %get-tuple-element.78), channel_id=1, source_target_pairs={{0,6},{1,7},{2,4},{3,5},{4,2},{5,3},{6,0},{7,1},{8,14},{9,15},{10,... | collective-permute-start | bytes 1769480 | tf_op jit(solution)/shard_map/ppermute | solution.py:277
  58.7 13.1 %collective-permute-start.12 = (bf16[2,8,64,256]{3,2,1,0:T(8,128)(2,1)S(1)}, bf16[2,8,64,256]{3,2,1,0:T(8,128)(2,1)S(1)}, u32[]{:S(2)}, u32[]{:S(2)}) collective-permute-start(bf16[2,8,64,256]{3,2,1,0:T(8,128)(2,1)S(1)} %get-tuple-element.75), channel_id=1, source_target_pairs={{0,8},{1,9},{2,10},{3,11},{4,12},{5,13},{6,14},{7,15},{8,0},{9,1},... | collective-permute-start | bytes 1572872 | tf_op jit(solution)/shard_map/ppermute | solution.py:277
  59.0 14.0 %collective-permute-start.13 = (bf16[2,8,64,256]{3,2,1,0:T(8,128)(2,1)S(1)}, bf16[2,8,64,256]{3,2,1,0:T(8,128)(2,1)S(1)}, u32[]{:S(2)}, u32[]{:S(2)}) collective-permute-start(bf16[2,8,64,256]{3,2,1,0:T(8,128)(2,1)S(1)} %get-tuple-element.76), channel_id=1, source_target_pairs={{0,24},{1,25},{2,26},{3,27},{4,28},{5,29},{6,30},{7,31},{8,16},{9,... | collective-permute-start | bytes 1572872 | tf_op jit(solution)/shard_map/ppermute | solution.py:277
  73.3 9.7 %collective-permute-start.18 = (bf16[4,144,256]{2,1,0:T(8,128)(2,1)S(1)}, bf16[4,144,256]{2,1,0:T(8,128)(2,1)S(1)}, u32[]{:S(2)}, u32[]{:S(2)}) collective-permute-start(bf16[4,144,256]{2,1,0:T(8,128)(2,1)S(1)} %get-tuple-element.87), channel_id=1, source_target_pairs={{0,6},{1,7},{2,4},{3,5},{4,2},{5,3},{6,0},{7,1},{8,14},{9,15},{10,... | collective-permute-start | bytes 884744 | tf_op jit(solution)/shard_map/ppermute | solution.py:277
  75.2 7.9 %collective-permute-start.19 = (bf16[4,144,256]{2,1,0:T(8,128)(2,1)S(1)}, bf16[4,144,256]{2,1,0:T(8,128)(2,1)S(1)}, u32[]{:S(2)}, u32[]{:S(2)}) collective-permute-start(bf16[4,144,256]{2,1,0:T(8,128)(2,1)S(1)} %get-tuple-element.88), channel_id=1, source_target_pairs={{0,2},{1,3},{2,0},{3,1},{4,6},{5,7},{6,4},{7,5},{8,10},{9,11},{10,... | collective-permute-start | bytes 884744 | tf_op jit(solution)/shard_map/ppermute | solution.py:277
  75.2 7.9 %collective-permute-start.16 = (bf16[8,64,256]{2,1,0:T(8,128)(2,1)S(1)}, bf16[8,64,256]{2,1,0:T(8,128)(2,1)S(1)}, u32[]{:S(2)}, u32[]{:S(2)}) collective-permute-start(bf16[8,64,256]{2,1,0:T(8,128)(2,1)S(1)} %get-tuple-element.85), channel_id=1, source_target_pairs={{0,24},{1,25},{2,26},{3,27},{4,28},{5,29},{6,30},{7,31},{8,16},{9,... | collective-permute-start | bytes 786440 | tf_op jit(solution)/shard_map/ppermute | solution.py:277
  75.2 7.9 %collective-permute-start.17 = (bf16[8,64,256]{2,1,0:T(8,128)(2,1)S(1)}, bf16[8,64,256]{2,1,0:T(8,128)(2,1)S(1)}, u32[]{:S(2)}, u32[]{:S(2)}) collective-permute-start(bf16[8,64,256]{2,1,0:T(8,128)(2,1)S(1)} %get-tuple-element.86), channel_id=1, source_target_pairs={{0,8},{1,9},{2,10},{3,11},{4,12},{5,13},{6,14},{7,15},{8,0},{9,1},... | collective-permute-start | bytes 786440 | tf_op jit(solution)/shard_map/ppermute | solution.py:277
  84.3 3.9 %collective-permute-start.20 = (bf16[2,8,16,256]{3,2,1,0:T(8,128)(2,1)S(1)}, bf16[2,8,16,256]{3,2,1,0:T(8,128)(2,1)S(1)}, u32[]{:S(2)}, u32[]{:S(2)}) collective-permute-start(bf16[2,8,16,256]{3,2,1,0:T(8,128)(2,1)S(1)} %get-tuple-element.96), channel_id=1, source_target_pairs={{0,2},{1,3},{2,0},{3,1},{4,6},{5,7},{6,4},{7,5},{8,10},{9,11},{10,... | collective-permute-start | bytes 393224 | tf_op jit(solution)/shard_map/ppermute | solution.py:277
  85.6 5.0 %collective-permute-start.21 = (bf16[2,8,16,256]{3,2,1,0:T(8,128)(2,1)S(1)}, bf16[2,8,16,256]{3,2,1,0:T(8,128)(2,1)S(1)}, u32[]{:S(2)}, u32[]{:S(2)}) collective-permute-start(bf16[2,8,16,256]{3,2,1,0:T(8,128)(2,1)S(1)} %get-tuple-element.97), channel_id=1, source_target_pairs={{0,6},{1,7},{2,4},{3,5},{4,2},{5,3},{6,0},{7,1},{8,14},{9,15},{10,... | collective-permute-start | bytes 393224 | tf_op jit(solution)/shard_map/ppermute | solution.py:277
  85.9 4.7 %collective-permute-start.22 = (bf16[2,8,16,256]{3,2,1,0:T(8,128)(2,1)S(1)}, bf16[2,8,16,256]{3,2,1,0:T(8,128)(2,1)S(1)}, u32[]{:S(2)}, u32[]{:S(2)}) collective-permute-start(bf16[2,8,16,256]{3,2,1,0:T(8,128)(2,1)S(1)} %get-tuple-element.98), channel_id=1, source_target_pairs={{0,8},{1,9},{2,10},{3,11},{4,12},{5,13},{6,14},{7,15},{8,0},{9,1},... | collective-permute-start | bytes 393224 | tf_op jit(solution)/shard_map/ppermute | solution.py:277
  85.9 5.0 %collective-permute-start.23 = (bf16[2,8,16,256]{3,2,1,0:T(8,128)(2,1)S(1)}, bf16[2,8,16,256]{3,2,1,0:T(8,128)(2,1)S(1)}, u32[]{:S(2)}, u32[]{:S(2)}) collective-permute-start(bf16[2,8,16,256]{3,2,1,0:T(8,128)(2,1)S(1)} %get-tuple-element.99), channel_id=1, source_target_pairs={{0,24},{1,25},{2,26},{3,27},{4,28},{5,29},{6,30},{7,31},{8,16},{9,... | collective-permute-start | bytes 393224 | tf_op jit(solution)/shard_map/ppermute | solution.py:277
  90.9 23.3 %copy-start.7 = (bf16[512,512]{1,0:T(8,128)(2,1)S(1)}, bf16[512,512]{1,0:T(8,128)(2,1)}, u32[]{:S(2)}) copy-start(bf16[512,512]{1,0:T(8,128)(2,1)} %copy-done.6) | copy-start | bytes 1572868
  90.9 23.3 %copy-start.9 = (bf16[512,512]{1,0:T(8,128)(2,1)S(1)}, bf16[512,512]{1,0:T(8,128)(2,1)}, u32[]{:S(2)}) copy-start(bf16[512,512]{1,0:T(8,128)(2,1)} %copy-done.8) | copy-start | bytes 1572868
  90.9 23.3 %copy-start.13 = (bf16[512,512]{1,0:T(8,128)(2,1)S(1)}, bf16[512,512]{1,0:T(8,128)(2,1)}, u32[]{:S(2)}) copy-start(bf16[512,512]{1,0:T(8,128)(2,1)} %copy-done.12) | copy-start | bytes 1572868
  90.9 23.3 %copy-start.15 = (bf16[512,512]{1,0:T(8,128)(2,1)S(1)}, bf16[512,512]{1,0:T(8,128)(2,1)}, u32[]{:S(2)}) copy-start(bf16[512,512]{1,0:T(8,128)(2,1)} %copy-done.14) | copy-start | bytes 1572868
  91.0 4.4 %collective-permute-start.24 = (bf16[8,16,256]{2,1,0:T(8,128)(2,1)S(1)}, bf16[8,16,256]{2,1,0:T(8,128)(2,1)S(1)}, u32[]{:S(2)}, u32[]{:S(2)}) collective-permute-start(bf16[8,16,256]{2,1,0:T(8,128)(2,1)S(1)} %get-tuple-element.106), channel_id=1, source_target_pairs={{0,6},{1,7},{2,4},{3,5},{4,2},{5,3},{6,0},{7,1},{8,14},{9,15},{10,... | collective-permute-start | bytes 196616 | tf_op jit(solution)/shard_map/ppermute | solution.py:277
  93.8 3.1 %collective-permute-start.25 = (bf16[8,16,256]{2,1,0:T(8,128)(2,1)S(1)}, bf16[8,16,256]{2,1,0:T(8,128)(2,1)S(1)}, u32[]{:S(2)}, u32[]{:S(2)}) collective-permute-start(bf16[8,16,256]{2,1,0:T(8,128)(2,1)S(1)} %get-tuple-element.107), channel_id=1, source_target_pairs={{0,2},{1,3},{2,0},{3,1},{4,6},{5,7},{6,4},{7,5},{8,10},{9,11},{10,... | collective-permute-start | bytes 196616 | tf_op jit(solution)/shard_map/ppermute | solution.py:277
  93.8 4.3 %collective-permute-start.26 = (bf16[8,16,256]{2,1,0:T(8,128)(2,1)S(1)}, bf16[8,16,256]{2,1,0:T(8,128)(2,1)S(1)}, u32[]{:S(2)}, u32[]{:S(2)}) collective-permute-start(bf16[8,16,256]{2,1,0:T(8,128)(2,1)S(1)} %get-tuple-element.108), channel_id=1, source_target_pairs={{0,24},{1,25},{2,26},{3,27},{4,28},{5,29},{6,30},{7,31},{8,16},{9,... | collective-permute-start | bytes 196616 | tf_op jit(solution)/shard_map/ppermute | solution.py:277
  95.2 3.1 %collective-permute-start.27 = (bf16[8,16,256]{2,1,0:T(8,128)(2,1)S(1)}, bf16[8,16,256]{2,1,0:T(8,128)(2,1)S(1)}, u32[]{:S(2)}, u32[]{:S(2)}) collective-permute-start(bf16[8,16,256]{2,1,0:T(8,128)(2,1)S(1)} %get-tuple-element.109), channel_id=1, source_target_pairs={{0,8},{1,9},{2,10},{3,11},{4,12},{5,13},{6,14},{7,15},{8,0},{9,1},... | collective-permute-start | bytes 196616 | tf_op jit(solution)/shard_map/ppermute | solution.py:277
  99.1 15.1 %collective-permute-start.28 = (bf16[2048,1024]{1,0:T(8,128)(2,1)}, bf16[2048,1024]{1,0:T(8,128)(2,1)}, u32[]{:S(2)}, u32[]{:S(2)}) collective-permute-start(bf16[2048,1024]{1,0:T(8,128)(2,1)} %all-gather.2.cloned.1.call-done.refs_4_), channel_id=1, source_target_pairs={{0,1},{1,0},{2,3},{3,2},{4,5},{5,4},{6,7},{7,6},{8,9},{9,8},{10,11... | collective-permute-start | bytes 12582920 | tf_op jit(solution)/shard_map/ppermute | solution.py:46
  104.9 20.3 %all-to-all-start = ((bf16[16,8,1024]{2,1,0:T(8,128)(2,1)}), bf16[16,8,1024]{2,1,0:T(8,128)(2,1)S(1)}, u32[]{:S(2)}, u32[]{:S(2)}) async-start(bf16[16,8,1024]{2,1,0:T(8,128)(2,1)} %bitcast.19), calls=%async_computation | async-start | bytes 524288 | tf_op jit(solution)/shard_map/all_to_all | solution.py:464
  114.2 2.2 %copy-start.11 = (bf16[2048,1024]{1,0:T(8,128)(2,1)S(1)}, bf16[2048,1024]{1,0:T(8,128)(2,1)}, u32[]{:S(2)}) copy-start(bf16[2048,1024]{1,0:T(8,128)(2,1)} %all-gather.2.cloned.1.call-done.refs_4_) | copy-start | bytes 12582916
Sparse Core Ops, SparseCore 0:
  22.9 56.1 all-gather.1

commit v3 on v2

--- a/solution.py
+++ b/solution.py
@@ -139,10 +139,10 @@
 
 def arrange_kernel(place_ref, *refs):
     shards, out_ref = refs[:-1], refs[-1]
-    rows = shards[0].shape[0]
+    rows = shards[0].shape[1]
     for k, shard in enumerate(shards):
         first = lax.rem(place_ref[0] + NX - k, NX) * rows
-        out_ref[pl.ds(pl.multiple_of(first, rows), rows), :] = shard[...]
+        out_ref[:, pl.ds(pl.multiple_of(first, rows), rows), :] = shard[...]
 
 
 def split(place_ref, first, rows_of, refs):
@@ -235,18 +235,27 @@
     out[:, :, half:] = y_total[...].astype(out.dtype)
 
 
-def encoded_kernel(*refs):
-    grads, weights, out_ref = refs[:4], refs[4:-1], refs[-1]
+def encoded_kernel(order_ref, *refs):
+    grads, pieces, out_ref, results, sems = refs[:4], refs[4:-3], *refs[-3:]
     half = grads[0].shape[1]
-    total = None
-    for index, grad in enumerate(grads):
-        part = index % 2
-        term = dot_last(grad[...], weights[index // 2][:, part * half : part * half + half])
-        total = term if total is None else total + term
-    out_ref[...] = total.astype(jnp.bfloat16)
-
-
-def kernel_call(kernel, name, out_shape, mebibytes=24, flops=0, moved=0, **options):
+    core = order_ref[NZ]
+    stores = []
+    for k, piece in enumerate(pieces):
+        total = None
+        for index, grad in enumerate(grads):
+            side, part = lax.rem(core + index // 2, NC), index % 2
+            term = dot_last(grad[...], piece[side, :, part * half : part * half + half])
+            total = term if total is None else total + term
+        results[k] = total.astype(jnp.bfloat16)
+        columns = pl.ds(pl.multiple_of(order_ref[k] * 256, 256), 256)
+        store = pltpu.make_async_copy(results.at[k], out_ref.at[:, columns], sems.at[k])
+        store.start()
+        stores.append(store)
+    for store in stores:
+        store.wait()
+
+
+def kernel_call(kernel, name, out_shape, mebibytes=12, flops=0, moved=0, **options):
     return pl.pallas_call(
         kernel,
         out_shape=out_shape,
@@ -285,7 +294,7 @@
     return permutation(lambda z, x, y, c: (z, x ^ bits if axis == "x" else x, y ^ bits if axis == "y" else y, c))
 
 
-def halving(outs, axes, steps):
+def halving(outs, axes, steps, beside=()):
     kept, sent = outs[0::2], outs[1::2]
     ways = [(axis, *bits) for axis in axes for bits in ((1, 3), (3, 1))]
     first = [send(value, flipped(axis, near)) for value, (axis, near, _) in zip(sent, ways)]
@@ -304,7 +313,7 @@
         out_specs=[pl.BlockSpec((shape[1] // steps, *shape[2:]), lambda i: (i, 0, 0)) for shape in shapes],
     )(*kept, *first)
     last = [send(value, flipped(axis, far)) for value, (axis, _, far) in zip(middle, ways)]
-    last = lax.optimization_barrier(last)
+    last, beside = lax.optimization_barrier((last, beside))
     operands, specs = [], []
     for start in (0, 2):
         for values in (kept, first, last):
@@ -314,7 +323,7 @@
                 shape = (1,) * (value.ndim - 3) + (inner[0] // steps, *inner[1:])
                 leading = (0,) * (value.ndim - 3)
                 specs.append(pl.BlockSpec(shape, lambda i, leading=leading: (*leading, i, 0, 0)))
-    return operands, specs
+    return operands, specs, middle[0], beside
 
 
 def on_device(queries, key_rows, value_rows, encoded, key_weight, value_weight, grad_out, lengths):
@@ -329,10 +338,9 @@
     queries, grad_out = queries[0], grad_out[0]
     key_rows, value_rows, encoded = key_rows[0], value_rows[0], encoded[0]
     f32, bf16 = jnp.float32, jnp.bfloat16
-    encoded_other = swap_cores(encoded)
     smem = pl.BlockSpec(memory_space=pltpu.SMEM)
 
-    shard = jnp.where(core == 0, key_weight, value_weight)
+    shard = jnp.stack([key_weight, value_weight])
     shards = [shard] + [send(shard, along("x", k)) for k in range(1, NX)]
 
     stats_shape = like((3 * pairs, 2 * answer), f32)
@@ -348,21 +356,10 @@
         out_specs=pl.BlockSpec(stats_shape.shape, lambda p: (0, 0)),
     )(lengths, queries, key_rows, value_rows, grad_out)
 
-    whole_vmem = pl.BlockSpec(memory_space=pltpu.VMEM)
-    shards = lax.optimization_barrier((*shards, stats))[:-1]
-    ordered = kernel_call(
-        arrange_kernel,
-        "arrange",
-        like((NX * shard.shape[0], features), bf16),
-        in_specs=[smem] + [whole_vmem] * NX,
-        out_specs=whole_vmem,
-    )(place, *shards)
-    gathered = lax.all_gather(
-        ordered, AXES, axis=0, tiled=True, axis_index_groups=groups(lambda z, x, y, c: (x, y, c))
-    )
-
-    chip_stats = kernel_call(merge_kernel, "merge", stats_shape)(tie(stats, ordered), swap_cores(stats))
-    all_stats = [chip_stats] + [send(chip_stats, along("y", k)) for k in range(1, NY)]
+    chip_stats = kernel_call(merge_kernel, "merge", stats_shape)(stats, swap_cores(stats))
+    all_stats = [chip_stats] + [send(chip_stats, along("y", k)) for k in (1, 3)]
+    *shards, encoded_other, late = lax.optimization_barrier((*shards, swap_cores(encoded), chip_stats))
+    all_stats.append(send(late, along("y", 2)))
 
     def grads(first_pair):
         def rows(p):
@@ -378,7 +375,7 @@
             "grads",
             [
                 like((keys, half), bf16),
-                like((keys, half), bf16),
+                pltpu.HBM((keys, half), bf16),
                 like((NY // 2, PAIR, answer), f32),
                 like((NY // 2, PAIR, answer), bf16),
             ],
@@ -389,6 +386,20 @@
 
     mine_a, sent_a, query_kept_a, query_sent_a = grads(0)
     received_a = swap_cores(sent_a)
+
+    whole_vmem = pl.BlockSpec(memory_space=pltpu.VMEM)
+    shards = lax.optimization_barrier((*shards, mine_a))[:-1]
+    ordered = kernel_call(
+        arrange_kernel,
+        "arrange",
+        like((2, NX * shard.shape[1], features), bf16),
+        in_specs=[smem] + [whole_vmem] * NX,
+        out_specs=whole_vmem,
+    )(place, *shards)
+
+    around = permutation(lambda z, x, y, c: (z + 1 - 2 * c, x, y, c))
+    pieces = [ordered, send(ordered, around)]
+
     mine_b, sent_b, query_kept_b, query_sent_b = grads(pairs // 2)
     received_b = swap_cores(sent_b)
     query_received = [swap_cores(query_sent_a), swap_cores(query_sent_b)]
@@ -416,6 +427,7 @@
         weights_kernel,
         "weights",
         x_outs + y_outs,
+        20,
         grid=(4,),
         in_specs=[smem, encoded_spec, encoded_spec] + [whole] * 4 + [query_spec] * 4,
         out_specs=x_specs + y_specs,
@@ -434,7 +446,10 @@
         *query_received,
     )
 
-    operands, specs = halving(terms, "xy", 4)
+    pieces.append(send(tie(pieces[1], terms[0]), around))
+
+    operands, specs, middle, _ = halving(terms, "xy", 4)
+    pieces.append(send(tie(pieces[2], middle), around))
     chunk, query_shape = (2, NZ, 16, half // 2), (4, query_rows, half)
     chunk_outs, chunk_specs = split_outs(chunk)
     *second, query_grad = kernel_call(
@@ -449,7 +464,8 @@
     query_grad = query_grad.reshape(4, query_rows, 2, answer).transpose(2, 0, 1, 3)
     query_grad = query_grad.reshape(PAIR, answer).T.astype(bf16)[None]
 
-    operands, specs = halving(second, "yx", 1)
+    across = send(tie(pieces[3], second[0]), around)
+    operands, specs, _, across = halving(second, "yx", 1, across)
     last = kernel_call(
         last_kernel,
         "last",
@@ -459,8 +475,7 @@
         out_specs=pl.BlockSpec((NZ, 16, features), lambda i: (0, 0, 0)),
         scratch_shapes=[pltpu.VMEM((NZ, 16, half), f32)] * 2,
     )(*operands)
-    gathered = tie(gathered, last)
-    gathered_other = swap_cores(gathered)
+    swapped = [swap_cores(tie(piece, last)) for piece in pieces[1:4]]
     last = lax.all_to_all(
         last.reshape(NZ * NC, 8, features),
         AXES,
@@ -470,17 +485,23 @@
         axis_index_groups=groups(lambda z, x, y, c: (x, y)),
     )
 
-    weight_spec = pl.BlockSpec((width // 4, features), lambda i: (i, 0))
+    z_place, way = dp // NX, 1 - 2 * core
+    order = [(z_place + way * step + NZ) % NZ for step in (0, -1, -2, -3, 1, 2, 3, 4)]
+    in_hbm = pl.BlockSpec(memory_space=pltpu.HBM)
     encoded_grad = kernel_call(
         encoded_kernel,
         "encoded",
-        like((keys, width), bf16),
+        pltpu.HBM((keys, width), bf16),
+        24,
         flops=4 * keys * width * features,
         moved=14 * MIB,
-        grid=(4,),
-        in_specs=[whole] * 4 + [weight_spec] * 2,
-        out_specs=pl.BlockSpec((keys, width // 4), lambda i: (0, i)),
-    )(mine_a, mine_b, sent_a, sent_b, gathered, gathered_other)
+        in_specs=[smem] + [whole_vmem] * (NZ + 4),
+        out_specs=in_hbm,
+        scratch_shapes=[
+            pltpu.VMEM((NZ, keys, width // NZ), bf16),
+            pltpu.SemaphoreType.DMA((NZ,)),
+        ],
+    )(jnp.stack([*order, core]), mine_a, mine_b, sent_a, sent_b, *pieces, *swapped, across)
     summed = tie(last, encoded_grad).reshape(NZ, NC, 8, features).astype(f32).sum(0)
     key_weight_grad, value_weight_grad = summed[0], summed[1]
     return query_grad, encoded_grad[None], key_weight_grad, value_weight_grad

time: 133 us -> 128 us (0.962)
  between operations: 15 us -> 1.51 us
  starting transfers between devices: 41.7 us -> 47.1 us
  Pallas kernels: 31 us -> 33.6 us
    ppermute x22 -> x26, starting transfers between devices: 23.1 us -> 30 us  [send(): return lax.ppermute(value, AXES, links)]
    ppermute x22 -> x26, waiting for transfers between devices: 30.2 us -> 33.1 us  [send(): return lax.ppermute(value, AXES, links)]
    ppermute x7 -> x9, waiting for transfers between devices: 5.25 us -> 2.7 us  [swap_cores(): lax.ppermute(value, AXES, permutation(lambda z, x, y, c: (z, x, y, 1 - c)))]
    all_to_all x1, starting transfers between devices: 8.58 us -> 6.88 us  [on_device(): lax.all_to_all(last.reshape(NZ * NC, 8, features), AXES, 0, 0, tiled=True...]
    all_to_all x1, waiting for transfers between devices: 1.37 us -> 0.01 us  [on_device(): lax.all_to_all(last.reshape(NZ * NC, 8, features), AXES, 0, 0, tiled=True...]
    pallas_call x2, Pallas kernels: 6.85 us -> 8.2 us  [grads(): kernel_call(functools.partial(grads_kernel, first_pair), 'grads', [like((...]
    unnamed x33 -> x35, local copies, waits for them, and re-layouts: 6.46 us -> 7.29 us
    ppermute x7 -> x9, starting transfers between devices: 9.97 us -> 10.2 us  [swap_cores(): lax.ppermute(value, AXES, permutation(lambda z, x, y, c: (z, x, y, 1 - c)))]
  transfers between devices with their start and end apart: 31 -> 36, of which waited for: 16 -> 18; matrix products, arithmetic and copies ran while one was open for 1% -> 2% of each run, Pallas kernels for 23% -> 21%
where the time goes in v3:
time: 128 us; the launch traced here: 127 us
  starting transfers between devices  47.1 us (37%)
  waiting for transfers between devices  35.8 us (28%)
  Pallas kernels  33.6 us (26%)
  local copies, waits for them, and re-layouts  8.09 us (6%)
  between operations  1.51 us (1%)
    ppermute x26, waiting for transfers between devices, send(): return lax.ppermute(value, AXES, links)  33.1 us
    ppermute x26, starting transfers between devices, send(): return lax.ppermute(value, AXES, links)  30 us
    ppermute x9, starting transfers between devices, swap_cores(): lax.ppermute(value, AXES, permutation(lambda z, x, y, c: (z, x, y, 1 - c)))  10.2 us
    pallas_call x2, Pallas kernels, grads(): kernel_call(functools.partial(grads_kernel, first_pair), 'grads', [like((...  8.2 us
    pallas_call x1, Pallas kernels, on_device(): kernel_call(encoded_kernel, 'encoded', pltpu.HBM((keys, width), bf16), 24...  7.98 us
    pallas_call x1, Pallas kernels, on_device(): kernel_call(weights_kernel, 'weights', x_outs + y_outs, 20, grid=(4,), in...  7.35 us
    unnamed x35, local copies, waits for them, and re-layouts  7.29 us
    all_to_all x1, starting transfers between devices, on_device(): lax.all_to_all(last.reshape(NZ * NC, 8, features), AXES, 0, 0, tiled=True...  6.88 us
  transfers between devices with their start and end apart: 36, of which 18 were waited for; matrix products, arithmetic and copies ran while one was open for 2% of the time, Pallas kernels for 21%

profile of v3, /device:TPU:1, one launch (start us, length us, event | category | flops | bytes accessed | tf_op | source)
XLA Modules:
  0.0 127.2 jit_solution(8375168391459210818)
XLA Ops:
  0.7 3.3 %collective-permute-start.3 = (bf16[512,2048]{1,0:T(8,128)(2,1)}, bf16[512,2048]{1,0:T(8,128)(2,1)}, u32[]{:S(2)}, u32[]{:S(2)}) collective-permute-start(bf16[512,2048]{1,0:T(8,128)(2,1)} %bitcast.55), channel_id=1, source_target_pairs={{0,1},{1,0},{2,3},{3,2},{4,5},{5,4},{6,7},{7,6},{8,9},{9,8},{10,11... | collective-permute-start | bytes 6291464 | tf_op jit(solution)/shard_map/ppermute | solution.py:46
  4.0 1.0 pad_maximum_fusion.refs_0_
  5.1 1.9 %collective-permute-start.1 = (bf16[2,64,1024]{2,1,0:T(8,128)(2,1)S(1)}, bf16[2,64,1024]{2,1,0:T(8,128)(2,1)}, u32[]{:S(2)}, u32[]{:S(2)}) collective-permute-start(bf16[2,64,1024]{2,1,0:T(8,128)(2,1)S(1)} %pad_maximum_fusion.refs_0_), channel_id=1, source_target_pairs={{0,16},{1,17},{2,18},{3,19},{4,20},{5,21},{6,22},{7,23},{8,24},{9,... | collective-permute-start | bytes 786440 | tf_op jit(solution)/shard_map/ppermute | solution.py:286
  7.0 1.2 collective-permute-start.2
  8.8 6.2 %stats.1.left_ref = f32[24,512]{1,0:T(8,128)} custom-call(s32[1]{0:T(128)S(6)} %copy.18.length_ref, bf16[256,1024]{1,0:T(8,128)(2,1)} %bitcast.49, bf16[512,1024]{1,0:T(8,128)(2,1)} %bitcast.43, bf16[512,1024]{1,0:T(8,128)(2,1)} %bitcast.46, bf16[256,1024]{1,0:T(8,128)(2,1)} %bitcast.52), custom_call_target="tpu_custom_call" | custom-call | tf_op jit(solution)/shard_map/stats/pallas_call | solution.py:349
  15.0 0.9 collective-permute-start.4
  15.9 1.1 collective-permute-done.4.right_ref
  17.0 0.8 copy-done.11
  17.8 1.4 %collective-permute-start.5 = (f32[24,512]{1,0:T(8,128)S(1)}, f32[24,512]{1,0:T(8,128)S(1)}, u32[]{:S(2)}, u32[]{:S(2)}) collective-permute-start(f32[24,512]{1,0:T(8,128)S(1)} %merge.1.refs_0_), channel_id=1, source_target_pairs={{0,2},{1,3},{2,4},{3,5},{4,6},{5,7},{6,0},{7,1},{8,10},{9,11},{10,... | collective-permute-start | bytes 147464 | tf_op jit(solution)/shard_map/ppermute | solution.py:286
  19.2 0.7 collective-permute-done.refs_1_
  19.9 0.9 collective-permute-start.6
  20.7 1.6 %collective-permute-start.7 = (f32[24,512]{1,0:T(8,128)S(1)}, f32[24,512]{1,0:T(8,128)S(1)}, u32[]{:S(2)}, u32[]{:S(2)}) collective-permute-start(f32[24,512]{1,0:T(8,128)S(1)} %merge.1.refs_0_), channel_id=1, source_target_pairs={{0,4},{1,5},{2,6},{3,7},{4,0},{5,1},{6,2},{7,3},{8,12},{9,13},{10,... | collective-permute-start | bytes 147464 | tf_op jit(solution)/shard_map/ppermute | solution.py:286
  22.5 0.6 collective-permute-done.6.refs_2_
  23.1 2.2 %collective-permute-done.7.refs_3_ = f32[24,512]{1,0:T(8,128)S(1)} collective-permute-done((f32[24,512]{1,0:T(8,128)S(1)}, f32[24,512]{1,0:T(8,128)S(1)}, u32[]{:S(2)}, u32[]{:S(2)}) %collective-permute-start.7) | collective-permute-done | bytes 49184 | tf_op jit(solution)/shard_map/ppermute | solution.py:286
  25.3 1.2 copy-done.1
  26.5 1.0 copy-done.4
  27.6 4.1 %grads.2 = (bf16[512,512]{1,0:T(8,128)(2,1)S(1)}, bf16[512,512]{1,0:T(8,128)(2,1)}, f32[2,128,256]{2,1,0:T(8,128)S(1)}, bf16[2,128,256]{2,1,0:T(8,128)(2,1)S(1)}) custom-call(s32[1]{0:T(128)} %bitcast.15.core_ref, s32[1]{0:T(128)S(6)} %copy.18.length_ref, bf16[256,1024]{1,0:T(8,128)(2,1)S(1)} %bitcast.50, bf16[512,1024]{1,0:T(8,128)(2,1)S(1)} %bitcast.44, ...), custom_call_target="tpu_custom_call" | custom-call | tf_op jit(solution)/shard_map/grads/pallas_call | solution.py:373
  31.7 1.4 %arrange.1.refs_4_ = bf16[2,256,1024]{2,1,0:T(8,128)(2,1)S(1)} custom-call(s32[8]{0:T(128)S(1)} %stack.72.place_ref, bf16[2,64,1024]{2,1,0:T(8,128)(2,1)S(1)} %pad_maximum_fusion.refs_0_, bf16[2,64,1024]{2,1,0:T(8,128)(2,1)} %collective-permute-done.refs_1_, bf16[2,64,1024]{2,1,0:T(8,128)(2,1)} %collective-permute-done.1.refs_2_, ...), custom_call_target="tpu_custom_call" | custom-call | tf_op jit(solution)/shard_map/arrange/pallas_call | solution.py:392
  33.1 5.6 %collective-permute-start.20 = (bf16[2,256,1024]{2,1,0:T(8,128)(2,1)S(1)}, bf16[2,256,1024]{2,1,0:T(8,128)(2,1)}, u32[]{:S(2)}, u32[]{:S(2)}) collective-permute-start(bf16[2,256,1024]{2,1,0:T(8,128)(2,1)S(1)} %arrange.1.refs_4_), channel_id=1, source_target_pairs={{0,32},{1,225},{2,34},{3,227},{4,36},{5,229},{6,38},{7,231},{8,40}... | collective-permute-start | bytes 3145736 | tf_op jit(solution)/shard_map/ppermute | solution.py:286
  38.7 4.1 %grads.3 = (bf16[512,512]{1,0:T(8,128)(2,1)S(1)}, bf16[512,512]{1,0:T(8,128)(2,1)}, f32[2,128,256]{2,1,0:T(8,128)S(1)}, bf16[2,128,256]{2,1,0:T(8,128)(2,1)S(1)}) custom-call(s32[1]{0:T(128)} %bitcast.15.core_ref, s32[1]{0:T(128)S(6)} %copy.18.length_ref, bf16[256,1024]{1,0:T(8,128)(2,1)S(1)} %bitcast.51, bf16[512,1024]{1,0:T(8,128)(2,1)S(1)} %bitcast.45, ...), custom_call_target="tpu_custom_call" | custom-call | tf_op jit(solution)/shard_map/grads/pallas_call | solution.py:373
  42.9 0.5 collective-permute-start.9
  43.4 0.5 collective-permute-start.11
  43.8 1.1 collective-permute-done.10.refs_6_
  45.0 0.3 collective-permute-done.11.refs_7_
  45.2 0.2 collective-permute-done.9.refs_3_
  45.4 7.3 %weights.1 = (f32[2,8,64,256]{3,2,1,0:T(8,128)S(1)}, bf16[2,8,64,256]{3,2,1,0:T(8,128)(2,1)S(1)}, f32[2,8,64,256]{3,2,1,0:T(8,128)S(1)}, bf16[2,8,64,256]{3,2,1,...) custom-call(s32[8]{0:T(128)S(1)} %stack.72.place_ref, ...), custom_call_target="tpu_custom_call" | custom-call | tf_op jit(solution)/shard_map/weights/pallas_call | solution.py:426
  52.8 1.8 %collective-permute-start.21 = (bf16[2,256,1024]{2,1,0:T(8,128)(2,1)}, bf16[2,256,1024]{2,1,0:T(8,128)(2,1)S(1)}, u32[]{:S(2)}, u32[]{:S(2)}) collective-permute-start(bf16[2,256,1024]{2,1,0:T(8,128)(2,1)} %collective-permute-done.20.refs_5_), channel_id=1, source_target_pairs={{0,32},{1,225},{2,34},{3,227},{4,36},{5,229},{6,38},{7,231},{8,40}... | collective-permute-start | bytes 3145736 | tf_op jit(solution)/shard_map/ppermute | solution.py:286
  54.7 1.9 %collective-permute-start.15 = (bf16[2,4,144,256]{3,2,1,0:T(8,128)(2,1)S(1)}, bf16[2,4,144,256]{3,2,1,0:T(8,128)(2,1)S(1)}, u32[]{:S(2)}, u32[]{:S(2)}) collective-permute-start(bf16[2,4,144,256]{3,2,1,0:T(8,128)(2,1)S(1)} %get-tuple-element.86), channel_id=1, source_target_pairs={{0,6},{1,7},{2,4},{3,5},{4,2},{5,3},{6,0},{7,1},{8,14},{9,15},{10,... | collective-permute-start | bytes 1769480 | tf_op jit(solution)/shard_map/ppermute | solution.py:286
  56.6 0.7 collective-permute-start.12
  57.3 1.6 %collective-permute-start.13 = (bf16[2,8,64,256]{3,2,1,0:T(8,128)(2,1)S(1)}, bf16[2,8,64,256]{3,2,1,0:T(8,128)(2,1)S(1)}, u32[]{:S(2)}, u32[]{:S(2)}) collective-permute-start(bf16[2,8,64,256]{3,2,1,0:T(8,128)(2,1)S(1)} %get-tuple-element.84), channel_id=1, source_target_pairs={{0,24},{1,25},{2,26},{3,27},{4,28},{5,29},{6,30},{7,31},{8,16},{9,... | collective-permute-start | bytes 1572872 | tf_op jit(solution)/shard_map/ppermute | solution.py:286
  58.9 11.5 %collective-permute-done.12.refs_4_.refs_2_ = bf16[2,8,64,256]{3,2,1,0:T(8,128)(2,1)S(1)} collective-permute-done((bf16[2,8,64,256]{3,2,1,0:T(8,128)(2,1)S(1)}, bf16[2,8,64,256]{3,2,1,0:T(8,128)(2,1)S(1)}, u32[]{:S(2)}, u32[]{:S(2)}) %collective-permute-start.12) | collective-permute-done | bytes 524320 | tf_op jit(solution)/shard_map/ppermute | solution.py:286
  70.4 1.7 %collective-permute-done.13.refs_5_.refs_3_ = bf16[2,8,64,256]{3,2,1,0:T(8,128)(2,1)S(1)} collective-permute-done((bf16[2,8,64,256]{3,2,1,0:T(8,128)(2,1)S(1)}, bf16[2,8,64,256]{3,2,1,0:T(8,128)(2,1)S(1)}, u32[]{:S(2)}, u32[]{:S(2)}) %collective-permute-start.13) | collective-permute-done | bytes 524320 | tf_op jit(solution)/shard_map/ppermute | solution.py:286
  72.0 0.3 middle.2
  72.3 0.5 collective-permute-start.22
  72.8 1.3 %collective-permute-start.18 = (bf16[4,144,256]{2,1,0:T(8,128)(2,1)S(1)}, bf16[4,144,256]{2,1,0:T(8,128)(2,1)S(1)}, u32[]{:S(2)}, u32[]{:S(2)}) collective-permute-start(bf16[4,144,256]{2,1,0:T(8,128)(2,1)S(1)} %get-tuple-element.95), channel_id=1, source_target_pairs={{0,6},{1,7},{2,4},{3,5},{4,2},{5,3},{6,0},{7,1},{8,14},{9,15},{10,... | collective-permute-start | bytes 884744 | tf_op jit(solution)/shard_map/ppermute | solution.py:286
  74.1 1.6 %collective-permute-start.16 = (bf16[8,64,256]{2,1,0:T(8,128)(2,1)S(1)}, bf16[8,64,256]{2,1,0:T(8,128)(2,1)S(1)}, u32[]{:S(2)}, u32[]{:S(2)}) collective-permute-start(bf16[8,64,256]{2,1,0:T(8,128)(2,1)S(1)} %get-tuple-element.93), channel_id=1, source_target_pairs={{0,24},{1,25},{2,26},{3,27},{4,28},{5,29},{6,30},{7,31},{8,16},{9,... | collective-permute-start | bytes 786440 | tf_op jit(solution)/shard_map/ppermute | solution.py:286
  75.8 7.2 %collective-permute-done.16.refs_4_ = bf16[8,64,256]{2,1,0:T(8,128)(2,1)S(1)} collective-permute-done((bf16[8,64,256]{2,1,0:T(8,128)(2,1)S(1)}, bf16[8,64,256]{2,1,0:T(8,128)(2,1)S(1)}, u32[]{:S(2)}, u32[]{:S(2)}) %collective-permute-start.16) | collective-permute-done | bytes 262176 | tf_op jit(solution)/shard_map/ppermute | solution.py:286
  83.0 0.2 collective-permute-done.17.refs_5_
  83.2 1.2 second.1
  84.5 2.0 %collective-permute-done.22.refs_7_ = bf16[2,256,1024]{2,1,0:T(8,128)(2,1)} collective-permute-done((bf16[2,256,1024]{2,1,0:T(8,128)(2,1)S(1)}, bf16[2,256,1024]{2,1,0:T(8,128)(2,1)}, u32[]{:S(2)}, u32[]{:S(2)}) %collective-permute-start.22) | collective-permute-done | bytes 1048608 | tf_op jit(solution)/shard_map/ppermute | solution.py:286
  86.4 1.3 %collective-permute-start.31 = (bf16[2,256,1024]{2,1,0:T(8,128)(2,1)}, bf16[2,256,1024]{2,1,0:T(8,128)(2,1)S(1)}, u32[]{:S(2)}, u32[]{:S(2)}) collective-permute-start(bf16[2,256,1024]{2,1,0:T(8,128)(2,1)} %collective-permute-done.22.refs_7_), channel_id=1, source_target_pairs={{0,32},{1,225},{2,34},{3,227},{4,36},{5,229},{6,38},{7,231},{8,40}... | collective-permute-start | bytes 3145736 | tf_op jit(solution)/shard_map/ppermute | solution.py:286
  87.8 0.4 collective-permute-start.23
  88.2 0.9 collective-permute-start.24
  89.1 0.7 collective-permute-start.25
  89.8 1.6 %collective-permute-start.26 = (bf16[2,8,16,256]{3,2,1,0:T(8,128)(2,1)S(1)}, bf16[2,8,16,256]{3,2,1,0:T(8,128)(2,1)S(1)}, u32[]{:S(2)}, u32[]{:S(2)}) collective-permute-start(bf16[2,8,16,256]{3,2,1,0:T(8,128)(2,1)S(1)} %get-tuple-element.117), channel_id=1, source_target_pairs={{0,24},{1,25},{2,26},{3,27},{4,28},{5,29},{6,30},{7,31},{8,16},{9,... | collective-permute-start | bytes 393224 | tf_op jit(solution)/shard_map/ppermute | solution.py:286
  91.4 0.2 collective-permute-done.23.refs_4_.refs_2_
  91.6 1.6 %collective-permute-done.24.refs_5_.refs_3_ = bf16[2,8,16,256]{3,2,1,0:T(8,128)(2,1)S(1)} collective-permute-done((bf16[2,8,16,256]{3,2,1,0:T(8,128)(2,1)S(1)}, bf16[2,8,16,256]{3,2,1,0:T(8,128)(2,1)S(1)}, u32[]{:S(2)}, u32[]{:S(2)}) %collective-permute-start.24) | collective-permute-done | bytes 131104 | tf_op jit(solution)/shard_map/ppermute | solution.py:286
  93.2 1.9 %collective-permute-done.26.refs_7_.refs_9_ = bf16[2,8,16,256]{3,2,1,0:T(8,128)(2,1)S(1)} collective-permute-done((bf16[2,8,16,256]{3,2,1,0:T(8,128)(2,1)S(1)}, bf16[2,8,16,256]{3,2,1,0:T(8,128)(2,1)S(1)}, u32[]{:S(2)}, u32[]{:S(2)}) %collective-permute-start.26) | collective-permute-done | bytes 131104 | tf_op jit(solution)/shard_map/ppermute | solution.py:286
  95.2 1.2 collective-permute-start.27
  96.3 1.6 %collective-permute-start.29 = (bf16[8,16,256]{2,1,0:T(8,128)(2,1)S(1)}, bf16[8,16,256]{2,1,0:T(8,128)(2,1)S(1)}, u32[]{:S(2)}, u32[]{:S(2)}) collective-permute-start(bf16[8,16,256]{2,1,0:T(8,128)(2,1)S(1)} %get-tuple-element.126), channel_id=1, source_target_pairs={{0,24},{1,25},{2,26},{3,27},{4,28},{5,29},{6,30},{7,31},{8,16},{9,... | collective-permute-start | bytes 196616 | tf_op jit(solution)/shard_map/ppermute | solution.py:286
  97.9 1.9 %collective-permute-done.27.refs_4_ = bf16[8,16,256]{2,1,0:T(8,128)(2,1)S(1)} collective-permute-done((bf16[8,16,256]{2,1,0:T(8,128)(2,1)S(1)}, bf16[8,16,256]{2,1,0:T(8,128)(2,1)S(1)}, u32[]{:S(2)}, u32[]{:S(2)}) %collective-permute-start.27) | collective-permute-done | bytes 65568 | tf_op jit(solution)/shard_map/ppermute | solution.py:286
  99.9 1.1 collective-permute-done.29.refs_10_
  101.0 0.4 collective-permute-done.30.refs_11_
  101.4 0.9 last.1
  102.3 0.1 copy-done.12
  102.4 4.5 %collective-permute-start.32 = (bf16[2,256,1024]{2,1,0:T(8,128)(2,1)}, bf16[2,256,1024]{2,1,0:T(8,128)(2,1)}, u32[]{:S(2)}, u32[]{:S(2)}) collective-permute-start(bf16[2,256,1024]{2,1,0:T(8,128)(2,1)} %collective-permute-done.20.refs_5_), channel_id=1, source_target_pairs={{0,1},{1,0},{2,3},{3,2},{4,5},{5,4},{6,7},{7,6},{8,9},{9,8},{10,11... | collective-permute-start | bytes 3145736 | tf_op jit(solution)/shard_map/ppermute | solution.py:46
  106.9 0.5 collective-permute-start.34
  107.4 6.9 %all-to-all-start = ((bf16[16,8,1024]{2,1,0:T(8,128)(2,1)}), bf16[16,8,1024]{2,1,0:T(8,128)(2,1)S(1)}, u32[]{:S(2)}, u32[]{:S(2)}) async-start(bf16[16,8,1024]{2,1,0:T(8,128)(2,1)} %bitcast.29), calls=%async_computation | async-start | bytes 524288 | tf_op jit(solution)/shard_map/all_to_all | solution.py:479
  114.4 0.7 copy.14
  115.2 1.2 copy-done.13
  116.4 1.0 copy-done.15
  117.5 1.0 copy-done.16
  118.5 8.0 %encoded.1 = bf16[512,2048]{1,0:T(8,128)(2,1)} custom-call(s32[9]{0:T(128)S(1)} %stack.84.order_ref, bf16[512,512]{1,0:T(8,128)(2,1)S(1)} %copy-done.8, bf16[512,512]{1,0:T(8,128)(2,1)S(1)} %copy-done.10, bf16[512,512]{1,0:T(8,128)(2,1)S(1)} %copy-done.15, bf16[512,512]{1,0:T(8,128)(2,1)S(1)} %copy-done.16, bf16[2,256,1024]{2,1,0:T(8,128)(2,1)S(1)} %arrange.1.refs_4_, ...), custom_call_target="tpu_custom_call" | custom-call | flops 4294967296 | bytes 14680064 | tf_op jit(solution)/shard_map/encoded/pallas_call | solution.py:491
  126.5 0.6 slice_bitcast_fusion
  (61 shorter events, 0.7 us)
Async XLA Ops:
  0.6 24.7 %copy-start.3 = (bf16[1,256,1024]{2,1,0:T(8,128)(2,1)S(1)}, bf16[1,256,1024]{2,1,0:T(8,128)(2,1)}, u32[]{:S(2)}) copy-start(bf16[1,256,1024]{2,1,0:T(8,128)(2,1)} %param.8) | copy-start | bytes 1572868
  0.6 24.6 %copy-start = (bf16[1,512,1024]{2,1,0:T(8,128)(2,1)S(1)}, bf16[1,512,1024]{2,1,0:T(8,128)(2,1)}, u32[]{:S(2)}) copy-start(bf16[1,512,1024]{2,1,0:T(8,128)(2,1)} %param.9) | copy-start | bytes 3145732
  0.7 20.1 %collective-permute-start.3 = (bf16[512,2048]{1,0:T(8,128)(2,1)}, bf16[512,2048]{1,0:T(8,128)(2,1)}, u32[]{:S(2)}, u32[]{:S(2)}) collective-permute-start(bf16[512,2048]{1,0:T(8,128)(2,1)} %bitcast.55), channel_id=1, source_target_pairs={{0,1},{1,0},{2,3},{3,2},{4,5},{5,4},{6,7},{7,6},{8,9},{9,8},{10,11... | collective-permute-start | bytes 6291464 | tf_op jit(solution)/shard_map/ppermute | solution.py:46
  5.0 14.9 %collective-permute-start = (bf16[2,64,1024]{2,1,0:T(8,128)(2,1)S(1)}, bf16[2,64,1024]{2,1,0:T(8,128)(2,1)}, u32[]{:S(2)}, u32[]{:S(2)}) collective-permute-start(bf16[2,64,1024]{2,1,0:T(8,128)(2,1)S(1)} %pad_maximum_fusion.refs_0_), channel_id=1, source_target_pairs={{0,8},{1,9},{2,10},{3,11},{4,12},{5,13},{6,14},{7,15},{8,16},{9,17... | collective-permute-start | bytes 786440 | tf_op jit(solution)/shard_map/ppermute | solution.py:286
  5.1 15.7 %collective-permute-start.1 = (bf16[2,64,1024]{2,1,0:T(8,128)(2,1)S(1)}, bf16[2,64,1024]{2,1,0:T(8,128)(2,1)}, u32[]{:S(2)}, u32[]{:S(2)}) collective-permute-start(bf16[2,64,1024]{2,1,0:T(8,128)(2,1)S(1)} %pad_maximum_fusion.refs_0_), channel_id=1, source_target_pairs={{0,16},{1,17},{2,18},{3,19},{4,20},{5,21},{6,22},{7,23},{8,24},{9,... | collective-permute-start | bytes 786440 | tf_op jit(solution)/shard_map/ppermute | solution.py:286
  7.0 13.7 %collective-permute-start.2 = (bf16[2,64,1024]{2,1,0:T(8,128)(2,1)S(1)}, bf16[2,64,1024]{2,1,0:T(8,128)(2,1)}, u32[]{:S(2)}, u32[]{:S(2)}) collective-permute-start(bf16[2,64,1024]{2,1,0:T(8,128)(2,1)S(1)} %pad_maximum_fusion.refs_0_), channel_id=1, source_target_pairs={{0,24},{1,25},{2,26},{3,27},{4,28},{5,29},{6,30},{7,31},{8,0},{9,1... | collective-permute-start | bytes 786440 | tf_op jit(solution)/shard_map/ppermute | solution.py:286
  15.0 2.0 %collective-permute-start.4 = (f32[24,512]{1,0:T(8,128)}, f32[24,512]{1,0:T(8,128)S(1)}, u32[]{:S(2)}, u32[]{:S(2)}) collective-permute-start(f32[24,512]{1,0:T(8,128)} %stats.1.left_ref), channel_id=1, source_target_pairs={{0,1},{1,0},{2,3},{3,2},{4,5},{5,4},{6,7},{7,6},{8,9},{9,8},{10,11... | collective-permute-start | bytes 147464 | tf_op jit(solution)/shard_map/ppermute | solution.py:46
  17.0 0.8 copy-start.11
  17.8 4.7 %collective-permute-start.5 = (f32[24,512]{1,0:T(8,128)S(1)}, f32[24,512]{1,0:T(8,128)S(1)}, u32[]{:S(2)}, u32[]{:S(2)}) collective-permute-start(f32[24,512]{1,0:T(8,128)S(1)} %merge.1.refs_0_), channel_id=1, source_target_pairs={{0,2},{1,3},{2,4},{3,5},{4,6},{5,7},{6,0},{7,1},{8,10},{9,11},{10,... | collective-permute-start | bytes 147464 | tf_op jit(solution)/shard_map/ppermute | solution.py:286
  19.9 3.2 %collective-permute-start.6 = (f32[24,512]{1,0:T(8,128)S(1)}, f32[24,512]{1,0:T(8,128)S(1)}, u32[]{:S(2)}, u32[]{:S(2)}) collective-permute-start(f32[24,512]{1,0:T(8,128)S(1)} %merge.1.refs_0_), channel_id=1, source_target_pairs={{0,6},{1,7},{2,0},{3,1},{4,2},{5,3},{6,4},{7,5},{8,14},{9,15},{10,... | collective-permute-start | bytes 147464 | tf_op jit(solution)/shard_map/ppermute | solution.py:286
  20.7 4.5 %collective-permute-start.7 = (f32[24,512]{1,0:T(8,128)S(1)}, f32[24,512]{1,0:T(8,128)S(1)}, u32[]{:S(2)}, u32[]{:S(2)}) collective-permute-start(f32[24,512]{1,0:T(8,128)S(1)} %merge.1.refs_0_), channel_id=1, source_target_pairs={{0,4},{1,5},{2,6},{3,7},{4,0},{5,1},{6,2},{7,3},{8,12},{9,13},{10,... | collective-permute-start | bytes 147464 | tf_op jit(solution)/shard_map/ppermute | solution.py:286
  25.3 1.2 copy-start.1
  26.5 1.0 copy-start.4
  27.6 11.2 %copy-start.2 = (bf16[1,512,1024]{2,1,0:T(8,128)(2,1)S(1)}, bf16[1,512,1024]{2,1,0:T(8,128)(2,1)}, u32[]{:S(2)}) copy-start(bf16[1,512,1024]{2,1,0:T(8,128)(2,1)} %param.10) | copy-start | bytes 3145732
  27.6 11.2 %copy-start.5 = (bf16[1,256,1024]{2,1,0:T(8,128)(2,1)S(1)}, bf16[1,256,1024]{2,1,0:T(8,128)(2,1)}, u32[]{:S(2)}) copy-start(bf16[1,256,1024]{2,1,0:T(8,128)(2,1)} %param.14) | copy-start | bytes 1572868
  31.7 13.8 %copy-start.7 = (bf16[512,512]{1,0:T(8,128)(2,1)}, bf16[512,512]{1,0:T(8,128)(2,1)S(1)}, u32[]{:S(2)}) copy-start(bf16[512,512]{1,0:T(8,128)(2,1)S(1)} %get-tuple-element.73.refs_0_) | copy-start | bytes 1572868
  31.7 7.1 %copy-start.14 = (bf16[512,512]{1,0:T(8,128)(2,1)S(1)}, bf16[512,512]{1,0:T(8,128)(2,1)}, u32[]{:S(2)}) copy-start(bf16[512,512]{1,0:T(8,128)(2,1)} %get-tuple-element.75.refs_2_) | copy-start | bytes 1572868
  33.1 12.4 %copy-start.6 = (bf16[1,512,2048]{2,1,0:T(8,128)(2,1)S(1)}, bf16[1,512,2048]{2,1,0:T(8,128)(2,1)}, u32[]{:S(2)}) copy-start(bf16[1,512,2048]{2,1,0:T(8,128)(2,1)} %param.11) | copy-start | bytes 6291460
  33.1 19.7 %collective-permute-start.20 = (bf16[2,256,1024]{2,1,0:T(8,128)(2,1)S(1)}, bf16[2,256,1024]{2,1,0:T(8,128)(2,1)}, u32[]{:S(2)}, u32[]{:S(2)}) collective-permute-start(bf16[2,256,1024]{2,1,0:T(8,128)(2,1)S(1)} %arrange.1.refs_4_), channel_id=1, source_target_pairs={{0,32},{1,225},{2,34},{3,227},{4,36},{5,229},{6,38},{7,231},{8,40}... | collective-permute-start | bytes 3145736 | tf_op jit(solution)/shard_map/ppermute | solution.py:286
  38.7 6.5 %collective-permute-start.8 = (bf16[512,512]{1,0:T(8,128)(2,1)S(1)}, bf16[512,512]{1,0:T(8,128)(2,1)S(1)}, u32[]{:S(2)}, u32[]{:S(2)}) collective-permute-start(bf16[512,512]{1,0:T(8,128)(2,1)S(1)} %copy-done.14), channel_id=1, source_target_pairs={{0,1},{1,0},{2,3},{3,2},{4,5},{5,4},{6,7},{7,6},{8,9},{9,8},{10,11... | collective-permute-start | bytes 1572872 | tf_op jit(solution)/shard_map/ppermute | solution.py:46
  42.9 10.0 %copy-start.9 = (bf16[512,512]{1,0:T(8,128)(2,1)}, bf16[512,512]{1,0:T(8,128)(2,1)S(1)}, u32[]{:S(2)}) copy-start(bf16[512,512]{1,0:T(8,128)(2,1)S(1)} %get-tuple-element.74.refs_1_) | copy-start | bytes 1572868
  42.9 2.6 %collective-permute-start.9 = (bf16[512,512]{1,0:T(8,128)(2,1)}, bf16[512,512]{1,0:T(8,128)(2,1)S(1)}, u32[]{:S(2)}, u32[]{:S(2)}) collective-permute-start(bf16[512,512]{1,0:T(8,128)(2,1)} %get-tuple-element.76.refs_3_), channel_id=1, source_target_pairs={{0,1},{1,0},{2,3},{3,2},{4,5},{5,4},{6,7},{7,6},{8,9},{9,8},{10,11... | collective-permute-start | bytes 1572872 | tf_op jit(solution)/shard_map/ppermute | solution.py:46
  43.3 1.6 %collective-permute-start.10 = (bf16[2,128,256]{2,1,0:T(8,128)(2,1)S(1)}, bf16[2,128,256]{2,1,0:T(8,128)(2,1)S(1)}, u32[]{:S(2)}, u32[]{:S(2)}) collective-permute-start(bf16[2,128,256]{2,1,0:T(8,128)(2,1)S(1)} %get-tuple-element.79), channel_id=1, source_target_pairs={{0,1},{1,0},{2,3},{3,2},{4,5},{5,4},{6,7},{7,6},{8,9},{9,8},{10,11... | collective-permute-start | bytes 393224 | tf_op jit(solution)/shard_map/ppermute | solution.py:46
  43.4 1.9 %collective-permute-start.11 = (bf16[2,128,256]{2,1,0:T(8,128)(2,1)S(1)}, bf16[2,128,256]{2,1,0:T(8,128)(2,1)S(1)}, u32[]{:S(2)}, u32[]{:S(2)}) collective-permute-start(bf16[2,128,256]{2,1,0:T(8,128)(2,1)S(1)} %get-tuple-element.80), channel_id=1, source_target_pairs={{0,1},{1,0},{2,3},{3,2},{4,5},{5,4},{6,7},{7,6},{8,9},{9,8},{10,11... | collective-permute-start | bytes 393224 | tf_op jit(solution)/shard_map/ppermute | solution.py:46
  52.8 19.5 %collective-permute-start.21 = (bf16[2,256,1024]{2,1,0:T(8,128)(2,1)}, bf16[2,256,1024]{2,1,0:T(8,128)(2,1)S(1)}, u32[]{:S(2)}, u32[]{:S(2)}) collective-permute-start(bf16[2,256,1024]{2,1,0:T(8,128)(2,1)} %collective-permute-done.20.refs_5_), channel_id=1, source_target_pairs={{0,32},{1,225},{2,34},{3,227},{4,36},{5,229},{6,38},{7,231},{8,40}... | collective-permute-start | bytes 3145736 | tf_op jit(solution)/shard_map/ppermute | solution.py:286
  54.6 17.4 %collective-permute-start.14 = (bf16[2,4,144,256]{3,2,1,0:T(8,128)(2,1)S(1)}, bf16[2,4,144,256]{3,2,1,0:T(8,128)(2,1)S(1)}, u32[]{:S(2)}, u32[]{:S(2)}) collective-permute-start(bf16[2,4,144,256]{3,2,1,0:T(8,128)(2,1)S(1)} %get-tuple-element.85), channel_id=1, source_target_pairs={{0,2},{1,3},{2,0},{3,1},{4,6},{5,7},{6,4},{7,5},{8,10},{9,11},{10,... | collective-permute-start | bytes 1769480 | tf_op jit(solution)/shard_map/ppermute | solution.py:286
  54.7 17.3 %collective-permute-start.15 = (bf16[2,4,144,256]{3,2,1,0:T(8,128)(2,1)S(1)}, bf16[2,4,144,256]{3,2,1,0:T(8,128)(2,1)S(1)}, u32[]{:S(2)}, u32[]{:S(2)}) collective-permute-start(bf16[2,4,144,256]{3,2,1,0:T(8,128)(2,1)S(1)} %get-tuple-element.86), channel_id=1, source_target_pairs={{0,6},{1,7},{2,4},{3,5},{4,2},{5,3},{6,0},{7,1},{8,14},{9,15},{10,... | collective-permute-start | bytes 1769480 | tf_op jit(solution)/shard_map/ppermute | solution.py:286
  56.6 13.7 %collective-permute-start.12 = (bf16[2,8,64,256]{3,2,1,0:T(8,128)(2,1)S(1)}, bf16[2,8,64,256]{3,2,1,0:T(8,128)(2,1)S(1)}, u32[]{:S(2)}, u32[]{:S(2)}) collective-permute-start(bf16[2,8,64,256]{3,2,1,0:T(8,128)(2,1)S(1)} %get-tuple-element.83), channel_id=1, source_target_pairs={{0,8},{1,9},{2,10},{3,11},{4,12},{5,13},{6,14},{7,15},{8,0},{9,1},... | collective-permute-start | bytes 1572872 | tf_op jit(solution)/shard_map/ppermute | solution.py:286
  57.3 14.8 %collective-permute-start.13 = (bf16[2,8,64,256]{3,2,1,0:T(8,128)(2,1)S(1)}, bf16[2,8,64,256]{3,2,1,0:T(8,128)(2,1)S(1)}, u32[]{:S(2)}, u32[]{:S(2)}) collective-permute-start(bf16[2,8,64,256]{3,2,1,0:T(8,128)(2,1)S(1)} %get-tuple-element.84), channel_id=1, source_target_pairs={{0,24},{1,25},{2,26},{3,27},{4,28},{5,29},{6,30},{7,31},{8,16},{9,... | collective-permute-start | bytes 1572872 | tf_op jit(solution)/shard_map/ppermute | solution.py:286
  72.3 14.1 %collective-permute-start.22 = (bf16[2,256,1024]{2,1,0:T(8,128)(2,1)S(1)}, bf16[2,256,1024]{2,1,0:T(8,128)(2,1)}, u32[]{:S(2)}, u32[]{:S(2)}) collective-permute-start(bf16[2,256,1024]{2,1,0:T(8,128)(2,1)S(1)} %collective-permute-done.21.refs_6_), channel_id=1, source_target_pairs={{0,32},{1,225},{2,34},{3,227},{4,36},{5,229},{6,38},{7,231},{8,40}... | collective-permute-start | bytes 3145736 | tf_op jit(solution)/shard_map/ppermute | solution.py:286
  72.8 10.4 %collective-permute-start.18 = (bf16[4,144,256]{2,1,0:T(8,128)(2,1)S(1)}, bf16[4,144,256]{2,1,0:T(8,128)(2,1)S(1)}, u32[]{:S(2)}, u32[]{:S(2)}) collective-permute-start(bf16[4,144,256]{2,1,0:T(8,128)(2,1)S(1)} %get-tuple-element.95), channel_id=1, source_target_pairs={{0,6},{1,7},{2,4},{3,5},{4,2},{5,3},{6,0},{7,1},{8,14},{9,15},{10,... | collective-permute-start | bytes 884744 | tf_op jit(solution)/shard_map/ppermute | solution.py:286
  74.1 9.1 %collective-permute-start.19 = (bf16[4,144,256]{2,1,0:T(8,128)(2,1)S(1)}, bf16[4,144,256]{2,1,0:T(8,128)(2,1)S(1)}, u32[]{:S(2)}, u32[]{:S(2)}) collective-permute-start(bf16[4,144,256]{2,1,0:T(8,128)(2,1)S(1)} %get-tuple-element.96), channel_id=1, source_target_pairs={{0,2},{1,3},{2,0},{3,1},{4,6},{5,7},{6,4},{7,5},{8,10},{9,11},{10,... | collective-permute-start | bytes 884744 | tf_op jit(solution)/shard_map/ppermute | solution.py:286
  74.1 8.9 %collective-permute-start.16 = (bf16[8,64,256]{2,1,0:T(8,128)(2,1)S(1)}, bf16[8,64,256]{2,1,0:T(8,128)(2,1)S(1)}, u32[]{:S(2)}, u32[]{:S(2)}) collective-permute-start(bf16[8,64,256]{2,1,0:T(8,128)(2,1)S(1)} %get-tuple-element.93), channel_id=1, source_target_pairs={{0,24},{1,25},{2,26},{3,27},{4,28},{5,29},{6,30},{7,31},{8,16},{9,... | collective-permute-start | bytes 786440 | tf_op jit(solution)/shard_map/ppermute | solution.py:286
  75.8 7.5 %collective-permute-start.17 = (bf16[8,64,256]{2,1,0:T(8,128)(2,1)S(1)}, bf16[8,64,256]{2,1,0:T(8,128)(2,1)S(1)}, u32[]{:S(2)}, u32[]{:S(2)}) collective-permute-start(bf16[8,64,256]{2,1,0:T(8,128)(2,1)S(1)} %get-tuple-element.94), channel_id=1, source_target_pairs={{0,8},{1,9},{2,10},{3,11},{4,12},{5,13},{6,14},{7,15},{8,0},{9,1},... | collective-permute-start | bytes 786440 | tf_op jit(solution)/shard_map/ppermute | solution.py:286
  86.4 14.9 %collective-permute-start.31 = (bf16[2,256,1024]{2,1,0:T(8,128)(2,1)}, bf16[2,256,1024]{2,1,0:T(8,128)(2,1)S(1)}, u32[]{:S(2)}, u32[]{:S(2)}) collective-permute-start(bf16[2,256,1024]{2,1,0:T(8,128)(2,1)} %collective-permute-done.22.refs_7_), channel_id=1, source_target_pairs={{0,32},{1,225},{2,34},{3,227},{4,36},{5,229},{6,38},{7,231},{8,40}... | collective-permute-start | bytes 3145736 | tf_op jit(solution)/shard_map/ppermute | solution.py:286
  87.8 3.8 %collective-permute-start.23 = (bf16[2,8,16,256]{3,2,1,0:T(8,128)(2,1)S(1)}, bf16[2,8,16,256]{3,2,1,0:T(8,128)(2,1)S(1)}, u32[]{:S(2)}, u32[]{:S(2)}) collective-permute-start(bf16[2,8,16,256]{3,2,1,0:T(8,128)(2,1)S(1)} %get-tuple-element.114), channel_id=1, source_target_pairs={{0,2},{1,3},{2,0},{3,1},{4,6},{5,7},{6,4},{7,5},{8,10},{9,11},{10,... | collective-permute-start | bytes 393224 | tf_op jit(solution)/shard_map/ppermute | solution.py:286
  88.2 5.0 %collective-permute-start.24 = (bf16[2,8,16,256]{3,2,1,0:T(8,128)(2,1)S(1)}, bf16[2,8,16,256]{3,2,1,0:T(8,128)(2,1)S(1)}, u32[]{:S(2)}, u32[]{:S(2)}) collective-permute-start(bf16[2,8,16,256]{3,2,1,0:T(8,128)(2,1)S(1)} %get-tuple-element.115), channel_id=1, source_target_pairs={{0,6},{1,7},{2,4},{3,5},{4,2},{5,3},{6,0},{7,1},{8,14},{9,15},{10,... | collective-permute-start | bytes 393224 | tf_op jit(solution)/shard_map/ppermute | solution.py:286
  89.1 4.1 %collective-permute-start.25 = (bf16[2,8,16,256]{3,2,1,0:T(8,128)(2,1)S(1)}, bf16[2,8,16,256]{3,2,1,0:T(8,128)(2,1)S(1)}, u32[]{:S(2)}, u32[]{:S(2)}) collective-permute-start(bf16[2,8,16,256]{3,2,1,0:T(8,128)(2,1)S(1)} %get-tuple-element.116), channel_id=1, source_target_pairs={{0,8},{1,9},{2,10},{3,11},{4,12},{5,13},{6,14},{7,15},{8,0},{9,1},... | collective-permute-start | bytes 393224 | tf_op jit(solution)/shard_map/ppermute | solution.py:286
  89.8 5.3 %collective-permute-start.26 = (bf16[2,8,16,256]{3,2,1,0:T(8,128)(2,1)S(1)}, bf16[2,8,16,256]{3,2,1,0:T(8,128)(2,1)S(1)}, u32[]{:S(2)}, u32[]{:S(2)}) collective-permute-start(bf16[2,8,16,256]{3,2,1,0:T(8,128)(2,1)S(1)} %get-tuple-element.117), channel_id=1, source_target_pairs={{0,24},{1,25},{2,26},{3,27},{4,28},{5,29},{6,30},{7,31},{8,16},{9,... | collective-permute-start | bytes 393224 | tf_op jit(solution)/shard_map/ppermute | solution.py:286
  95.1 20.0 %copy-start.8 = (bf16[512,512]{1,0:T(8,128)(2,1)S(1)}, bf16[512,512]{1,0:T(8,128)(2,1)}, u32[]{:S(2)}) copy-start(bf16[512,512]{1,0:T(8,128)(2,1)} %copy-done.7) | copy-start | bytes 1572868
  95.1 20.1 %copy-start.10 = (bf16[512,512]{1,0:T(8,128)(2,1)S(1)}, bf16[512,512]{1,0:T(8,128)(2,1)}, u32[]{:S(2)}) copy-start(bf16[512,512]{1,0:T(8,128)(2,1)} %copy-done.9) | copy-start | bytes 1572868
  95.2 4.7 %collective-permute-start.27 = (bf16[8,16,256]{2,1,0:T(8,128)(2,1)S(1)}, bf16[8,16,256]{2,1,0:T(8,128)(2,1)S(1)}, u32[]{:S(2)}, u32[]{:S(2)}) collective-permute-start(bf16[8,16,256]{2,1,0:T(8,128)(2,1)S(1)} %get-tuple-element.124), channel_id=1, source_target_pairs={{0,6},{1,7},{2,4},{3,5},{4,2},{5,3},{6,0},{7,1},{8,14},{9,15},{10,... | collective-permute-start | bytes 196616 | tf_op jit(solution)/shard_map/ppermute | solution.py:286
  96.3 3.6 %collective-permute-start.28 = (bf16[8,16,256]{2,1,0:T(8,128)(2,1)S(1)}, bf16[8,16,256]{2,1,0:T(8,128)(2,1)S(1)}, u32[]{:S(2)}, u32[]{:S(2)}) collective-permute-start(bf16[8,16,256]{2,1,0:T(8,128)(2,1)S(1)} %get-tuple-element.125), channel_id=1, source_target_pairs={{0,2},{1,3},{2,0},{3,1},{4,6},{5,7},{6,4},{7,5},{8,10},{9,11},{10,... | collective-permute-start | bytes 196616 | tf_op jit(solution)/shard_map/ppermute | solution.py:286
  96.3 4.6 %collective-permute-start.29 = (bf16[8,16,256]{2,1,0:T(8,128)(2,1)S(1)}, bf16[8,16,256]{2,1,0:T(8,128)(2,1)S(1)}, u32[]{:S(2)}, u32[]{:S(2)}) collective-permute-start(bf16[8,16,256]{2,1,0:T(8,128)(2,1)S(1)} %get-tuple-element.126), channel_id=1, source_target_pairs={{0,24},{1,25},{2,26},{3,27},{4,28},{5,29},{6,30},{7,31},{8,16},{9,... | collective-permute-start | bytes 196616 | tf_op jit(solution)/shard_map/ppermute | solution.py:286
  97.9 3.4 %collective-permute-start.30 = (bf16[8,16,256]{2,1,0:T(8,128)(2,1)S(1)}, bf16[8,16,256]{2,1,0:T(8,128)(2,1)S(1)}, u32[]{:S(2)}, u32[]{:S(2)}) collective-permute-start(bf16[8,16,256]{2,1,0:T(8,128)(2,1)S(1)} %get-tuple-element.127), channel_id=1, source_target_pairs={{0,8},{1,9},{2,10},{3,11},{4,12},{5,13},{6,14},{7,15},{8,0},{9,1},... | collective-permute-start | bytes 196616 | tf_op jit(solution)/shard_map/ppermute | solution.py:286
  101.4 1.1 copy-start.12
  102.4 12.7 %collective-permute-start.32 = (bf16[2,256,1024]{2,1,0:T(8,128)(2,1)}, bf16[2,256,1024]{2,1,0:T(8,128)(2,1)}, u32[]{:S(2)}, u32[]{:S(2)}) collective-permute-start(bf16[2,256,1024]{2,1,0:T(8,128)(2,1)} %collective-permute-done.20.refs_5_), channel_id=1, source_target_pairs={{0,1},{1,0},{2,3},{3,2},{4,5},{5,4},{6,7},{7,6},{8,9},{9,8},{10,11... | collective-permute-start | bytes 3145736 | tf_op jit(solution)/shard_map/ppermute | solution.py:46
  106.9 8.3 %collective-permute-start.33 = (bf16[2,256,1024]{2,1,0:T(8,128)(2,1)S(1)}, bf16[2,256,1024]{2,1,0:T(8,128)(2,1)}, u32[]{:S(2)}, u32[]{:S(2)}) collective-permute-start(bf16[2,256,1024]{2,1,0:T(8,128)(2,1)S(1)} %collective-permute-done.21.refs_6_), channel_id=1, source_target_pairs={{0,1},{1,0},{2,3},{3,2},{4,5},{5,4},{6,7},{7,6},{8,9},{9,8},{10,11... | collective-permute-start | bytes 3145736 | tf_op jit(solution)/shard_map/ppermute | solution.py:46
  106.9 8.3 %collective-permute-start.34 = (bf16[2,256,1024]{2,1,0:T(8,128)(2,1)}, bf16[2,256,1024]{2,1,0:T(8,128)(2,1)}, u32[]{:S(2)}, u32[]{:S(2)}) collective-permute-start(bf16[2,256,1024]{2,1,0:T(8,128)(2,1)} %collective-permute-done.22.refs_7_), channel_id=1, source_target_pairs={{0,1},{1,0},{2,3},{3,2},{4,5},{5,4},{6,7},{7,6},{8,9},{9,8},{10,11... | collective-permute-start | bytes 3145736 | tf_op jit(solution)/shard_map/ppermute | solution.py:46
  107.4 19.1 %all-to-all-start = ((bf16[16,8,1024]{2,1,0:T(8,128)(2,1)}), bf16[16,8,1024]{2,1,0:T(8,128)(2,1)S(1)}, u32[]{:S(2)}, u32[]{:S(2)}) async-start(bf16[16,8,1024]{2,1,0:T(8,128)(2,1)} %bitcast.29), calls=%async_computation | async-start | bytes 524288 | tf_op jit(solution)/shard_map/all_to_all | solution.py:479
  115.2 1.2 copy-start.13
  116.4 1.0 copy-start.15
  117.5 1.0 copy-start.16

commit v4 on v3

--- a/solution.py
+++ b/solution.py
@@ -94,8 +94,8 @@
 
 
 def grads_kernel(first_pair, core_ref, length_ref, query_ref, key_ref, value_ref, grad_ref, *refs):
-    stats_refs = refs[:NY]
-    mine_ref, sent_ref, query_kept_ref, query_sent_ref = refs[NY:]
+    stats_refs = refs[:2]
+    joint_ref, mine_ref, sent_ref, query_kept_ref, query_sent_ref = refs[-5:]
     keeps_key = core_ref[0] == 0
     query_grads = []
     for part in range(2):
@@ -118,6 +118,8 @@
         score_grad = (prob * (prob_grad - row_delta)).astype(jnp.bfloat16)
         value_grad = jnp.dot(prob_low, grads, preferred_element_type=jnp.float32)
         key_grad = jnp.dot(score_grad, queries, preferred_element_type=jnp.float32) * SCALE
+        joint_ref[0, :, lanes] = key_grad.astype(jnp.bfloat16)
+        joint_ref[1, :, lanes] = value_grad.astype(jnp.bfloat16)
         mine_ref[:, lanes] = jnp.where(keeps_key, key_grad, value_grad).astype(jnp.bfloat16)
         sent_ref[:, lanes] = jnp.where(keeps_key, value_grad, key_grad).astype(jnp.bfloat16)
         flipped = key.T
@@ -140,22 +142,23 @@
 def arrange_kernel(place_ref, *refs):
     shards, out_ref = refs[:-1], refs[-1]
     rows = shards[0].shape[1]
-    for k, shard in enumerate(shards):
-        first = lax.rem(place_ref[0] + NX - k, NX) * rows
-        out_ref[:, pl.ds(pl.multiple_of(first, rows), rows), :] = shard[...]
+    for flip, shard in zip((0, 1, 3, 2), shards):
+        first = pl.multiple_of(place_ref[flip] * rows, rows)
+        out_ref[:, pl.ds(first, rows), :] = shard[...]
 
 
 def split(place_ref, first, rows_of, refs):
-    kept_left, sent_left, kept_right, sent_right = refs
-    for kept, sent, near, far, side in ((kept_left, sent_left, 1, 3, 0), (kept_right, sent_right, 3, 1, 1)):
+    sides = len(refs) // 2
+    for side, (near, far) in zip(range(sides), ((1, 3), (3, 1))):
+        kept, sent = refs[2 * side : 2 * side + 2]
         for out, order in ((kept, (0, far)), (sent, (near, 2))):
             for index, flip in enumerate(order):
                 rows_of(out.at[index], place_ref[first + flip], side)
 
 
-def side_of(ref, index, rows, side):
-    half = ref.shape[-1] // 2
-    return ref[index, rows, side * half : side * half + half]
+def side_of(ref, index, rows, side, sides=2):
+    part = ref.shape[-1] // sides
+    return ref[index, rows, side * part : side * part + part]
 
 
 def weights_kernel(place_ref, own_ref, other_ref, *refs):
@@ -198,54 +201,49 @@
 
 
 def add_parts(refs, total):
-    half = total.shape[-1] // 2
-    for side in range(2):
-        kept, first, last = refs[side], refs[2 + side], refs[4 + side]
+    sides = len(refs) // 3
+    part = total.shape[-1] // sides
+    for side in range(sides):
+        kept, first, last = refs[side::sides]
         rows = kept[0] + first[0].astype(jnp.float32) + last[...].astype(jnp.float32)
-        total[:, :, side * half : side * half + half] = rows
+        total[:, :, side * part : side * part + part] = rows
 
 
 def second_kernel(place_ref, *refs):
     add_parts(refs[:6], refs[-2])
     add_parts(refs[6:12], refs[-1])
-    x_outs, y_outs = refs[12:16], refs[16:20]
-    query_out, x_total, y_total = refs[20:]
+    x_outs, y_outs = refs[12:14], refs[14:16]
+    query_out, x_total, y_total = refs[16:]
     query_out[...] = y_total[:, NZ // 4 * NX * 16 :]
 
     def x_rows(out, chosen, side):
         for z in range(NZ // 4):
             rows = pl.ds(pl.multiple_of(chosen * 16, 16), 16)
-            out[z] = side_of(x_total, z, rows, side).astype(out.dtype)
+            out[z] = side_of(x_total, z, rows, side, 1).astype(out.dtype)
 
     def y_rows(out, chosen, side):
         for z in range(NZ // 4):
             rows = pl.ds(pl.multiple_of(z * NX * 16 + chosen * 16, 16), 16)
-            out[z] = side_of(y_total, 0, rows, side).astype(out.dtype)
+            out[z] = side_of(y_total, 0, rows, side, 1).astype(out.dtype)
 
     split(place_ref, 4, x_rows, x_outs)
     split(place_ref, 0, y_rows, y_outs)
 
 
 def last_kernel(*refs):
-    out, x_total, y_total = refs[12:]
+    out, x_total, y_total = refs[6:]
     half = x_total.shape[2]
-    add_parts(refs[:6], x_total)
-    add_parts(refs[6:12], y_total)
+    add_parts(refs[:3], x_total)
+    add_parts(refs[3:6], y_total)
     out[:, :, :half] = x_total[...].astype(out.dtype)
     out[:, :, half:] = y_total[...].astype(out.dtype)
 
 
 def encoded_kernel(order_ref, *refs):
-    grads, pieces, out_ref, results, sems = refs[:4], refs[4:-3], *refs[-3:]
-    half = grads[0].shape[1]
-    core = order_ref[NZ]
+    grads, pieces, out_ref, results, sems = refs[0], refs[1:-3], *refs[-3:]
     stores = []
     for k, piece in enumerate(pieces):
-        total = None
-        for index, grad in enumerate(grads):
-            side, part = lax.rem(core + index // 2, NC), index % 2
-            term = dot_last(grad[...], piece[side, :, part * half : part * half + half])
-            total = term if total is None else total + term
+        total = dot_last(grads[0], piece[0]) + dot_last(grads[1], piece[1])
         results[k] = total.astype(jnp.bfloat16)
         columns = pl.ds(pl.multiple_of(order_ref[k] * 256, 256), 256)
         store = pltpu.make_async_copy(results.at[k], out_ref.at[:, columns], sems.at[k])
@@ -296,7 +294,8 @@
 
 def halving(outs, axes, steps, beside=()):
     kept, sent = outs[0::2], outs[1::2]
-    ways = [(axis, *bits) for axis in axes for bits in ((1, 3), (3, 1))]
+    sides = len(kept) // 2
+    ways = [(axis, *bits) for axis in axes for bits in ((1, 3), (3, 1))[:sides]]
     first = [send(value, flipped(axis, near)) for value, (axis, near, _) in zip(sent, ways)]
     first = lax.optimization_barrier(first)
 
@@ -315,9 +314,9 @@
     last = [send(value, flipped(axis, far)) for value, (axis, _, far) in zip(middle, ways)]
     last, beside = lax.optimization_barrier((last, beside))
     operands, specs = [], []
-    for start in (0, 2):
+    for start in (0, sides):
         for values in (kept, first, last):
-            for value in values[start : start + 2]:
+            for value in values[start : start + sides]:
                 operands.append(value)
                 inner = value.shape[-3:]
                 shape = (1,) * (value.ndim - 3) + (inner[0] // steps, *inner[1:])
@@ -341,7 +340,7 @@
     smem = pl.BlockSpec(memory_space=pltpu.SMEM)
 
     shard = jnp.stack([key_weight, value_weight])
-    shards = [shard] + [send(shard, along("x", k)) for k in range(1, NX)]
+    shards = [shard] + [send(shard, flipped("x", bits)) for bits in (1, 3)]
 
     stats_shape = like((3 * pairs, 2 * answer), f32)
     row_spec = pl.BlockSpec((answer, 2 * PAIR), lambda p: (0, p))
@@ -349,46 +348,21 @@
     stats = kernel_call(
         stats_kernel,
         "stats",
-        stats_shape,
+        pltpu.VMEM(stats_shape.shape, f32),
         62,
         grid=(pairs // 2,),
         in_specs=[smem, row_spec, key_spec, key_spec, row_spec],
         out_specs=pl.BlockSpec(stats_shape.shape, lambda p: (0, 0)),
     )(lengths, queries, key_rows, value_rows, grad_out)
 
-    chip_stats = kernel_call(merge_kernel, "merge", stats_shape)(stats, swap_cores(stats))
-    all_stats = [chip_stats] + [send(chip_stats, along("y", k)) for k in (1, 3)]
-    *shards, encoded_other, late = lax.optimization_barrier((*shards, swap_cores(encoded), chip_stats))
-    all_stats.append(send(late, along("y", 2)))
-
-    def grads(first_pair):
-        def rows(p):
-            return (0, first_pair // 2 + p)
-
-        row_spec = pl.BlockSpec((answer, 2 * PAIR), rows)
-        key_spec = pl.BlockSpec((keys, 2 * PAIR), rows)
-        out_spec = pl.BlockSpec((keys, 2 * PAIR), lambda p: (0, p))
-        stats_spec = pl.BlockSpec(stats_shape.shape, lambda p: (0, 0))
-        query_spec = pl.BlockSpec((1, PAIR, answer), lambda p: (p, 0, 0))
-        return kernel_call(
-            functools.partial(grads_kernel, first_pair),
-            "grads",
-            [
-                like((keys, half), bf16),
-                pltpu.HBM((keys, half), bf16),
-                like((NY // 2, PAIR, answer), f32),
-                like((NY // 2, PAIR, answer), bf16),
-            ],
-            grid=(pairs // 4,),
-            in_specs=[smem, smem, row_spec, key_spec, key_spec, row_spec] + [stats_spec] * NY,
-            out_specs=[out_spec, out_spec, query_spec, query_spec],
-        )(core[None], lengths, queries, key_rows, value_rows, grad_out, *all_stats)
-
-    mine_a, sent_a, query_kept_a, query_sent_a = grads(0)
-    received_a = swap_cores(sent_a)
+    shards.append(send(tie(shards[1], stats), flipped("x", 3)))
+    stats = kernel_call(merge_kernel, "merge", stats_shape)(stats, send(stats, along("core", 1)))
+    met, encoded_other = lax.optimization_barrier((send(stats, flipped("y", 1)), swap_cores(encoded)))
+    stats = kernel_call(merge_kernel, "merge", stats_shape)(stats, met)
+    all_stats = [stats, send(stats, flipped("y", 3))]
 
     whole_vmem = pl.BlockSpec(memory_space=pltpu.VMEM)
-    shards = lax.optimization_barrier((*shards, mine_a))[:-1]
+    shards = lax.optimization_barrier((*shards, stats))[:-1]
     ordered = kernel_call(
         arrange_kernel,
         "arrange",
@@ -400,7 +374,43 @@
     around = permutation(lambda z, x, y, c: (z + 1 - 2 * c, x, y, c))
     pieces = [ordered, send(ordered, around)]
 
-    mine_b, sent_b, query_kept_b, query_sent_b = grads(pairs // 2)
+    def grads(first_pair, joint):
+        def rows(p):
+            return (0, first_pair // 2 + p)
+
+        row_spec = pl.BlockSpec((answer, 2 * PAIR), rows)
+        key_spec = pl.BlockSpec((keys, 2 * PAIR), rows)
+        out_spec = pl.BlockSpec((keys, 2 * PAIR), lambda p: (0, p))
+        stats_spec = pl.BlockSpec(stats_shape.shape, lambda p: (0, 0))
+        query_spec = pl.BlockSpec((1, PAIR, answer), lambda p: (p, 0, 0))
+        joint_spec = pl.BlockSpec((2, keys, 2 * PAIR), lambda p: (0, 0, first_pair // 2 + p))
+        operands = (core[None], lengths, queries, key_rows, value_rows, grad_out, *all_stats)
+        specs = [smem, smem, row_spec, key_spec, key_spec, row_spec] + [stats_spec] * len(all_stats)
+        aliases = {}
+        if joint is not None:
+            aliases = {len(operands): 0}
+            operands += (joint,)
+            specs.append(pl.BlockSpec(memory_space=pl.ANY))
+        return kernel_call(
+            functools.partial(grads_kernel, first_pair),
+            "grads",
+            [
+                pltpu.HBM((2, keys, features), bf16),
+                like((keys, half), bf16),
+                like((keys, half), bf16),
+                like((NY // 2, PAIR, answer), f32),
+                like((NY // 2, PAIR, answer), bf16),
+            ],
+            grid=(pairs // 4,),
+            in_specs=specs,
+            out_specs=[joint_spec, out_spec, out_spec, query_spec, query_spec],
+            input_output_aliases=aliases,
+        )(*operands)
+
+    joint, mine_a, sent_a, query_kept_a, query_sent_a = grads(0, None)
+    received_a = swap_cores(sent_a)
+
+    joint, mine_b, sent_b, query_kept_b, query_sent_b = grads(pairs // 2, joint)
     received_b = swap_cores(sent_b)
     query_received = [swap_cores(query_sent_a), swap_cores(query_sent_b)]
 
@@ -414,15 +424,15 @@
     x_shape = (2, NZ, 64, half // 2)
     y_shape = (2, 4, NZ // 4 * NX * 16 + query_rows, half // 2)
 
-    def split_outs(shape):
+    def split_outs(shape, sides):
         spec = pl.BlockSpec((2, shape[1] // 4, *shape[2:]), lambda i: (0, i, 0, 0))
-        return [like(shape, f32), like(shape, bf16)] * 2, [spec] * 4
+        return [like(shape, f32), like(shape, bf16)] * sides, [spec] * 2 * sides
 
     def total(shape):
         return pltpu.VMEM((shape[1] // 4, shape[2], 2 * shape[3]), f32)
 
-    x_outs, x_specs = split_outs(x_shape)
-    y_outs, y_specs = split_outs(y_shape)
+    x_outs, x_specs = split_outs(x_shape, 2)
+    y_outs, y_specs = split_outs(y_shape, 2)
     terms = kernel_call(
         weights_kernel,
         "weights",
@@ -450,8 +460,8 @@
 
     operands, specs, middle, _ = halving(terms, "xy", 4)
     pieces.append(send(tie(pieces[2], middle), around))
-    chunk, query_shape = (2, NZ, 16, half // 2), (4, query_rows, half)
-    chunk_outs, chunk_specs = split_outs(chunk)
+    chunk, query_shape = (2, NZ, 16, half), (4, query_rows, half)
+    chunk_outs, chunk_specs = split_outs(chunk, 1)
     *second, query_grad = kernel_call(
         second_kernel,
         "second",
@@ -495,13 +505,13 @@
         24,
         flops=4 * keys * width * features,
         moved=14 * MIB,
-        in_specs=[smem] + [whole_vmem] * (NZ + 4),
+        in_specs=[smem] + [whole_vmem] * (NZ + 1),
         out_specs=in_hbm,
         scratch_shapes=[
             pltpu.VMEM((NZ, keys, width // NZ), bf16),
             pltpu.SemaphoreType.DMA((NZ,)),
         ],
-    )(jnp.stack([*order, core]), mine_a, mine_b, sent_a, sent_b, *pieces, *swapped, across)
+    )(jnp.stack(order), joint, *pieces, *swapped, across)
     summed = tie(last, encoded_grad).reshape(NZ, NC, 8, features).astype(f32).sum(0)
     key_weight_grad, value_weight_grad = summed[0], summed[1]
     return query_grad, encoded_grad[None], key_weight_grad, value_weight_grad

time: 128 us -> 125 us (0.977)
  waiting for transfers between devices: 35.8 us -> 44.4 us
  starting transfers between devices: 47.1 us -> 41.5 us
  local copies, waits for them, and re-layouts: 8.09 us -> 2.86 us
    ppermute x26 -> x22, waiting for transfers between devices: 33.1 us -> 40.7 us  [send(): return lax.ppermute(value, AXES, links)]
    unnamed x35 -> x17, local copies, waits for them, and re-layouts: 7.29 us -> 1.45 us
    ppermute x9 -> x8, starting transfers between devices: 10.2 us -> 6 us  [swap_cores(): lax.ppermute(value, AXES, permutation(lambda z, x, y, c: (z, x, y, 1 - c)))]
    all_to_all x1, waiting for transfers between devices: 0.01 us -> 2.25 us  [on_device(): lax.all_to_all(last.reshape(NZ * NC, 8, features), AXES, 0, 0, tiled=True...]
    all_to_all x1, starting transfers between devices: 6.88 us -> 5.33 us  [on_device(): lax.all_to_all(last.reshape(NZ * NC, 8, features), AXES, 0, 0, tiled=True...]
    ppermute x9 -> x8, waiting for transfers between devices: 2.7 us -> 1.42 us  [swap_cores(): lax.ppermute(value, AXES, permutation(lambda z, x, y, c: (z, x, y, 1 - c)))]
    pallas_call x4 -> x5, Pallas kernels: 14.4 us -> 13.4 us  [the longest x2 8.21 us: grads(): kernel_call(functools.partial(grads_kernel, first_pair), 'grads', [pltpu....]
    ppermute x26 -> x22, starting transfers between devices: 30 us -> 30.1 us  [send(): return lax.ppermute(value, AXES, links)]
  transfers between devices with their start and end apart: 36 -> 31, of which waited for: 18 -> 17; matrix products, arithmetic and copies ran while one was open for 2% -> 2% of each run, Pallas kernels for 21% -> 25%
where the time goes in v4:
time: 125 us
  waiting for transfers between devices  44.4 us (36%)
  starting transfers between devices  41.5 us (33%)
  Pallas kernels  33.9 us (27%)
  local copies, waits for them, and re-layouts  2.86 us (2%)
  between operations  1.49 us (1%)
    ppermute x22, waiting for transfers between devices, send(): return lax.ppermute(value, AXES, links)  40.7 us
    ppermute x22, starting transfers between devices, send(): return lax.ppermute(value, AXES, links)  30.1 us
    pallas_call x1, Pallas kernels, on_device(): kernel_call(encoded_kernel, 'encoded', pltpu.HBM((keys, width), bf16), 24...  8.58 us
    pallas_call x2, Pallas kernels, grads(): kernel_call(functools.partial(grads_kernel, first_pair), 'grads', [pltpu....  8.21 us
    pallas_call x1, Pallas kernels, on_device(): kernel_call(weights_kernel, 'weights', x_outs + y_outs, 20, grid=(4,), in...  7.41 us
    ppermute x8, starting transfers between devices, swap_cores(): lax.ppermute(value, AXES, permutation(lambda z, x, y, c: (z, x, y, 1 - c)))  6 us
    all_to_all x1, starting transfers between devices, on_device(): lax.all_to_all(last.reshape(NZ * NC, 8, features), AXES, 0, 0, tiled=True...  5.33 us
    pallas_call x1, Pallas kernels, on_device(): kernel_call(stats_kernel, 'stats', pltpu.VMEM(stats_shape.shape, f32), 62...  5.14 us
  transfers between devices with their start and end apart: 31, of which 17 were waited for; matrix products, arithmetic and copies ran while one was open for 2% of the time, Pallas kernels for 25%

profile of v4, /device:TPU:1, one launch (start us, length us, event | category | flops | bytes accessed | tf_op | source)
XLA Modules:
  0.0 125.1 jit_solution(17790198854190745957)
XLA Ops:
  0.6 3.3 %collective-permute-start.2 = (bf16[512,2048]{1,0:T(8,128)(2,1)}, bf16[512,2048]{1,0:T(8,128)(2,1)}, u32[]{:S(2)}, u32[]{:S(2)}) collective-permute-start(bf16[512,2048]{1,0:T(8,128)(2,1)} %bitcast.55), channel_id=1, source_target_pairs={{0,1},{1,0},{2,3},{3,2},{4,5},{5,4},{6,7},{7,6},{8,9},{9,8},{10,11... | collective-permute-start | bytes 6291464 | tf_op jit(solution)/shard_map/ppermute | solution.py:46
  4.0 1.0 pad_maximum_fusion.refs_0_
  5.0 0.1 collective-permute-start.16
  5.1 1.3 %collective-permute-start.17 = (bf16[2,64,1024]{2,1,0:T(8,128)(2,1)S(1)}, bf16[2,64,1024]{2,1,0:T(8,128)(2,1)}, u32[]{:S(2)}, u32[]{:S(2)}) collective-permute-start(bf16[2,64,1024]{2,1,0:T(8,128)(2,1)S(1)} %pad_maximum_fusion.refs_0_), channel_id=1, source_target_pairs={{0,24},{1,25},{2,26},{3,27},{4,28},{5,29},{6,30},{7,31},{8,16},{9,... | collective-permute-start | bytes 786440 | tf_op jit(solution)/shard_map/ppermute | solution.py:284
  7.0 0.0 copy-start
  7.0 0.0 copy-start.2
  7.0 5.1 %stats.1.left_ref = f32[24,512]{1,0:T(8,128)S(1)} custom-call(s32[1]{0:T(128)S(6)} %copy.20.length_ref, bf16[256,1024]{1,0:T(8,128)(2,1)} %bitcast.49, bf16[512,1024]{1,0:T(8,128)(2,1)} %bitcast.43, bf16[512,1024]{1,0:T(8,128)(2,1)} %bitcast.46, bf16[256,1024]{1,0:T(8,128)(2,1)} %bitcast.52), custom_call_target="tpu_custom_call" | custom-call | tf_op jit(solution)/shard_map/stats/pallas_call | solution.py:348
  12.2 0.0 copy-start.1
  12.2 0.0 copy-start.3
  12.2 0.9 collective-permute-done.16.refs_1_
  13.1 0.7 collective-permute-start.18
  13.8 1.1 collective-permute-start
  14.9 0.9 collective-permute-done.right_ref
  15.8 1.4 %collective-permute-start.1 = (f32[24,512]{1,0:T(8,128)S(1)}, f32[24,512]{1,0:T(8,128)S(1)}, u32[]{:S(2)}, u32[]{:S(2)}) collective-permute-start(f32[24,512]{1,0:T(8,128)S(1)} %merge.2.left_ref), channel_id=1, source_target_pairs={{0,2},{1,3},{2,0},{3,1},{4,6},{5,7},{6,4},{7,5},{8,10},{9,11},{10,... | collective-permute-start | bytes 147464 | tf_op jit(solution)/shard_map/ppermute | solution.py:284
  17.2 0.7 stack.71.place_ref
  17.9 1.4 %collective-permute-done.1.right_ref = f32[24,512]{1,0:T(8,128)S(1)} collective-permute-done((f32[24,512]{1,0:T(8,128)S(1)}, f32[24,512]{1,0:T(8,128)S(1)}, u32[]{:S(2)}, u32[]{:S(2)}) %collective-permute-start.1) | collective-permute-done | bytes 49184 | tf_op jit(solution)/shard_map/ppermute | solution.py:284
  19.2 0.0 collective-permute-done.17.refs_2_
  19.3 2.4 %collective-permute-done.18.refs_3_ = bf16[2,64,1024]{2,1,0:T(8,128)(2,1)} collective-permute-done((bf16[2,64,1024]{2,1,0:T(8,128)(2,1)}, bf16[2,64,1024]{2,1,0:T(8,128)(2,1)}, u32[]{:S(2)}, u32[]{:S(2)}) %collective-permute-start.18) | collective-permute-done | bytes 262176 | tf_op jit(solution)/shard_map/ppermute | solution.py:284
  21.6 0.7 copy-done.6
  22.3 2.2 %arrange.1.refs_1_ = bf16[2,256,1024]{2,1,0:T(8,128)(2,1)} custom-call(s32[8]{0:T(128)S(1)} %copy-done.6, bf16[2,64,1024]{2,1,0:T(8,128)(2,1)S(1)} %pad_maximum_fusion.refs_0_, bf16[2,64,1024]{2,1,0:T(8,128)(2,1)} %collective-permute-done.16.refs_1_, bf16[2,64,1024]{2,1,0:T(8,128)(2,1)} %collective-permute-done.17.refs_2_, ...), custom_call_target="tpu_custom_call" | custom-call | tf_op jit(solution)/shard_map/arrange/pallas_call | solution.py:366
  24.5 5.0 %collective-permute-start.19 = (bf16[2,256,1024]{2,1,0:T(8,128)(2,1)}, bf16[2,256,1024]{2,1,0:T(8,128)(2,1)}, u32[]{:S(2)}, u32[]{:S(2)}) collective-permute-start(bf16[2,256,1024]{2,1,0:T(8,128)(2,1)} %arrange.1.refs_1_), channel_id=1, source_target_pairs={{0,32},{1,225},{2,34},{3,227},{4,36},{5,229},{6,38},{7,231},{8,40}... | collective-permute-start | bytes 3145736 | tf_op jit(solution)/shard_map/ppermute | solution.py:284
  29.5 2.7 %collective-permute-start.3 = (f32[24,512]{1,0:T(8,128)S(1)}, f32[24,512]{1,0:T(8,128)S(1)}, u32[]{:S(2)}, u32[]{:S(2)}) collective-permute-start(f32[24,512]{1,0:T(8,128)S(1)} %merge.3.refs_0_), channel_id=1, source_target_pairs={{0,6},{1,7},{2,4},{3,5},{4,2},{5,3},{6,0},{7,1},{8,14},{9,15},{10,... | collective-permute-start | bytes 147464 | tf_op jit(solution)/shard_map/ppermute | solution.py:284
  32.2 1.9 %collective-permute-done.3.refs_1_ = f32[24,512]{1,0:T(8,128)S(1)} collective-permute-done((f32[24,512]{1,0:T(8,128)S(1)}, f32[24,512]{1,0:T(8,128)S(1)}, u32[]{:S(2)}, u32[]{:S(2)}) %collective-permute-start.3) | collective-permute-done | bytes 49184 | tf_op jit(solution)/shard_map/ppermute | solution.py:284
  34.1 4.1 %grads.2 = (bf16[2,512,1024]{2,1,0:T(8,128)(2,1)}, bf16[512,512]{1,0:T(8,128)(2,1)S(1)}, bf16[512,512]{1,0:T(8,128)(2,1)S(1)}, f32[2,128,256]{2,1,0:T(8,128)S(1)}, bf16[2,128,256]{2,1,0:T(8,128)(2,1)S(1)}) custom-call(s32[1]{0:T(128)} %bitcast.13.core_ref, s32[1]{0:T(128)S(6)} %copy.20.length_ref, bf16[256,1024]{1,0:T(8,128)(2,1)S(1)} %bitcast.50, ...), custom_call_target="tpu_custom_call" | custom-call | tf_op jit(solution)/shard_map/grads/pallas_call | solution.py:394
  38.3 4.1 %grads.3 = (bf16[2,512,1024]{2,1,0:T(8,128)(2,1)}, bf16[512,512]{1,0:T(8,128)(2,1)S(1)}, bf16[512,512]{1,0:T(8,128)(2,1)S(1)}, f32[2,128,256]{2,1,0:T(8,128)S(1)}, bf16[2,128,256]{2,1,0:T(8,128)(2,1)S(1)}) custom-call(s32[1]{0:T(128)} %bitcast.13.core_ref, s32[1]{0:T(128)S(6)} %copy.20.length_ref, ...), custom_call_target="tpu_custom_call", output_to_operand_aliasing={{0}: (8, {})} | custom-call | tf_op jit(solution)/shard_map/grads/pallas_call | solution.py:394
  42.4 0.5 collective-permute-start.5
  42.8 0.0 collective-permute-start.6
  42.9 0.5 collective-permute-start.7
  43.4 1.2 collective-permute-done.6.refs_6_
  44.6 0.2 collective-permute-done.7.refs_7_
  44.8 0.0 collective-permute-done.4.refs_2_
  44.8 7.4 %weights.1 = (f32[2,8,64,256]{3,2,1,0:T(8,128)S(1)}, bf16[2,8,64,256]{3,2,1,0:T(8,128)(2,1)S(1)}, f32[2,8,64,256]{3,2,1,0:T(8,128)S(1)}, bf16[2,8,64,256]{3,2,1,...) custom-call(s32[8]{0:T(128)S(1)} %copy-done.7, ...), custom_call_target="tpu_custom_call" | custom-call | tf_op jit(solution)/shard_map/weights/pallas_call | solution.py:436
  52.2 2.1 %collective-permute-start.20 = (bf16[2,256,1024]{2,1,0:T(8,128)(2,1)}, bf16[2,256,1024]{2,1,0:T(8,128)(2,1)}, u32[]{:S(2)}, u32[]{:S(2)}) collective-permute-start(bf16[2,256,1024]{2,1,0:T(8,128)(2,1)} %collective-permute-done.19.refs_2_), channel_id=1, source_target_pairs={{0,32},{1,225},{2,34},{3,227},{4,36},{5,229},{6,38},{7,231},{8,40}... | collective-permute-start | bytes 3145736 | tf_op jit(solution)/shard_map/ppermute | solution.py:284
  54.3 0.1 collective-permute-start.10
  54.3 2.7 %collective-permute-start.11 = (bf16[2,4,144,256]{3,2,1,0:T(8,128)(2,1)S(1)}, bf16[2,4,144,256]{3,2,1,0:T(8,128)(2,1)S(1)}, u32[]{:S(2)}, u32[]{:S(2)}) collective-permute-start(bf16[2,4,144,256]{3,2,1,0:T(8,128)(2,1)S(1)} %get-tuple-element.76), channel_id=1, source_target_pairs={{0,6},{1,7},{2,4},{3,5},{4,2},{5,3},{6,0},{7,1},{8,14},{9,15},{10,... | collective-permute-start | bytes 1769480 | tf_op jit(solution)/shard_map/ppermute | solution.py:284
  57.0 1.5 %collective-permute-start.9 = (bf16[2,8,64,256]{3,2,1,0:T(8,128)(2,1)S(1)}, bf16[2,8,64,256]{3,2,1,0:T(8,128)(2,1)S(1)}, u32[]{:S(2)}, u32[]{:S(2)}) collective-permute-start(bf16[2,8,64,256]{3,2,1,0:T(8,128)(2,1)S(1)} %get-tuple-element.74), channel_id=1, source_target_pairs={{0,24},{1,25},{2,26},{3,27},{4,28},{5,29},{6,30},{7,31},{8,16},{9,... | collective-permute-start | bytes 1572872 | tf_op jit(solution)/shard_map/ppermute | solution.py:284
  58.5 11.7 %collective-permute-done.8.refs_4_.refs_2_ = bf16[2,8,64,256]{3,2,1,0:T(8,128)(2,1)S(1)} collective-permute-done((bf16[2,8,64,256]{3,2,1,0:T(8,128)(2,1)S(1)}, bf16[2,8,64,256]{3,2,1,0:T(8,128)(2,1)S(1)}, u32[]{:S(2)}, u32[]{:S(2)}) %collective-permute-start.8) | collective-permute-done | bytes 524320 | tf_op jit(solution)/shard_map/ppermute | solution.py:284
  70.2 0.9 collective-permute-done.9.refs_5_.refs_3_
  71.1 0.3 middle.2
  71.4 2.6 %collective-permute-start.21 = (bf16[2,256,1024]{2,1,0:T(8,128)(2,1)}, bf16[2,256,1024]{2,1,0:T(8,128)(2,1)}, u32[]{:S(2)}, u32[]{:S(2)}) collective-permute-start(bf16[2,256,1024]{2,1,0:T(8,128)(2,1)} %collective-permute-done.20.refs_3_), channel_id=1, source_target_pairs={{0,32},{1,225},{2,34},{3,227},{4,36},{5,229},{6,38},{7,231},{8,40}... | collective-permute-start | bytes 3145736 | tf_op jit(solution)/shard_map/ppermute | solution.py:284
  74.0 1.7 %collective-permute-start.14 = (bf16[4,144,256]{2,1,0:T(8,128)(2,1)S(1)}, bf16[4,144,256]{2,1,0:T(8,128)(2,1)S(1)}, u32[]{:S(2)}, u32[]{:S(2)}) collective-permute-start(bf16[4,144,256]{2,1,0:T(8,128)(2,1)S(1)} %get-tuple-element.85), channel_id=1, source_target_pairs={{0,6},{1,7},{2,4},{3,5},{4,2},{5,3},{6,0},{7,1},{8,14},{9,15},{10,... | collective-permute-start | bytes 884744 | tf_op jit(solution)/shard_map/ppermute | solution.py:284
  75.7 1.2 collective-permute-start.12
  76.8 7.5 %collective-permute-done.12.refs_4_ = bf16[8,64,256]{2,1,0:T(8,128)(2,1)S(1)} collective-permute-done((bf16[8,64,256]{2,1,0:T(8,128)(2,1)S(1)}, bf16[8,64,256]{2,1,0:T(8,128)(2,1)S(1)}, u32[]{:S(2)}, u32[]{:S(2)}) %collective-permute-start.12) | collective-permute-done | bytes 262176 | tf_op jit(solution)/shard_map/ppermute | solution.py:284
  84.4 0.3 collective-permute-done.13.refs_5_
  84.7 1.2 second.1
  85.9 0.1 collective-permute-done.21.refs_4_
  86.0 3.1 %collective-permute-start.26 = (bf16[2,256,1024]{2,1,0:T(8,128)(2,1)}, bf16[2,256,1024]{2,1,0:T(8,128)(2,1)S(1)}, u32[]{:S(2)}, u32[]{:S(2)}) collective-permute-start(bf16[2,256,1024]{2,1,0:T(8,128)(2,1)} %collective-permute-done.21.refs_4_), channel_id=1, source_target_pairs={{0,32},{1,225},{2,34},{3,227},{4,36},{5,229},{6,38},{7,231},{8,40}... | collective-permute-start | bytes 3145736 | tf_op jit(solution)/shard_map/ppermute | solution.py:284
  89.2 0.7 collective-permute-start.22
  89.8 7.0 %collective-permute-done.22.refs_2_.refs_1_ = bf16[2,8,16,512]{3,2,1,0:T(8,128)(2,1)S(1)} collective-permute-done((bf16[2,8,16,512]{3,2,1,0:T(8,128)(2,1)S(1)}, bf16[2,8,16,512]{3,2,1,0:T(8,128)(2,1)S(1)}, u32[]{:S(2)}, u32[]{:S(2)}) %collective-permute-start.22) | collective-permute-done | bytes 262176 | tf_op jit(solution)/shard_map/ppermute | solution.py:284
  96.8 1.3 %collective-permute-done.23.refs_3_.refs_4_ = bf16[2,8,16,512]{3,2,1,0:T(8,128)(2,1)S(1)} collective-permute-done((bf16[2,8,16,512]{3,2,1,0:T(8,128)(2,1)S(1)}, bf16[2,8,16,512]{3,2,1,0:T(8,128)(2,1)S(1)}, u32[]{:S(2)}, u32[]{:S(2)}) %collective-permute-start.23) | collective-permute-done | bytes 262176 | tf_op jit(solution)/shard_map/ppermute | solution.py:284
  98.1 0.1 middle.3
  98.2 0.7 collective-permute-start.24
  98.9 1.5 %collective-permute-start.25 = (bf16[8,16,512]{2,1,0:T(8,128)(2,1)S(1)}, bf16[8,16,512]{2,1,0:T(8,128)(2,1)S(1)}, u32[]{:S(2)}, u32[]{:S(2)}) collective-permute-start(bf16[8,16,512]{2,1,0:T(8,128)(2,1)S(1)} %get-tuple-element.107), channel_id=1, source_target_pairs={{0,24},{1,25},{2,26},{3,27},{4,28},{5,29},{6,30},{7,31},{8,16},{9,... | collective-permute-start | bytes 393224 | tf_op jit(solution)/shard_map/ppermute | solution.py:284
  100.4 3.8 %collective-permute-done.24.refs_2_ = bf16[8,16,512]{2,1,0:T(8,128)(2,1)S(1)} collective-permute-done((bf16[8,16,512]{2,1,0:T(8,128)(2,1)S(1)}, bf16[8,16,512]{2,1,0:T(8,128)(2,1)S(1)}, u32[]{:S(2)}, u32[]{:S(2)}) %collective-permute-start.24) | collective-permute-done | bytes 131104 | tf_op jit(solution)/shard_map/ppermute | solution.py:284
  104.2 0.6 collective-permute-done.25.refs_5_
  104.9 0.8 last.1
  105.7 1.2 collective-permute-start.27
  106.9 0.5 collective-permute-start.29
  107.4 5.3 %all-to-all-start = ((bf16[16,8,1024]{2,1,0:T(8,128)(2,1)}), bf16[16,8,1024]{2,1,0:T(8,128)(2,1)S(1)}, u32[]{:S(2)}, u32[]{:S(2)}) async-start(bf16[16,8,1024]{2,1,0:T(8,128)(2,1)} %bitcast.29), calls=%async_computation | async-start | bytes 524288 | tf_op jit(solution)/shard_map/all_to_all | solution.py:489
  112.7 0.1 stack.80.order_ref
  112.8 0.7 copy.15
  113.6 8.6 %encoded.1 = bf16[512,2048]{1,0:T(8,128)(2,1)} custom-call(s32[8]{0:T(128)S(1)} %stack.80.order_ref, bf16[2,512,1024]{2,1,0:T(8,128)(2,1)S(1)} %copy-done.5, bf16[2,256,1024]{2,1,0:T(8,128)(2,1)} %arrange.1.refs_1_, bf16[2,256,1024]{2,1,0:T(8,128)(2,1)} %collective-permute-done.19.refs_2_, bf16[2,256,1024]{2,1,0:T(8,128)(2,1)} %collective-permute-done.20.refs_3_, ...), custom_call_target="tpu_custom_call" | custom-call | flops 4294967296 | bytes 14680064 | tf_op jit(solution)/shard_map/encoded/pallas_call | solution.py:501
  122.1 2.3 %all-to-all-done = bf16[16,8,1024]{2,1,0:T(8,128)(2,1)S(1)} async-done(((bf16[16,8,1024]{2,1,0:T(8,128)(2,1)}), bf16[16,8,1024]{2,1,0:T(8,128)(2,1)S(1)}, u32[]{:S(2)}, u32[]{:S(2)}) %all-to-all-start) | async-done | bytes 262176 | tf_op jit(solution)/shard_map/all_to_all | solution.py:489
  124.4 0.6 slice_bitcast_fusion
  (34 shorter events, 0.2 us)
Async XLA Ops:
  0.6 18.6 %collective-permute-start.2 = (bf16[512,2048]{1,0:T(8,128)(2,1)}, bf16[512,2048]{1,0:T(8,128)(2,1)}, u32[]{:S(2)}, u32[]{:S(2)}) collective-permute-start(bf16[512,2048]{1,0:T(8,128)(2,1)} %bitcast.55), channel_id=1, source_target_pairs={{0,1},{1,0},{2,3},{3,2},{4,5},{5,4},{6,7},{7,6},{8,9},{9,8},{10,11... | collective-permute-start | bytes 6291464 | tf_op jit(solution)/shard_map/ppermute | solution.py:46
  5.0 8.1 %collective-permute-start.16 = (bf16[2,64,1024]{2,1,0:T(8,128)(2,1)S(1)}, bf16[2,64,1024]{2,1,0:T(8,128)(2,1)}, u32[]{:S(2)}, u32[]{:S(2)}) collective-permute-start(bf16[2,64,1024]{2,1,0:T(8,128)(2,1)S(1)} %pad_maximum_fusion.refs_0_), channel_id=1, source_target_pairs={{0,8},{1,9},{2,10},{3,11},{4,12},{5,13},{6,14},{7,15},{8,0},{9,1},... | collective-permute-start | bytes 786440 | tf_op jit(solution)/shard_map/ppermute | solution.py:284
  5.1 14.2 %collective-permute-start.17 = (bf16[2,64,1024]{2,1,0:T(8,128)(2,1)S(1)}, bf16[2,64,1024]{2,1,0:T(8,128)(2,1)}, u32[]{:S(2)}, u32[]{:S(2)}) collective-permute-start(bf16[2,64,1024]{2,1,0:T(8,128)(2,1)S(1)} %pad_maximum_fusion.refs_0_), channel_id=1, source_target_pairs={{0,24},{1,25},{2,26},{3,27},{4,28},{5,29},{6,30},{7,31},{8,16},{9,... | collective-permute-start | bytes 786440 | tf_op jit(solution)/shard_map/ppermute | solution.py:284
  7.0 27.1 %copy-start = (bf16[1,512,1024]{2,1,0:T(8,128)(2,1)S(1)}, bf16[1,512,1024]{2,1,0:T(8,128)(2,1)}, u32[]{:S(2)}) copy-start(bf16[1,512,1024]{2,1,0:T(8,128)(2,1)} %param.9) | copy-start | bytes 3145732
  7.0 27.1 %copy-start.2 = (bf16[1,256,1024]{2,1,0:T(8,128)(2,1)S(1)}, bf16[1,256,1024]{2,1,0:T(8,128)(2,1)}, u32[]{:S(2)}) copy-start(bf16[1,256,1024]{2,1,0:T(8,128)(2,1)} %param.8) | copy-start | bytes 1572868
  12.2 22.0 %copy-start.1 = (bf16[1,512,1024]{2,1,0:T(8,128)(2,1)S(1)}, bf16[1,512,1024]{2,1,0:T(8,128)(2,1)}, u32[]{:S(2)}) copy-start(bf16[1,512,1024]{2,1,0:T(8,128)(2,1)} %param.10) | copy-start | bytes 3145732
  12.2 22.0 %copy-start.3 = (bf16[1,256,1024]{2,1,0:T(8,128)(2,1)S(1)}, bf16[1,256,1024]{2,1,0:T(8,128)(2,1)}, u32[]{:S(2)}) copy-start(bf16[1,256,1024]{2,1,0:T(8,128)(2,1)} %param.14) | copy-start | bytes 1572868
  13.1 8.6 %collective-permute-start.18 = (bf16[2,64,1024]{2,1,0:T(8,128)(2,1)}, bf16[2,64,1024]{2,1,0:T(8,128)(2,1)}, u32[]{:S(2)}, u32[]{:S(2)}) collective-permute-start(bf16[2,64,1024]{2,1,0:T(8,128)(2,1)} %collective-permute-done.16.refs_1_), channel_id=1, source_target_pairs={{0,24},{1,25},{2,26},{3,27},{4,28},{5,29},{6,30},{7,31},{8,16},{9,... | collective-permute-start | bytes 786440 | tf_op jit(solution)/shard_map/ppermute | solution.py:284
  13.8 2.0 %collective-permute-start = (f32[24,512]{1,0:T(8,128)S(1)}, f32[24,512]{1,0:T(8,128)S(1)}, u32[]{:S(2)}, u32[]{:S(2)}) collective-permute-start(f32[24,512]{1,0:T(8,128)S(1)} %stats.1.left_ref), channel_id=1, source_target_pairs={{0,1},{1,0},{2,3},{3,2},{4,5},{5,4},{6,7},{7,6},{8,9},{9,8},{10,11... | collective-permute-start | bytes 147464 | tf_op jit(solution)/shard_map/ppermute | solution.py:284
  15.8 3.4 %collective-permute-start.1 = (f32[24,512]{1,0:T(8,128)S(1)}, f32[24,512]{1,0:T(8,128)S(1)}, u32[]{:S(2)}, u32[]{:S(2)}) collective-permute-start(f32[24,512]{1,0:T(8,128)S(1)} %merge.2.left_ref), channel_id=1, source_target_pairs={{0,2},{1,3},{2,0},{3,1},{4,6},{5,7},{6,4},{7,5},{8,10},{9,11},{10,... | collective-permute-start | bytes 147464 | tf_op jit(solution)/shard_map/ppermute | solution.py:284
  21.6 0.7 copy-start.6
  24.5 27.7 %collective-permute-start.19 = (bf16[2,256,1024]{2,1,0:T(8,128)(2,1)}, bf16[2,256,1024]{2,1,0:T(8,128)(2,1)}, u32[]{:S(2)}, u32[]{:S(2)}) collective-permute-start(bf16[2,256,1024]{2,1,0:T(8,128)(2,1)} %arrange.1.refs_1_), channel_id=1, source_target_pairs={{0,32},{1,225},{2,34},{3,227},{4,36},{5,229},{6,38},{7,231},{8,40}... | collective-permute-start | bytes 3145736 | tf_op jit(solution)/shard_map/ppermute | solution.py:284
  29.5 4.6 %collective-permute-start.3 = (f32[24,512]{1,0:T(8,128)S(1)}, f32[24,512]{1,0:T(8,128)S(1)}, u32[]{:S(2)}, u32[]{:S(2)}) collective-permute-start(f32[24,512]{1,0:T(8,128)S(1)} %merge.3.refs_0_), channel_id=1, source_target_pairs={{0,6},{1,7},{2,4},{3,5},{4,2},{5,3},{6,0},{7,1},{8,14},{9,15},{10,... | collective-permute-start | bytes 147464 | tf_op jit(solution)/shard_map/ppermute | solution.py:284
  38.2 6.5 %collective-permute-start.4 = (bf16[512,512]{1,0:T(8,128)(2,1)S(1)}, bf16[512,512]{1,0:T(8,128)(2,1)S(1)}, u32[]{:S(2)}, u32[]{:S(2)}) collective-permute-start(bf16[512,512]{1,0:T(8,128)(2,1)S(1)} %get-tuple-element.65), channel_id=1, source_target_pairs={{0,1},{1,0},{2,3},{3,2},{4,5},{5,4},{6,7},{7,6},{8,9},{9,8},{10,11... | collective-permute-start | bytes 1572872 | tf_op jit(solution)/shard_map/ppermute | solution.py:46
  38.2 6.5 %copy-start.4 = (bf16[1,512,2048]{2,1,0:T(8,128)(2,1)S(1)}, bf16[1,512,2048]{2,1,0:T(8,128)(2,1)}, u32[]{:S(2)}) copy-start(bf16[1,512,2048]{2,1,0:T(8,128)(2,1)} %param.11) | copy-start | bytes 6291460
  38.2 6.5 %copy-start.7 = (s32[8]{0:T(128)S(1)}, s32[8]{0:T(128)}, u32[]{:S(2)}) copy-start(s32[8]{0:T(128)} %stack.71.place_ref) | copy-start | bytes 100
  42.4 2.4 %collective-permute-start.5 = (bf16[512,512]{1,0:T(8,128)(2,1)S(1)}, bf16[512,512]{1,0:T(8,128)(2,1)S(1)}, u32[]{:S(2)}, u32[]{:S(2)}) collective-permute-start(bf16[512,512]{1,0:T(8,128)(2,1)S(1)} %get-tuple-element.66), channel_id=1, source_target_pairs={{0,1},{1,0},{2,3},{3,2},{4,5},{5,4},{6,7},{7,6},{8,9},{9,8},{10,11... | collective-permute-start | bytes 1572872 | tf_op jit(solution)/shard_map/ppermute | solution.py:46
  42.8 1.7 %collective-permute-start.6 = (bf16[2,128,256]{2,1,0:T(8,128)(2,1)S(1)}, bf16[2,128,256]{2,1,0:T(8,128)(2,1)S(1)}, u32[]{:S(2)}, u32[]{:S(2)}) collective-permute-start(bf16[2,128,256]{2,1,0:T(8,128)(2,1)S(1)} %get-tuple-element.69), channel_id=1, source_target_pairs={{0,1},{1,0},{2,3},{3,2},{4,5},{5,4},{6,7},{7,6},{8,9},{9,8},{10,11... | collective-permute-start | bytes 393224 | tf_op jit(solution)/shard_map/ppermute | solution.py:46
  42.9 1.9 %collective-permute-start.7 = (bf16[2,128,256]{2,1,0:T(8,128)(2,1)S(1)}, bf16[2,128,256]{2,1,0:T(8,128)(2,1)S(1)}, u32[]{:S(2)}, u32[]{:S(2)}) collective-permute-start(bf16[2,128,256]{2,1,0:T(8,128)(2,1)S(1)} %get-tuple-element.70), channel_id=1, source_target_pairs={{0,1},{1,0},{2,3},{3,2},{4,5},{5,4},{6,7},{7,6},{8,9},{9,8},{10,11... | collective-permute-start | bytes 393224 | tf_op jit(solution)/shard_map/ppermute | solution.py:46
  52.2 19.2 %collective-permute-start.20 = (bf16[2,256,1024]{2,1,0:T(8,128)(2,1)}, bf16[2,256,1024]{2,1,0:T(8,128)(2,1)}, u32[]{:S(2)}, u32[]{:S(2)}) collective-permute-start(bf16[2,256,1024]{2,1,0:T(8,128)(2,1)} %collective-permute-done.19.refs_2_), channel_id=1, source_target_pairs={{0,32},{1,225},{2,34},{3,227},{4,36},{5,229},{6,38},{7,231},{8,40}... | collective-permute-start | bytes 3145736 | tf_op jit(solution)/shard_map/ppermute | solution.py:284
  54.3 16.9 %collective-permute-start.10 = (bf16[2,4,144,256]{3,2,1,0:T(8,128)(2,1)S(1)}, bf16[2,4,144,256]{3,2,1,0:T(8,128)(2,1)S(1)}, u32[]{:S(2)}, u32[]{:S(2)}) collective-permute-start(bf16[2,4,144,256]{3,2,1,0:T(8,128)(2,1)S(1)} %get-tuple-element.75), channel_id=1, source_target_pairs={{0,2},{1,3},{2,0},{3,1},{4,6},{5,7},{6,4},{7,5},{8,10},{9,11},{10,... | collective-permute-start | bytes 1769480 | tf_op jit(solution)/shard_map/ppermute | solution.py:284
  54.3 16.8 %collective-permute-start.11 = (bf16[2,4,144,256]{3,2,1,0:T(8,128)(2,1)S(1)}, bf16[2,4,144,256]{3,2,1,0:T(8,128)(2,1)S(1)}, u32[]{:S(2)}, u32[]{:S(2)}) collective-permute-start(bf16[2,4,144,256]{3,2,1,0:T(8,128)(2,1)S(1)} %get-tuple-element.76), channel_id=1, source_target_pairs={{0,6},{1,7},{2,4},{3,5},{4,2},{5,3},{6,0},{7,1},{8,14},{9,15},{10,... | collective-permute-start | bytes 1769480 | tf_op jit(solution)/shard_map/ppermute | solution.py:284
  57.0 13.2 %collective-permute-start.8 = (bf16[2,8,64,256]{3,2,1,0:T(8,128)(2,1)S(1)}, bf16[2,8,64,256]{3,2,1,0:T(8,128)(2,1)S(1)}, u32[]{:S(2)}, u32[]{:S(2)}) collective-permute-start(bf16[2,8,64,256]{3,2,1,0:T(8,128)(2,1)S(1)} %get-tuple-element.73), channel_id=1, source_target_pairs={{0,8},{1,9},{2,10},{3,11},{4,12},{5,13},{6,14},{7,15},{8,0},{9,1},... | collective-permute-start | bytes 1572872 | tf_op jit(solution)/shard_map/ppermute | solution.py:284
  57.0 14.1 %collective-permute-start.9 = (bf16[2,8,64,256]{3,2,1,0:T(8,128)(2,1)S(1)}, bf16[2,8,64,256]{3,2,1,0:T(8,128)(2,1)S(1)}, u32[]{:S(2)}, u32[]{:S(2)}) collective-permute-start(bf16[2,8,64,256]{3,2,1,0:T(8,128)(2,1)S(1)} %get-tuple-element.74), channel_id=1, source_target_pairs={{0,24},{1,25},{2,26},{3,27},{4,28},{5,29},{6,30},{7,31},{8,16},{9,... | collective-permute-start | bytes 1572872 | tf_op jit(solution)/shard_map/ppermute | solution.py:284
  71.4 14.6 %collective-permute-start.21 = (bf16[2,256,1024]{2,1,0:T(8,128)(2,1)}, bf16[2,256,1024]{2,1,0:T(8,128)(2,1)}, u32[]{:S(2)}, u32[]{:S(2)}) collective-permute-start(bf16[2,256,1024]{2,1,0:T(8,128)(2,1)} %collective-permute-done.20.refs_3_), channel_id=1, source_target_pairs={{0,32},{1,225},{2,34},{3,227},{4,36},{5,229},{6,38},{7,231},{8,40}... | collective-permute-start | bytes 3145736 | tf_op jit(solution)/shard_map/ppermute | solution.py:284
  74.0 10.7 %collective-permute-start.14 = (bf16[4,144,256]{2,1,0:T(8,128)(2,1)S(1)}, bf16[4,144,256]{2,1,0:T(8,128)(2,1)S(1)}, u32[]{:S(2)}, u32[]{:S(2)}) collective-permute-start(bf16[4,144,256]{2,1,0:T(8,128)(2,1)S(1)} %get-tuple-element.85), channel_id=1, source_target_pairs={{0,6},{1,7},{2,4},{3,5},{4,2},{5,3},{6,0},{7,1},{8,14},{9,15},{10,... | collective-permute-start | bytes 884744 | tf_op jit(solution)/shard_map/ppermute | solution.py:284
  75.6 9.1 %collective-permute-start.15 = (bf16[4,144,256]{2,1,0:T(8,128)(2,1)S(1)}, bf16[4,144,256]{2,1,0:T(8,128)(2,1)S(1)}, u32[]{:S(2)}, u32[]{:S(2)}) collective-permute-start(bf16[4,144,256]{2,1,0:T(8,128)(2,1)S(1)} %get-tuple-element.86), channel_id=1, source_target_pairs={{0,2},{1,3},{2,0},{3,1},{4,6},{5,7},{6,4},{7,5},{8,10},{9,11},{10,... | collective-permute-start | bytes 884744 | tf_op jit(solution)/shard_map/ppermute | solution.py:284
  75.7 8.7 %collective-permute-start.12 = (bf16[8,64,256]{2,1,0:T(8,128)(2,1)S(1)}, bf16[8,64,256]{2,1,0:T(8,128)(2,1)S(1)}, u32[]{:S(2)}, u32[]{:S(2)}) collective-permute-start(bf16[8,64,256]{2,1,0:T(8,128)(2,1)S(1)} %get-tuple-element.83), channel_id=1, source_target_pairs={{0,24},{1,25},{2,26},{3,27},{4,28},{5,29},{6,30},{7,31},{8,16},{9,... | collective-permute-start | bytes 786440 | tf_op jit(solution)/shard_map/ppermute | solution.py:284
  76.8 7.9 %collective-permute-start.13 = (bf16[8,64,256]{2,1,0:T(8,128)(2,1)S(1)}, bf16[8,64,256]{2,1,0:T(8,128)(2,1)S(1)}, u32[]{:S(2)}, u32[]{:S(2)}) collective-permute-start(bf16[8,64,256]{2,1,0:T(8,128)(2,1)S(1)} %get-tuple-element.84), channel_id=1, source_target_pairs={{0,8},{1,9},{2,10},{3,11},{4,12},{5,13},{6,14},{7,15},{8,0},{9,1},... | collective-permute-start | bytes 786440 | tf_op jit(solution)/shard_map/ppermute | solution.py:284
  86.0 18.8 %collective-permute-start.26 = (bf16[2,256,1024]{2,1,0:T(8,128)(2,1)}, bf16[2,256,1024]{2,1,0:T(8,128)(2,1)S(1)}, u32[]{:S(2)}, u32[]{:S(2)}) collective-permute-start(bf16[2,256,1024]{2,1,0:T(8,128)(2,1)} %collective-permute-done.21.refs_4_), channel_id=1, source_target_pairs={{0,32},{1,225},{2,34},{3,227},{4,36},{5,229},{6,38},{7,231},{8,40}... | collective-permute-start | bytes 3145736 | tf_op jit(solution)/shard_map/ppermute | solution.py:284
  89.2 7.7 %collective-permute-start.22 = (bf16[2,8,16,512]{3,2,1,0:T(8,128)(2,1)S(1)}, bf16[2,8,16,512]{3,2,1,0:T(8,128)(2,1)S(1)}, u32[]{:S(2)}, u32[]{:S(2)}) collective-permute-start(bf16[2,8,16,512]{3,2,1,0:T(8,128)(2,1)S(1)} %get-tuple-element.101), channel_id=1, source_target_pairs={{0,2},{1,3},{2,0},{3,1},{4,6},{5,7},{6,4},{7,5},{8,10},{9,11},{10,... | collective-permute-start | bytes 786440 | tf_op jit(solution)/shard_map/ppermute | solution.py:284
  89.8 8.3 %collective-permute-start.23 = (bf16[2,8,16,512]{3,2,1,0:T(8,128)(2,1)S(1)}, bf16[2,8,16,512]{3,2,1,0:T(8,128)(2,1)S(1)}, u32[]{:S(2)}, u32[]{:S(2)}) collective-permute-start(bf16[2,8,16,512]{3,2,1,0:T(8,128)(2,1)S(1)} %get-tuple-element.102), channel_id=1, source_target_pairs={{0,8},{1,9},{2,10},{3,11},{4,12},{5,13},{6,14},{7,15},{8,0},{9,1},... | collective-permute-start | bytes 786440 | tf_op jit(solution)/shard_map/ppermute | solution.py:284
  98.1 15.4 %copy-start.5 = (bf16[2,512,1024]{2,1,0:T(8,128)(2,1)S(1)}, bf16[2,512,1024]{2,1,0:T(8,128)(2,1)}, u32[]{:S(2)}) copy-start(bf16[2,512,1024]{2,1,0:T(8,128)(2,1)} %get-tuple-element.92.refs_0_) | copy-start | bytes 6291460
  98.2 6.0 %collective-permute-start.24 = (bf16[8,16,512]{2,1,0:T(8,128)(2,1)S(1)}, bf16[8,16,512]{2,1,0:T(8,128)(2,1)S(1)}, u32[]{:S(2)}, u32[]{:S(2)}) collective-permute-start(bf16[8,16,512]{2,1,0:T(8,128)(2,1)S(1)} %get-tuple-element.106), channel_id=1, source_target_pairs={{0,6},{1,7},{2,4},{3,5},{4,2},{5,3},{6,0},{7,1},{8,14},{9,15},{10,... | collective-permute-start | bytes 393224 | tf_op jit(solution)/shard_map/ppermute | solution.py:284
  98.9 5.9 %collective-permute-start.25 = (bf16[8,16,512]{2,1,0:T(8,128)(2,1)S(1)}, bf16[8,16,512]{2,1,0:T(8,128)(2,1)S(1)}, u32[]{:S(2)}, u32[]{:S(2)}) collective-permute-start(bf16[8,16,512]{2,1,0:T(8,128)(2,1)S(1)} %get-tuple-element.107), channel_id=1, source_target_pairs={{0,24},{1,25},{2,26},{3,27},{4,28},{5,29},{6,30},{7,31},{8,16},{9,... | collective-permute-start | bytes 393224 | tf_op jit(solution)/shard_map/ppermute | solution.py:284
  105.7 7.9 %collective-permute-start.27 = (bf16[2,256,1024]{2,1,0:T(8,128)(2,1)}, bf16[2,256,1024]{2,1,0:T(8,128)(2,1)}, u32[]{:S(2)}, u32[]{:S(2)}) collective-permute-start(bf16[2,256,1024]{2,1,0:T(8,128)(2,1)} %collective-permute-done.19.refs_2_), channel_id=1, source_target_pairs={{0,1},{1,0},{2,3},{3,2},{4,5},{5,4},{6,7},{7,6},{8,9},{9,8},{10,11... | collective-permute-start | bytes 3145736 | tf_op jit(solution)/shard_map/ppermute | solution.py:46
  106.8 6.7 %collective-permute-start.28 = (bf16[2,256,1024]{2,1,0:T(8,128)(2,1)}, bf16[2,256,1024]{2,1,0:T(8,128)(2,1)}, u32[]{:S(2)}, u32[]{:S(2)}) collective-permute-start(bf16[2,256,1024]{2,1,0:T(8,128)(2,1)} %collective-permute-done.20.refs_3_), channel_id=1, source_target_pairs={{0,1},{1,0},{2,3},{3,2},{4,5},{5,4},{6,7},{7,6},{8,9},{9,8},{10,11... | collective-permute-start | bytes 3145736 | tf_op jit(solution)/shard_map/ppermute | solution.py:46
  106.9 6.7 %collective-permute-start.29 = (bf16[2,256,1024]{2,1,0:T(8,128)(2,1)}, bf16[2,256,1024]{2,1,0:T(8,128)(2,1)}, u32[]{:S(2)}, u32[]{:S(2)}) collective-permute-start(bf16[2,256,1024]{2,1,0:T(8,128)(2,1)} %collective-permute-done.21.refs_4_), channel_id=1, source_target_pairs={{0,1},{1,0},{2,3},{3,2},{4,5},{5,4},{6,7},{7,6},{8,9},{9,8},{10,11... | collective-permute-start | bytes 3145736 | tf_op jit(solution)/shard_map/ppermute | solution.py:46
  107.4 17.0 %all-to-all-start = ((bf16[16,8,1024]{2,1,0:T(8,128)(2,1)}), bf16[16,8,1024]{2,1,0:T(8,128)(2,1)S(1)}, u32[]{:S(2)}, u32[]{:S(2)}) async-start(bf16[16,8,1024]{2,1,0:T(8,128)(2,1)} %bitcast.29), calls=%async_computation | async-start | bytes 524288 | tf_op jit(solution)/shard_map/all_to_all | solution.py:489

commit v5 on v4

--- a/solution.py
+++ b/solution.py
@@ -362,7 +362,7 @@
     all_stats = [stats, send(stats, flipped("y", 3))]
 
     whole_vmem = pl.BlockSpec(memory_space=pltpu.VMEM)
-    shards = lax.optimization_barrier((*shards, stats))[:-1]
+    shards = lax.optimization_barrier((*shards, all_stats[1]))[:-1]
     ordered = kernel_call(
         arrange_kernel,
         "arrange",

time: 125 us -> 123 us (0.984)
  waiting for transfers between devices: 44.4 us -> 41.8 us
    ppermute x22, waiting for transfers between devices: 40.7 us -> 39 us  [send(): return lax.ppermute(value, AXES, links)]
  transfers between devices with their start and end apart: 31 -> 31, of which waited for: 17 -> 15; matrix products, arithmetic and copies ran while one was open for 2% -> 2% of each run, Pallas kernels for 25% -> 25%
where the time goes in v5:
time: 123 us; the launch traced here: 122 us
  waiting for transfers between devices  41.8 us (34%)
  starting transfers between devices  41.5 us (34%)
  Pallas kernels  33.6 us (27%)
  local copies, waits for them, and re-layouts  2.96 us (2%)
  between operations  1.48 us (1%)
    ppermute x22, waiting for transfers between devices, send(): return lax.ppermute(value, AXES, links)  39 us
    ppermute x22, starting transfers between devices, send(): return lax.ppermute(value, AXES, links)  30.1 us
    pallas_call x1, Pallas kernels, on_device(): kernel_call(encoded_kernel, 'encoded', pltpu.HBM((keys, width), bf16), 24...  8.26 us
    pallas_call x2, Pallas kernels, grads(): kernel_call(functools.partial(grads_kernel, first_pair), 'grads', [pltpu....  8.18 us
    pallas_call x1, Pallas kernels, on_device(): kernel_call(weights_kernel, 'weights', x_outs + y_outs, 20, grid=(4,), in...  7.41 us
    ppermute x8, starting transfers between devices, swap_cores(): lax.ppermute(value, AXES, permutation(lambda z, x, y, c: (z, x, y, 1 - c)))  5.97 us
    all_to_all x1, starting transfers between devices, on_device(): lax.all_to_all(last.reshape(NZ * NC, 8, features), AXES, 0, 0, tiled=True...  5.41 us
    pallas_call x1, Pallas kernels, on_device(): kernel_call(stats_kernel, 'stats', pltpu.VMEM(stats_shape.shape, f32), 62...  5.14 us
  transfers between devices with their start and end apart: 31, of which 15 were waited for; matrix products, arithmetic and copies ran while one was open for 2% of the time, Pallas kernels for 25%

profile of v5, /device:TPU:1, one launch (start us, length us, event | category | flops | bytes accessed | tf_op | source)
XLA Modules:
  0.0 122.4 jit_solution(5869791526813961991)
XLA Ops:
  0.6 3.3 %collective-permute-start.2 = (bf16[512,2048]{1,0:T(8,128)(2,1)}, bf16[512,2048]{1,0:T(8,128)(2,1)}, u32[]{:S(2)}, u32[]{:S(2)}) collective-permute-start(bf16[512,2048]{1,0:T(8,128)(2,1)} %bitcast.55), channel_id=1, source_target_pairs={{0,1},{1,0},{2,3},{3,2},{4,5},{5,4},{6,7},{7,6},{8,9},{9,8},{10,11... | collective-permute-start | bytes 6291464 | tf_op jit(solution)/shard_map/ppermute | solution.py:46
  4.0 1.0 pad_maximum_fusion.refs_0_
  5.0 0.1 collective-permute-start.16
  5.1 1.3 %collective-permute-start.17 = (bf16[2,64,1024]{2,1,0:T(8,128)(2,1)S(1)}, bf16[2,64,1024]{2,1,0:T(8,128)(2,1)}, u32[]{:S(2)}, u32[]{:S(2)}) collective-permute-start(bf16[2,64,1024]{2,1,0:T(8,128)(2,1)S(1)} %pad_maximum_fusion.refs_0_), channel_id=1, source_target_pairs={{0,24},{1,25},{2,26},{3,27},{4,28},{5,29},{6,30},{7,31},{8,16},{9,... | collective-permute-start | bytes 786440 | tf_op jit(solution)/shard_map/ppermute | solution.py:284
  7.0 0.0 copy-start
  7.0 0.0 copy-start.2
  7.0 5.1 %stats.1.left_ref = f32[24,512]{1,0:T(8,128)S(1)} custom-call(s32[1]{0:T(128)S(6)} %copy.20.length_ref, bf16[256,1024]{1,0:T(8,128)(2,1)} %bitcast.49, bf16[512,1024]{1,0:T(8,128)(2,1)} %bitcast.43, bf16[512,1024]{1,0:T(8,128)(2,1)} %bitcast.46, bf16[256,1024]{1,0:T(8,128)(2,1)} %bitcast.52), custom_call_target="tpu_custom_call" | custom-call | tf_op jit(solution)/shard_map/stats/pallas_call | solution.py:348
  12.2 0.0 copy-start.1
  12.2 0.0 copy-start.3
  12.2 0.9 collective-permute-done.16.refs_1_
  13.1 0.7 collective-permute-start.18
  13.8 1.1 collective-permute-start
  14.9 0.9 collective-permute-done.right_ref
  15.8 1.4 %collective-permute-start.1 = (f32[24,512]{1,0:T(8,128)S(1)}, f32[24,512]{1,0:T(8,128)S(1)}, u32[]{:S(2)}, u32[]{:S(2)}) collective-permute-start(f32[24,512]{1,0:T(8,128)S(1)} %merge.2.left_ref), channel_id=1, source_target_pairs={{0,2},{1,3},{2,0},{3,1},{4,6},{5,7},{6,4},{7,5},{8,10},{9,11},{10,... | collective-permute-start | bytes 147464 | tf_op jit(solution)/shard_map/ppermute | solution.py:284
  17.2 2.0 %collective-permute-done.1.right_ref = f32[24,512]{1,0:T(8,128)S(1)} collective-permute-done((f32[24,512]{1,0:T(8,128)S(1)}, f32[24,512]{1,0:T(8,128)S(1)}, u32[]{:S(2)}, u32[]{:S(2)}) %collective-permute-start.1) | collective-permute-done | bytes 49184 | tf_op jit(solution)/shard_map/ppermute | solution.py:284
  19.2 0.0 collective-permute-done.2.other_ref
  19.2 2.8 %collective-permute-start.3 = (f32[24,512]{1,0:T(8,128)S(1)}, f32[24,512]{1,0:T(8,128)S(1)}, u32[]{:S(2)}, u32[]{:S(2)}) collective-permute-start(f32[24,512]{1,0:T(8,128)S(1)} %merge.3.refs_0_), channel_id=1, source_target_pairs={{0,6},{1,7},{2,4},{3,5},{4,2},{5,3},{6,0},{7,1},{8,14},{9,15},{10,... | collective-permute-start | bytes 147464 | tf_op jit(solution)/shard_map/ppermute | solution.py:284
  22.1 0.1 stack.71.place_ref
  22.1 0.0 collective-permute-done.17.refs_2_
  22.2 1.4 %collective-permute-done.3.refs_1_ = f32[24,512]{1,0:T(8,128)S(1)} collective-permute-done((f32[24,512]{1,0:T(8,128)S(1)}, f32[24,512]{1,0:T(8,128)S(1)}, u32[]{:S(2)}, u32[]{:S(2)}) %collective-permute-start.3) | collective-permute-done | bytes 49184 | tf_op jit(solution)/shard_map/ppermute | solution.py:284
  23.5 2.2 %arrange.1.refs_1_ = bf16[2,256,1024]{2,1,0:T(8,128)(2,1)} custom-call(s32[8]{0:T(128)S(1)} %stack.71.place_ref, bf16[2,64,1024]{2,1,0:T(8,128)(2,1)S(1)} %pad_maximum_fusion.refs_0_, bf16[2,64,1024]{2,1,0:T(8,128)(2,1)} %collective-permute-done.16.refs_1_, bf16[2,64,1024]{2,1,0:T(8,128)(2,1)} %collective-permute-done.17.refs_2_, ...), custom_call_target="tpu_custom_call" | custom-call | tf_op jit(solution)/shard_map/arrange/pallas_call | solution.py:366
  25.7 5.6 %collective-permute-start.19 = (bf16[2,256,1024]{2,1,0:T(8,128)(2,1)}, bf16[2,256,1024]{2,1,0:T(8,128)(2,1)}, u32[]{:S(2)}, u32[]{:S(2)}) collective-permute-start(bf16[2,256,1024]{2,1,0:T(8,128)(2,1)} %arrange.1.refs_1_), channel_id=1, source_target_pairs={{0,32},{1,225},{2,34},{3,227},{4,36},{5,229},{6,38},{7,231},{8,40}... | collective-permute-start | bytes 3145736 | tf_op jit(solution)/shard_map/ppermute | solution.py:284
  31.3 4.1 %grads.2 = (bf16[2,512,1024]{2,1,0:T(8,128)(2,1)}, bf16[512,512]{1,0:T(8,128)(2,1)S(1)}, bf16[512,512]{1,0:T(8,128)(2,1)S(1)}, f32[2,128,256]{2,1,0:T(8,128)S(1)}, bf16[2,128,256]{2,1,0:T(8,128)(2,1)S(1)}) custom-call(s32[1]{0:T(128)} %bitcast.13.core_ref, s32[1]{0:T(128)S(6)} %copy.20.length_ref, bf16[256,1024]{1,0:T(8,128)(2,1)S(1)} %bitcast.50, ...), custom_call_target="tpu_custom_call" | custom-call | tf_op jit(solution)/shard_map/grads/pallas_call | solution.py:394
  35.4 4.1 %grads.3 = (bf16[2,512,1024]{2,1,0:T(8,128)(2,1)}, bf16[512,512]{1,0:T(8,128)(2,1)S(1)}, bf16[512,512]{1,0:T(8,128)(2,1)S(1)}, f32[2,128,256]{2,1,0:T(8,128)S(1)}, bf16[2,128,256]{2,1,0:T(8,128)(2,1)S(1)}) custom-call(s32[1]{0:T(128)} %bitcast.13.core_ref, s32[1]{0:T(128)S(6)} %copy.20.length_ref, ...), custom_call_target="tpu_custom_call", output_to_operand_aliasing={{0}: (8, {})} | custom-call | tf_op jit(solution)/shard_map/grads/pallas_call | solution.py:394
  39.5 0.5 collective-permute-start.5
  40.0 0.0 collective-permute-start.6
  40.0 0.5 collective-permute-start.7
  40.5 1.2 collective-permute-done.6.refs_6_
  41.7 0.2 collective-permute-done.7.refs_7_
  41.9 7.4 %weights.1 = (f32[2,8,64,256]{3,2,1,0:T(8,128)S(1)}, bf16[2,8,64,256]{3,2,1,0:T(8,128)(2,1)S(1)}, f32[2,8,64,256]{3,2,1,0:T(8,128)S(1)}, bf16[2,8,64,256]{3,2,1,...) custom-call(s32[8]{0:T(128)S(1)} %stack.71.place_ref, ...), custom_call_target="tpu_custom_call" | custom-call | tf_op jit(solution)/shard_map/weights/pallas_call | solution.py:436
  49.4 2.1 %collective-permute-start.20 = (bf16[2,256,1024]{2,1,0:T(8,128)(2,1)}, bf16[2,256,1024]{2,1,0:T(8,128)(2,1)S(1)}, u32[]{:S(2)}, u32[]{:S(2)}) collective-permute-start(bf16[2,256,1024]{2,1,0:T(8,128)(2,1)} %collective-permute-done.19.refs_2_), channel_id=1, source_target_pairs={{0,32},{1,225},{2,34},{3,227},{4,36},{5,229},{6,38},{7,231},{8,40}... | collective-permute-start | bytes 3145736 | tf_op jit(solution)/shard_map/ppermute | solution.py:284
  51.5 0.1 collective-permute-start.10
  51.6 2.6 %collective-permute-start.11 = (bf16[2,4,144,256]{3,2,1,0:T(8,128)(2,1)S(1)}, bf16[2,4,144,256]{3,2,1,0:T(8,128)(2,1)S(1)}, u32[]{:S(2)}, u32[]{:S(2)}) collective-permute-start(bf16[2,4,144,256]{3,2,1,0:T(8,128)(2,1)S(1)} %get-tuple-element.76), channel_id=1, source_target_pairs={{0,6},{1,7},{2,4},{3,5},{4,2},{5,3},{6,0},{7,1},{8,14},{9,15},{10,... | collective-permute-start | bytes 1769480 | tf_op jit(solution)/shard_map/ppermute | solution.py:284
  54.2 0.9 collective-permute-start.9
  55.1 12.2 %collective-permute-done.8.refs_4_.refs_2_ = bf16[2,8,64,256]{3,2,1,0:T(8,128)(2,1)S(1)} collective-permute-done((bf16[2,8,64,256]{3,2,1,0:T(8,128)(2,1)S(1)}, bf16[2,8,64,256]{3,2,1,0:T(8,128)(2,1)S(1)}, u32[]{:S(2)}, u32[]{:S(2)}) %collective-permute-start.8) | collective-permute-done | bytes 524320 | tf_op jit(solution)/shard_map/ppermute | solution.py:284
  67.4 1.1 collective-permute-done.9.refs_5_.refs_3_
  68.5 0.3 middle.2
  68.8 2.4 %collective-permute-start.21 = (bf16[2,256,1024]{2,1,0:T(8,128)(2,1)S(1)}, bf16[2,256,1024]{2,1,0:T(8,128)(2,1)}, u32[]{:S(2)}, u32[]{:S(2)}) collective-permute-start(bf16[2,256,1024]{2,1,0:T(8,128)(2,1)S(1)} %collective-permute-done.20.refs_3_), channel_id=1, source_target_pairs={{0,32},{1,225},{2,34},{3,227},{4,36},{5,229},{6,38},{7,231},{8,40}... | collective-permute-start | bytes 3145736 | tf_op jit(solution)/shard_map/ppermute | solution.py:284
  71.1 1.6 %collective-permute-start.14 = (bf16[4,144,256]{2,1,0:T(8,128)(2,1)S(1)}, bf16[4,144,256]{2,1,0:T(8,128)(2,1)S(1)}, u32[]{:S(2)}, u32[]{:S(2)}) collective-permute-start(bf16[4,144,256]{2,1,0:T(8,128)(2,1)S(1)} %get-tuple-element.85), channel_id=1, source_target_pairs={{0,6},{1,7},{2,4},{3,5},{4,2},{5,3},{6,0},{7,1},{8,14},{9,15},{10,... | collective-permute-start | bytes 884744 | tf_op jit(solution)/shard_map/ppermute | solution.py:284
  72.7 0.9 collective-permute-start.12
  73.6 7.9 %collective-permute-done.12.refs_4_ = bf16[8,64,256]{2,1,0:T(8,128)(2,1)S(1)} collective-permute-done((bf16[8,64,256]{2,1,0:T(8,128)(2,1)S(1)}, bf16[8,64,256]{2,1,0:T(8,128)(2,1)S(1)}, u32[]{:S(2)}, u32[]{:S(2)}) %collective-permute-start.12) | collective-permute-done | bytes 262176 | tf_op jit(solution)/shard_map/ppermute | solution.py:284
  81.6 1.2 %second.1 = (f32[2,8,16,512]{3,2,1,0:T(8,128)S(1)}, bf16[2,8,16,512]{3,2,1,0:T(8,128)(2,1)S(1)}, f32[2,8,16,512]{3,2,1,0:T(8,128)S(1)}, bf16[2,8,16,512]{3,2,1,0:T(8,128)(2,1)S(1)}, f32[4,16,512]{2,1,0:T(8,128)S(1)}) custom-call(s32[8]{0:T(128)S(1)} %stack.71.place_ref, f32[2,8,64,256]{3,2,1,0:T(8,128)S(1)} %get-tuple-element.71.refs_0_, ...), custom_call_target="tpu_custom_call" | custom-call | tf_op jit(solution)/shard_map/second/pallas_call | solution.py:465
  82.8 0.1 collective-permute-done.21.refs_4_
  82.9 3.2 %collective-permute-start.26 = (bf16[2,256,1024]{2,1,0:T(8,128)(2,1)}, bf16[2,256,1024]{2,1,0:T(8,128)(2,1)S(1)}, u32[]{:S(2)}, u32[]{:S(2)}) collective-permute-start(bf16[2,256,1024]{2,1,0:T(8,128)(2,1)} %collective-permute-done.21.refs_4_), channel_id=1, source_target_pairs={{0,32},{1,225},{2,34},{3,227},{4,36},{5,229},{6,38},{7,231},{8,40}... | collective-permute-start | bytes 3145736 | tf_op jit(solution)/shard_map/ppermute | solution.py:284
  86.1 0.5 collective-permute-start.22
  86.6 0.2 collective-permute-start.23
  86.8 7.1 %collective-permute-done.22.refs_2_.refs_1_ = bf16[2,8,16,512]{3,2,1,0:T(8,128)(2,1)S(1)} collective-permute-done((bf16[2,8,16,512]{3,2,1,0:T(8,128)(2,1)S(1)}, bf16[2,8,16,512]{3,2,1,0:T(8,128)(2,1)S(1)}, u32[]{:S(2)}, u32[]{:S(2)}) %collective-permute-start.22) | collective-permute-done | bytes 262176 | tf_op jit(solution)/shard_map/ppermute | solution.py:284
  93.9 0.6 collective-permute-done.23.refs_3_.refs_4_
  94.5 0.1 middle.3
  94.6 1.3 %collective-permute-start.24 = (bf16[8,16,512]{2,1,0:T(8,128)(2,1)S(1)}, bf16[8,16,512]{2,1,0:T(8,128)(2,1)S(1)}, u32[]{:S(2)}, u32[]{:S(2)}) collective-permute-start(bf16[8,16,512]{2,1,0:T(8,128)(2,1)S(1)} %get-tuple-element.106), channel_id=1, source_target_pairs={{0,6},{1,7},{2,4},{3,5},{4,2},{5,3},{6,0},{7,1},{8,14},{9,15},{10,... | collective-permute-start | bytes 393224 | tf_op jit(solution)/shard_map/ppermute | solution.py:284
  95.9 1.3 %collective-permute-start.25 = (bf16[8,16,512]{2,1,0:T(8,128)(2,1)S(1)}, bf16[8,16,512]{2,1,0:T(8,128)(2,1)S(1)}, u32[]{:S(2)}, u32[]{:S(2)}) collective-permute-start(bf16[8,16,512]{2,1,0:T(8,128)(2,1)S(1)} %get-tuple-element.107), channel_id=1, source_target_pairs={{0,24},{1,25},{2,26},{3,27},{4,28},{5,29},{6,30},{7,31},{8,16},{9,... | collective-permute-start | bytes 393224 | tf_op jit(solution)/shard_map/ppermute | solution.py:284
  97.2 2.8 %collective-permute-done.24.refs_2_ = bf16[8,16,512]{2,1,0:T(8,128)(2,1)S(1)} collective-permute-done((bf16[8,16,512]{2,1,0:T(8,128)(2,1)S(1)}, bf16[8,16,512]{2,1,0:T(8,128)(2,1)S(1)}, u32[]{:S(2)}, u32[]{:S(2)}) %collective-permute-start.24) | collective-permute-done | bytes 131104 | tf_op jit(solution)/shard_map/ppermute | solution.py:284
  100.0 1.9 %collective-permute-done.25.refs_5_ = bf16[8,16,512]{2,1,0:T(8,128)(2,1)S(1)} collective-permute-done((bf16[8,16,512]{2,1,0:T(8,128)(2,1)S(1)}, bf16[8,16,512]{2,1,0:T(8,128)(2,1)S(1)}, u32[]{:S(2)}, u32[]{:S(2)}) %collective-permute-start.25) | collective-permute-done | bytes 131104 | tf_op jit(solution)/shard_map/ppermute | solution.py:284
  101.9 0.9 last.1
  102.8 0.2 copy-done.6
  103.0 1.1 collective-permute-start.27
  104.1 0.5 collective-permute-start.29
  104.6 5.4 %all-to-all-start = ((bf16[16,8,1024]{2,1,0:T(8,128)(2,1)}), bf16[16,8,1024]{2,1,0:T(8,128)(2,1)S(1)}, u32[]{:S(2)}, u32[]{:S(2)}) async-start(bf16[16,8,1024]{2,1,0:T(8,128)(2,1)} %bitcast.29), calls=%async_computation | async-start | bytes 524288 | tf_op jit(solution)/shard_map/all_to_all | solution.py:489
  110.0 0.1 stack.80.order_ref
  110.1 0.7 copy.15
  110.9 1.2 copy-done.7
  112.1 8.3 %encoded.1 = bf16[512,2048]{1,0:T(8,128)(2,1)} custom-call(s32[8]{0:T(128)S(1)} %stack.80.order_ref, bf16[2,512,1024]{2,1,0:T(8,128)(2,1)S(1)} %copy-done.5, bf16[2,256,1024]{2,1,0:T(8,128)(2,1)} %arrange.1.refs_1_, bf16[2,256,1024]{2,1,0:T(8,128)(2,1)} %collective-permute-done.19.refs_2_, bf16[2,256,1024]{2,1,0:T(8,128)(2,1)S(1)} %collective-permute-done.20.refs_3_, ...), custom_call_target="tpu_custom_call" | custom-call | flops 4294967296 | bytes 14680064 | tf_op jit(solution)/shard_map/encoded/pallas_call | solution.py:501
  120.4 1.3 %all-to-all-done = bf16[16,8,1024]{2,1,0:T(8,128)(2,1)S(1)} async-done(((bf16[16,8,1024]{2,1,0:T(8,128)(2,1)}), bf16[16,8,1024]{2,1,0:T(8,128)(2,1)S(1)}, u32[]{:S(2)}, u32[]{:S(2)}) %all-to-all-start) | async-done | bytes 262176 | tf_op jit(solution)/shard_map/all_to_all | solution.py:489
  121.8 0.6 slice_bitcast_fusion
  (34 shorter events, 0.2 us)
Async XLA Ops:
  0.6 18.6 %collective-permute-start.2 = (bf16[512,2048]{1,0:T(8,128)(2,1)}, bf16[512,2048]{1,0:T(8,128)(2,1)}, u32[]{:S(2)}, u32[]{:S(2)}) collective-permute-start(bf16[512,2048]{1,0:T(8,128)(2,1)} %bitcast.55), channel_id=1, source_target_pairs={{0,1},{1,0},{2,3},{3,2},{4,5},{5,4},{6,7},{7,6},{8,9},{9,8},{10,11... | collective-permute-start | bytes 6291464 | tf_op jit(solution)/shard_map/ppermute | solution.py:46
  5.0 8.1 %collective-permute-start.16 = (bf16[2,64,1024]{2,1,0:T(8,128)(2,1)S(1)}, bf16[2,64,1024]{2,1,0:T(8,128)(2,1)}, u32[]{:S(2)}, u32[]{:S(2)}) collective-permute-start(bf16[2,64,1024]{2,1,0:T(8,128)(2,1)S(1)} %pad_maximum_fusion.refs_0_), channel_id=1, source_target_pairs={{0,8},{1,9},{2,10},{3,11},{4,12},{5,13},{6,14},{7,15},{8,0},{9,1},... | collective-permute-start | bytes 786440 | tf_op jit(solution)/shard_map/ppermute | solution.py:284
  5.1 17.1 %collective-permute-start.17 = (bf16[2,64,1024]{2,1,0:T(8,128)(2,1)S(1)}, bf16[2,64,1024]{2,1,0:T(8,128)(2,1)}, u32[]{:S(2)}, u32[]{:S(2)}) collective-permute-start(bf16[2,64,1024]{2,1,0:T(8,128)(2,1)S(1)} %pad_maximum_fusion.refs_0_), channel_id=1, source_target_pairs={{0,24},{1,25},{2,26},{3,27},{4,28},{5,29},{6,30},{7,31},{8,16},{9,... | collective-permute-start | bytes 786440 | tf_op jit(solution)/shard_map/ppermute | solution.py:284
  7.0 24.3 %copy-start = (bf16[1,512,1024]{2,1,0:T(8,128)(2,1)S(1)}, bf16[1,512,1024]{2,1,0:T(8,128)(2,1)}, u32[]{:S(2)}) copy-start(bf16[1,512,1024]{2,1,0:T(8,128)(2,1)} %param.9) | copy-start | bytes 3145732
  7.0 24.3 %copy-start.2 = (bf16[1,256,1024]{2,1,0:T(8,128)(2,1)S(1)}, bf16[1,256,1024]{2,1,0:T(8,128)(2,1)}, u32[]{:S(2)}) copy-start(bf16[1,256,1024]{2,1,0:T(8,128)(2,1)} %param.8) | copy-start | bytes 1572868
  12.2 19.1 %copy-start.1 = (bf16[1,512,1024]{2,1,0:T(8,128)(2,1)S(1)}, bf16[1,512,1024]{2,1,0:T(8,128)(2,1)}, u32[]{:S(2)}) copy-start(bf16[1,512,1024]{2,1,0:T(8,128)(2,1)} %param.10) | copy-start | bytes 3145732
  12.2 19.1 %copy-start.3 = (bf16[1,256,1024]{2,1,0:T(8,128)(2,1)S(1)}, bf16[1,256,1024]{2,1,0:T(8,128)(2,1)}, u32[]{:S(2)}) copy-start(bf16[1,256,1024]{2,1,0:T(8,128)(2,1)} %param.14) | copy-start | bytes 1572868
  13.1 9.1 %collective-permute-start.18 = (bf16[2,64,1024]{2,1,0:T(8,128)(2,1)}, bf16[2,64,1024]{2,1,0:T(8,128)(2,1)}, u32[]{:S(2)}, u32[]{:S(2)}) collective-permute-start(bf16[2,64,1024]{2,1,0:T(8,128)(2,1)} %collective-permute-done.16.refs_1_), channel_id=1, source_target_pairs={{0,24},{1,25},{2,26},{3,27},{4,28},{5,29},{6,30},{7,31},{8,16},{9,... | collective-permute-start | bytes 786440 | tf_op jit(solution)/shard_map/ppermute | solution.py:284
  13.8 2.0 %collective-permute-start = (f32[24,512]{1,0:T(8,128)S(1)}, f32[24,512]{1,0:T(8,128)S(1)}, u32[]{:S(2)}, u32[]{:S(2)}) collective-permute-start(f32[24,512]{1,0:T(8,128)S(1)} %stats.1.left_ref), channel_id=1, source_target_pairs={{0,1},{1,0},{2,3},{3,2},{4,5},{5,4},{6,7},{7,6},{8,9},{9,8},{10,11... | collective-permute-start | bytes 147464 | tf_op jit(solution)/shard_map/ppermute | solution.py:284
  15.8 3.4 %collective-permute-start.1 = (f32[24,512]{1,0:T(8,128)S(1)}, f32[24,512]{1,0:T(8,128)S(1)}, u32[]{:S(2)}, u32[]{:S(2)}) collective-permute-start(f32[24,512]{1,0:T(8,128)S(1)} %merge.2.left_ref), channel_id=1, source_target_pairs={{0,2},{1,3},{2,0},{3,1},{4,6},{5,7},{6,4},{7,5},{8,10},{9,11},{10,... | collective-permute-start | bytes 147464 | tf_op jit(solution)/shard_map/ppermute | solution.py:284
  19.2 4.3 %collective-permute-start.3 = (f32[24,512]{1,0:T(8,128)S(1)}, f32[24,512]{1,0:T(8,128)S(1)}, u32[]{:S(2)}, u32[]{:S(2)}) collective-permute-start(f32[24,512]{1,0:T(8,128)S(1)} %merge.3.refs_0_), channel_id=1, source_target_pairs={{0,6},{1,7},{2,4},{3,5},{4,2},{5,3},{6,0},{7,1},{8,14},{9,15},{10,... | collective-permute-start | bytes 147464 | tf_op jit(solution)/shard_map/ppermute | solution.py:284
  25.7 23.6 %collective-permute-start.19 = (bf16[2,256,1024]{2,1,0:T(8,128)(2,1)}, bf16[2,256,1024]{2,1,0:T(8,128)(2,1)}, u32[]{:S(2)}, u32[]{:S(2)}) collective-permute-start(bf16[2,256,1024]{2,1,0:T(8,128)(2,1)} %arrange.1.refs_1_), channel_id=1, source_target_pairs={{0,32},{1,225},{2,34},{3,227},{4,36},{5,229},{6,38},{7,231},{8,40}... | collective-permute-start | bytes 3145736 | tf_op jit(solution)/shard_map/ppermute | solution.py:284
  35.4 6.5 %collective-permute-start.4 = (bf16[512,512]{1,0:T(8,128)(2,1)S(1)}, bf16[512,512]{1,0:T(8,128)(2,1)S(1)}, u32[]{:S(2)}, u32[]{:S(2)}) collective-permute-start(bf16[512,512]{1,0:T(8,128)(2,1)S(1)} %get-tuple-element.65), channel_id=1, source_target_pairs={{0,1},{1,0},{2,3},{3,2},{4,5},{5,4},{6,7},{7,6},{8,9},{9,8},{10,11... | collective-permute-start | bytes 1572872 | tf_op jit(solution)/shard_map/ppermute | solution.py:46
  35.4 6.5 %copy-start.4 = (bf16[1,512,2048]{2,1,0:T(8,128)(2,1)S(1)}, bf16[1,512,2048]{2,1,0:T(8,128)(2,1)}, u32[]{:S(2)}) copy-start(bf16[1,512,2048]{2,1,0:T(8,128)(2,1)} %param.11) | copy-start | bytes 6291460
  39.5 2.4 %collective-permute-start.5 = (bf16[512,512]{1,0:T(8,128)(2,1)S(1)}, bf16[512,512]{1,0:T(8,128)(2,1)S(1)}, u32[]{:S(2)}, u32[]{:S(2)}) collective-permute-start(bf16[512,512]{1,0:T(8,128)(2,1)S(1)} %get-tuple-element.66), channel_id=1, source_target_pairs={{0,1},{1,0},{2,3},{3,2},{4,5},{5,4},{6,7},{7,6},{8,9},{9,8},{10,11... | collective-permute-start | bytes 1572872 | tf_op jit(solution)/shard_map/ppermute | solution.py:46
  40.0 1.7 %collective-permute-start.6 = (bf16[2,128,256]{2,1,0:T(8,128)(2,1)S(1)}, bf16[2,128,256]{2,1,0:T(8,128)(2,1)S(1)}, u32[]{:S(2)}, u32[]{:S(2)}) collective-permute-start(bf16[2,128,256]{2,1,0:T(8,128)(2,1)S(1)} %get-tuple-element.69), channel_id=1, source_target_pairs={{0,1},{1,0},{2,3},{3,2},{4,5},{5,4},{6,7},{7,6},{8,9},{9,8},{10,11... | collective-permute-start | bytes 393224 | tf_op jit(solution)/shard_map/ppermute | solution.py:46
  40.0 1.9 %collective-permute-start.7 = (bf16[2,128,256]{2,1,0:T(8,128)(2,1)S(1)}, bf16[2,128,256]{2,1,0:T(8,128)(2,1)S(1)}, u32[]{:S(2)}, u32[]{:S(2)}) collective-permute-start(bf16[2,128,256]{2,1,0:T(8,128)(2,1)S(1)} %get-tuple-element.70), channel_id=1, source_target_pairs={{0,1},{1,0},{2,3},{3,2},{4,5},{5,4},{6,7},{7,6},{8,9},{9,8},{10,11... | collective-permute-start | bytes 393224 | tf_op jit(solution)/shard_map/ppermute | solution.py:46
  49.4 19.4 %collective-permute-start.20 = (bf16[2,256,1024]{2,1,0:T(8,128)(2,1)}, bf16[2,256,1024]{2,1,0:T(8,128)(2,1)S(1)}, u32[]{:S(2)}, u32[]{:S(2)}) collective-permute-start(bf16[2,256,1024]{2,1,0:T(8,128)(2,1)} %collective-permute-done.19.refs_2_), channel_id=1, source_target_pairs={{0,32},{1,225},{2,34},{3,227},{4,36},{5,229},{6,38},{7,231},{8,40}... | collective-permute-start | bytes 3145736 | tf_op jit(solution)/shard_map/ppermute | solution.py:284
  51.5 17.0 %collective-permute-start.10 = (bf16[2,4,144,256]{3,2,1,0:T(8,128)(2,1)S(1)}, bf16[2,4,144,256]{3,2,1,0:T(8,128)(2,1)S(1)}, u32[]{:S(2)}, u32[]{:S(2)}) collective-permute-start(bf16[2,4,144,256]{3,2,1,0:T(8,128)(2,1)S(1)} %get-tuple-element.75), channel_id=1, source_target_pairs={{0,2},{1,3},{2,0},{3,1},{4,6},{5,7},{6,4},{7,5},{8,10},{9,11},{10,... | collective-permute-start | bytes 1769480 | tf_op jit(solution)/shard_map/ppermute | solution.py:284
  51.6 16.9 %collective-permute-start.11 = (bf16[2,4,144,256]{3,2,1,0:T(8,128)(2,1)S(1)}, bf16[2,4,144,256]{3,2,1,0:T(8,128)(2,1)S(1)}, u32[]{:S(2)}, u32[]{:S(2)}) collective-permute-start(bf16[2,4,144,256]{3,2,1,0:T(8,128)(2,1)S(1)} %get-tuple-element.76), channel_id=1, source_target_pairs={{0,6},{1,7},{2,4},{3,5},{4,2},{5,3},{6,0},{7,1},{8,14},{9,15},{10,... | collective-permute-start | bytes 1769480 | tf_op jit(solution)/shard_map/ppermute | solution.py:284
  54.2 13.1 %collective-permute-start.8 = (bf16[2,8,64,256]{3,2,1,0:T(8,128)(2,1)S(1)}, bf16[2,8,64,256]{3,2,1,0:T(8,128)(2,1)S(1)}, u32[]{:S(2)}, u32[]{:S(2)}) collective-permute-start(bf16[2,8,64,256]{3,2,1,0:T(8,128)(2,1)S(1)} %get-tuple-element.73), channel_id=1, source_target_pairs={{0,8},{1,9},{2,10},{3,11},{4,12},{5,13},{6,14},{7,15},{8,0},{9,1},... | collective-permute-start | bytes 1572872 | tf_op jit(solution)/shard_map/ppermute | solution.py:284
  54.2 14.3 %collective-permute-start.9 = (bf16[2,8,64,256]{3,2,1,0:T(8,128)(2,1)S(1)}, bf16[2,8,64,256]{3,2,1,0:T(8,128)(2,1)S(1)}, u32[]{:S(2)}, u32[]{:S(2)}) collective-permute-start(bf16[2,8,64,256]{3,2,1,0:T(8,128)(2,1)S(1)} %get-tuple-element.74), channel_id=1, source_target_pairs={{0,24},{1,25},{2,26},{3,27},{4,28},{5,29},{6,30},{7,31},{8,16},{9,... | collective-permute-start | bytes 1572872 | tf_op jit(solution)/shard_map/ppermute | solution.py:284
  68.8 14.1 %collective-permute-start.21 = (bf16[2,256,1024]{2,1,0:T(8,128)(2,1)S(1)}, bf16[2,256,1024]{2,1,0:T(8,128)(2,1)}, u32[]{:S(2)}, u32[]{:S(2)}) collective-permute-start(bf16[2,256,1024]{2,1,0:T(8,128)(2,1)S(1)} %collective-permute-done.20.refs_3_), channel_id=1, source_target_pairs={{0,32},{1,225},{2,34},{3,227},{4,36},{5,229},{6,38},{7,231},{8,40}... | collective-permute-start | bytes 3145736 | tf_op jit(solution)/shard_map/ppermute | solution.py:284
  71.1 10.4 %collective-permute-start.14 = (bf16[4,144,256]{2,1,0:T(8,128)(2,1)S(1)}, bf16[4,144,256]{2,1,0:T(8,128)(2,1)S(1)}, u32[]{:S(2)}, u32[]{:S(2)}) collective-permute-start(bf16[4,144,256]{2,1,0:T(8,128)(2,1)S(1)} %get-tuple-element.85), channel_id=1, source_target_pairs={{0,6},{1,7},{2,4},{3,5},{4,2},{5,3},{6,0},{7,1},{8,14},{9,15},{10,... | collective-permute-start | bytes 884744 | tf_op jit(solution)/shard_map/ppermute | solution.py:284
  72.7 8.8 %collective-permute-start.15 = (bf16[4,144,256]{2,1,0:T(8,128)(2,1)S(1)}, bf16[4,144,256]{2,1,0:T(8,128)(2,1)S(1)}, u32[]{:S(2)}, u32[]{:S(2)}) collective-permute-start(bf16[4,144,256]{2,1,0:T(8,128)(2,1)S(1)} %get-tuple-element.86), channel_id=1, source_target_pairs={{0,2},{1,3},{2,0},{3,1},{4,6},{5,7},{6,4},{7,5},{8,10},{9,11},{10,... | collective-permute-start | bytes 884744 | tf_op jit(solution)/shard_map/ppermute | solution.py:284
  72.7 8.8 %collective-permute-start.12 = (bf16[8,64,256]{2,1,0:T(8,128)(2,1)S(1)}, bf16[8,64,256]{2,1,0:T(8,128)(2,1)S(1)}, u32[]{:S(2)}, u32[]{:S(2)}) collective-permute-start(bf16[8,64,256]{2,1,0:T(8,128)(2,1)S(1)} %get-tuple-element.83), channel_id=1, source_target_pairs={{0,24},{1,25},{2,26},{3,27},{4,28},{5,29},{6,30},{7,31},{8,16},{9,... | collective-permute-start | bytes 786440 | tf_op jit(solution)/shard_map/ppermute | solution.py:284
  73.6 7.9 %collective-permute-start.13 = (bf16[8,64,256]{2,1,0:T(8,128)(2,1)S(1)}, bf16[8,64,256]{2,1,0:T(8,128)(2,1)S(1)}, u32[]{:S(2)}, u32[]{:S(2)}) collective-permute-start(bf16[8,64,256]{2,1,0:T(8,128)(2,1)S(1)} %get-tuple-element.84), channel_id=1, source_target_pairs={{0,8},{1,9},{2,10},{3,11},{4,12},{5,13},{6,14},{7,15},{8,0},{9,1},... | collective-permute-start | bytes 786440 | tf_op jit(solution)/shard_map/ppermute | solution.py:284
  82.9 19.0 %collective-permute-start.26 = (bf16[2,256,1024]{2,1,0:T(8,128)(2,1)}, bf16[2,256,1024]{2,1,0:T(8,128)(2,1)S(1)}, u32[]{:S(2)}, u32[]{:S(2)}) collective-permute-start(bf16[2,256,1024]{2,1,0:T(8,128)(2,1)} %collective-permute-done.21.refs_4_), channel_id=1, source_target_pairs={{0,32},{1,225},{2,34},{3,227},{4,36},{5,229},{6,38},{7,231},{8,40}... | collective-permute-start | bytes 3145736 | tf_op jit(solution)/shard_map/ppermute | solution.py:284
  86.1 7.8 %collective-permute-start.22 = (bf16[2,8,16,512]{3,2,1,0:T(8,128)(2,1)S(1)}, bf16[2,8,16,512]{3,2,1,0:T(8,128)(2,1)S(1)}, u32[]{:S(2)}, u32[]{:S(2)}) collective-permute-start(bf16[2,8,16,512]{3,2,1,0:T(8,128)(2,1)S(1)} %get-tuple-element.101), channel_id=1, source_target_pairs={{0,2},{1,3},{2,0},{3,1},{4,6},{5,7},{6,4},{7,5},{8,10},{9,11},{10,... | collective-permute-start | bytes 786440 | tf_op jit(solution)/shard_map/ppermute | solution.py:284
  86.6 7.9 %collective-permute-start.23 = (bf16[2,8,16,512]{3,2,1,0:T(8,128)(2,1)S(1)}, bf16[2,8,16,512]{3,2,1,0:T(8,128)(2,1)S(1)}, u32[]{:S(2)}, u32[]{:S(2)}) collective-permute-start(bf16[2,8,16,512]{3,2,1,0:T(8,128)(2,1)S(1)} %get-tuple-element.102), channel_id=1, source_target_pairs={{0,8},{1,9},{2,10},{3,11},{4,12},{5,13},{6,14},{7,15},{8,0},{9,1},... | collective-permute-start | bytes 786440 | tf_op jit(solution)/shard_map/ppermute | solution.py:284
  94.5 16.4 %copy-start.5 = (bf16[2,512,1024]{2,1,0:T(8,128)(2,1)S(1)}, bf16[2,512,1024]{2,1,0:T(8,128)(2,1)}, u32[]{:S(2)}) copy-start(bf16[2,512,1024]{2,1,0:T(8,128)(2,1)} %get-tuple-element.92.refs_0_) | copy-start | bytes 6291460
  94.6 5.4 %collective-permute-start.24 = (bf16[8,16,512]{2,1,0:T(8,128)(2,1)S(1)}, bf16[8,16,512]{2,1,0:T(8,128)(2,1)S(1)}, u32[]{:S(2)}, u32[]{:S(2)}) collective-permute-start(bf16[8,16,512]{2,1,0:T(8,128)(2,1)S(1)} %get-tuple-element.106), channel_id=1, source_target_pairs={{0,6},{1,7},{2,4},{3,5},{4,2},{5,3},{6,0},{7,1},{8,14},{9,15},{10,... | collective-permute-start | bytes 393224 | tf_op jit(solution)/shard_map/ppermute | solution.py:284
  95.9 6.0 %collective-permute-start.25 = (bf16[8,16,512]{2,1,0:T(8,128)(2,1)S(1)}, bf16[8,16,512]{2,1,0:T(8,128)(2,1)S(1)}, u32[]{:S(2)}, u32[]{:S(2)}) collective-permute-start(bf16[8,16,512]{2,1,0:T(8,128)(2,1)S(1)} %get-tuple-element.107), channel_id=1, source_target_pairs={{0,24},{1,25},{2,26},{3,27},{4,28},{5,29},{6,30},{7,31},{8,16},{9,... | collective-permute-start | bytes 393224 | tf_op jit(solution)/shard_map/ppermute | solution.py:284
  101.9 1.1 copy-start.6
  103.0 7.9 %collective-permute-start.27 = (bf16[2,256,1024]{2,1,0:T(8,128)(2,1)}, bf16[2,256,1024]{2,1,0:T(8,128)(2,1)}, u32[]{:S(2)}, u32[]{:S(2)}) collective-permute-start(bf16[2,256,1024]{2,1,0:T(8,128)(2,1)} %collective-permute-done.19.refs_2_), channel_id=1, source_target_pairs={{0,1},{1,0},{2,3},{3,2},{4,5},{5,4},{6,7},{7,6},{8,9},{9,8},{10,11... | collective-permute-start | bytes 3145736 | tf_op jit(solution)/shard_map/ppermute | solution.py:46
  104.1 6.8 %collective-permute-start.28 = (bf16[2,256,1024]{2,1,0:T(8,128)(2,1)S(1)}, bf16[2,256,1024]{2,1,0:T(8,128)(2,1)}, u32[]{:S(2)}, u32[]{:S(2)}) collective-permute-start(bf16[2,256,1024]{2,1,0:T(8,128)(2,1)S(1)} %collective-permute-done.20.refs_3_), channel_id=1, source_target_pairs={{0,1},{1,0},{2,3},{3,2},{4,5},{5,4},{6,7},{7,6},{8,9},{9,8},{10,11... | collective-permute-start | bytes 3145736 | tf_op jit(solution)/shard_map/ppermute | solution.py:46
  104.1 6.8 %collective-permute-start.29 = (bf16[2,256,1024]{2,1,0:T(8,128)(2,1)}, bf16[2,256,1024]{2,1,0:T(8,128)(2,1)}, u32[]{:S(2)}, u32[]{:S(2)}) collective-permute-start(bf16[2,256,1024]{2,1,0:T(8,128)(2,1)} %collective-permute-done.21.refs_4_), channel_id=1, source_target_pairs={{0,1},{1,0},{2,3},{3,2},{4,5},{5,4},{6,7},{7,6},{8,9},{9,8},{10,11... | collective-permute-start | bytes 3145736 | tf_op jit(solution)/shard_map/ppermute | solution.py:46
  104.6 17.1 %all-to-all-start = ((bf16[16,8,1024]{2,1,0:T(8,128)(2,1)}), bf16[16,8,1024]{2,1,0:T(8,128)(2,1)S(1)}, u32[]{:S(2)}, u32[]{:S(2)}) async-start(bf16[16,8,1024]{2,1,0:T(8,128)(2,1)} %bitcast.29), calls=%async_computation | async-start | bytes 524288 | tf_op jit(solution)/shard_map/all_to_all | solution.py:489
  110.9 1.2 %copy-start.7 = (bf16[2,256,1024]{2,1,0:T(8,128)(2,1)S(1)}, bf16[2,256,1024]{2,1,0:T(8,128)(2,1)}, u32[]{:S(2)}) copy-start(bf16[2,256,1024]{2,1,0:T(8,128)(2,1)} %copy-done.6) | copy-start | bytes 3145732

commit v6 on v5

--- a/solution.py
+++ b/solution.py
@@ -355,24 +355,11 @@
         out_specs=pl.BlockSpec(stats_shape.shape, lambda p: (0, 0)),
     )(lengths, queries, key_rows, value_rows, grad_out)
 
+    stats = kernel_call(merge_kernel, "merge", stats_shape)(stats, send(stats, along("core", 1)))
     shards.append(send(tie(shards[1], stats), flipped("x", 3)))
-    stats = kernel_call(merge_kernel, "merge", stats_shape)(stats, send(stats, along("core", 1)))
     met, encoded_other = lax.optimization_barrier((send(stats, flipped("y", 1)), swap_cores(encoded)))
     stats = kernel_call(merge_kernel, "merge", stats_shape)(stats, met)
     all_stats = [stats, send(stats, flipped("y", 3))]
-
-    whole_vmem = pl.BlockSpec(memory_space=pltpu.VMEM)
-    shards = lax.optimization_barrier((*shards, all_stats[1]))[:-1]
-    ordered = kernel_call(
-        arrange_kernel,
-        "arrange",
-        like((2, NX * shard.shape[1], features), bf16),
-        in_specs=[smem] + [whole_vmem] * NX,
-        out_specs=whole_vmem,
-    )(place, *shards)
-
-    around = permutation(lambda z, x, y, c: (z + 1 - 2 * c, x, y, c))
-    pieces = [ordered, send(ordered, around)]
 
     def grads(first_pair, joint):
         def rows(p):
@@ -410,6 +397,19 @@
     joint, mine_a, sent_a, query_kept_a, query_sent_a = grads(0, None)
     received_a = swap_cores(sent_a)
 
+    whole_vmem = pl.BlockSpec(memory_space=pltpu.VMEM)
+    shards = lax.optimization_barrier((*shards, mine_a))[:-1]
+    ordered = kernel_call(
+        arrange_kernel,
+        "arrange",
+        like((2, NX * shard.shape[1], features), bf16),
+        in_specs=[smem] + [whole_vmem] * NX,
+        out_specs=whole_vmem,
+    )(place, *shards)
+
+    around = permutation(lambda z, x, y, c: (z + 1 - 2 * c, x, y, c))
+    pieces = [ordered, send(ordered, around)]
+
     joint, mine_b, sent_b, query_kept_b, query_sent_b = grads(pairs // 2, joint)
     received_b = swap_cores(sent_b)
     query_received = [swap_cores(query_sent_a), swap_cores(query_sent_b)]

time: 123 us -> 123 us (level)
  local copies, waits for them, and re-layouts: 2.96 us -> 5.25 us
  waiting for transfers between devices: 41.8 us -> 40.4 us
    unnamed x17 -> x25, local copies, waits for them, and re-layouts: 2.15 us -> 4.44 us
    ppermute x22, waiting for transfers between devices: 39 us -> 37.7 us  [send(): return lax.ppermute(value, AXES, links)]
    ppermute x8, starting transfers between devices: 5.97 us -> 7.24 us  [swap_cores(): lax.ppermute(value, AXES, permutation(lambda z, x, y, c: (z, x, y, 1 - c)))]
    ppermute x22, starting transfers between devices: 30.1 us -> 28.9 us  [send(): return lax.ppermute(value, AXES, links)]
  transfers between devices with their start and end apart: 31 -> 31, of which waited for: 15 -> 13; matrix products, arithmetic and copies ran while one was open for 2% -> 2% of each run, Pallas kernels for 25% -> 25%
where the time goes in v6:
time: 123 us
  starting transfers between devices  42 us (34%)
  waiting for transfers between devices  40.4 us (33%)
  Pallas kernels  32.4 us (26%)
  local copies, waits for them, and re-layouts  5.25 us (4%)
  between operations  1.49 us (1%)
    ppermute x22, waiting for transfers between devices, send(): return lax.ppermute(value, AXES, links)  37.7 us
    ppermute x22, starting transfers between devices, send(): return lax.ppermute(value, AXES, links)  28.9 us
    pallas_call x1, Pallas kernels, on_device(): kernel_call(encoded_kernel, 'encoded', pltpu.HBM((keys, width), bf16), 24...  8.26 us
    pallas_call x2, Pallas kernels, grads(): kernel_call(functools.partial(grads_kernel, first_pair), 'grads', [pltpu....  8.19 us
    pallas_call x1, Pallas kernels, on_device(): kernel_call(weights_kernel, 'weights', x_outs + y_outs, 20, grid=(4,), in...  7.4 us
    ppermute x8, starting transfers between devices, swap_cores(): lax.ppermute(value, AXES, permutation(lambda z, x, y, c: (z, x, y, 1 - c)))  7.24 us
    all_to_all x1, starting transfers between devices, on_device(): lax.all_to_all(last.reshape(NZ * NC, 8, features), AXES, 0, 0, tiled=True...  5.87 us
    pallas_call x1, Pallas kernels, on_device(): kernel_call(stats_kernel, 'stats', pltpu.VMEM(stats_shape.shape, f32), 62...  5.03 us
  transfers between devices with their start and end apart: 31, of which 13 were waited for; matrix products, arithmetic and copies ran while one was open for 2% of the time, Pallas kernels for 25%

profile of v6, /device:TPU:1, one launch (start us, length us, event | category | flops | bytes accessed | tf_op | source)
XLA Modules:
  0.0 122.6 jit_solution(15181083089085419212)
XLA Ops:
  0.6 0.0 copy-start.3
  0.6 0.0 copy-start
  0.7 3.3 %collective-permute-start.2 = (bf16[512,2048]{1,0:T(8,128)(2,1)}, bf16[512,2048]{1,0:T(8,128)(2,1)}, u32[]{:S(2)}, u32[]{:S(2)}) collective-permute-start(bf16[512,2048]{1,0:T(8,128)(2,1)} %bitcast.55), channel_id=1, source_target_pairs={{0,1},{1,0},{2,3},{3,2},{4,5},{5,4},{6,7},{7,6},{8,9},{9,8},{10,11... | collective-permute-start | bytes 6291464 | tf_op jit(solution)/shard_map/ppermute | solution.py:46
  4.0 1.0 pad_maximum_fusion.refs_0_
  5.0 0.1 collective-permute-start.16
  5.7 5.0 %stats.1.left_ref = f32[24,512]{1,0:T(8,128)S(1)} custom-call(s32[1]{0:T(128)S(6)} %copy.20.length_ref, bf16[256,1024]{1,0:T(8,128)(2,1)} %bitcast.49, bf16[512,1024]{1,0:T(8,128)(2,1)} %bitcast.43, bf16[512,1024]{1,0:T(8,128)(2,1)} %bitcast.46, bf16[256,1024]{1,0:T(8,128)(2,1)} %bitcast.52), custom_call_target="tpu_custom_call" | custom-call | tf_op jit(solution)/shard_map/stats/pallas_call | solution.py:348
  10.8 0.2 collective-permute-start
  11.0 1.6 %collective-permute-start.17 = (bf16[2,64,1024]{2,1,0:T(8,128)(2,1)S(1)}, bf16[2,64,1024]{2,1,0:T(8,128)(2,1)S(1)}, u32[]{:S(2)}, u32[]{:S(2)}) collective-permute-start(bf16[2,64,1024]{2,1,0:T(8,128)(2,1)S(1)} %pad_maximum_fusion.refs_0_), channel_id=1, source_target_pairs={{0,24},{1,25},{2,26},{3,27},{4,28},{5,29},{6,30},{7,31},{8,16},{9,... | collective-permute-start | bytes 786440 | tf_op jit(solution)/shard_map/ppermute | solution.py:284
  12.5 0.0 collective-permute-done.right_ref
  12.6 0.5 collective-permute-done.16.refs_1_
  13.1 0.7 collective-permute-start.18
  13.8 1.3 %collective-permute-start.1 = (f32[24,512]{1,0:T(8,128)S(1)}, f32[24,512]{1,0:T(8,128)S(1)}, u32[]{:S(2)}, u32[]{:S(2)}) collective-permute-start(f32[24,512]{1,0:T(8,128)S(1)} %merge.2.left_ref), channel_id=1, source_target_pairs={{0,2},{1,3},{2,0},{3,1},{4,6},{5,7},{6,4},{7,5},{8,10},{9,11},{10,... | collective-permute-start | bytes 147464 | tf_op jit(solution)/shard_map/ppermute | solution.py:284
  15.1 1.9 %collective-permute-done.1.right_ref = f32[24,512]{1,0:T(8,128)S(1)} collective-permute-done((f32[24,512]{1,0:T(8,128)S(1)}, f32[24,512]{1,0:T(8,128)S(1)}, u32[]{:S(2)}, u32[]{:S(2)}) %collective-permute-start.1) | collective-permute-done | bytes 49184 | tf_op jit(solution)/shard_map/ppermute | solution.py:284
  17.1 2.8 %collective-permute-start.3 = (f32[24,512]{1,0:T(8,128)S(1)}, f32[24,512]{1,0:T(8,128)S(1)}, u32[]{:S(2)}, u32[]{:S(2)}) collective-permute-start(f32[24,512]{1,0:T(8,128)S(1)} %merge.3.refs_0_), channel_id=1, source_target_pairs={{0,6},{1,7},{2,4},{3,5},{4,2},{5,3},{6,0},{7,1},{8,14},{9,15},{10,... | collective-permute-start | bytes 147464 | tf_op jit(solution)/shard_map/ppermute | solution.py:284
  19.9 0.1 stack.71.place_ref
  20.0 1.7 %collective-permute-done.3.refs_1_ = f32[24,512]{1,0:T(8,128)S(1)} collective-permute-done((f32[24,512]{1,0:T(8,128)S(1)}, f32[24,512]{1,0:T(8,128)S(1)}, u32[]{:S(2)}, u32[]{:S(2)}) %collective-permute-start.3) | collective-permute-done | bytes 49184 | tf_op jit(solution)/shard_map/ppermute | solution.py:284
  21.7 1.2 copy-done.1
  22.9 1.0 copy-done.4
  23.9 4.1 %grads.2 = (bf16[2,512,1024]{2,1,0:T(8,128)(2,1)}, bf16[512,512]{1,0:T(8,128)(2,1)S(1)}, bf16[512,512]{1,0:T(8,128)(2,1)S(1)}, f32[2,128,256]{2,1,0:T(8,128)S(1)}, bf16[2,128,256]{2,1,0:T(8,128)(2,1)S(1)}) custom-call(s32[1]{0:T(128)} %bitcast.13.core_ref, s32[1]{0:T(128)S(6)} %copy.20.length_ref, bf16[256,1024]{1,0:T(8,128)(2,1)S(1)} %bitcast.50, ...), custom_call_target="tpu_custom_call" | custom-call | tf_op jit(solution)/shard_map/grads/pallas_call | solution.py:381
  28.0 0.0 collective-permute-done.18.refs_3_
  28.0 1.0 arrange.1.refs_1_
  29.1 5.7 %collective-permute-start.19 = (bf16[2,256,1024]{2,1,0:T(8,128)(2,1)S(1)}, bf16[2,256,1024]{2,1,0:T(8,128)(2,1)}, u32[]{:S(2)}, u32[]{:S(2)}) collective-permute-start(bf16[2,256,1024]{2,1,0:T(8,128)(2,1)S(1)} %arrange.1.refs_1_), channel_id=1, source_target_pairs={{0,32},{1,225},{2,34},{3,227},{4,36},{5,229},{6,38},{7,231},{8,40}... | collective-permute-start | bytes 3145736 | tf_op jit(solution)/shard_map/ppermute | solution.py:284
  34.7 0.0 copy-start.6
  34.7 4.1 %grads.3 = (bf16[2,512,1024]{2,1,0:T(8,128)(2,1)}, bf16[512,512]{1,0:T(8,128)(2,1)S(1)}, bf16[512,512]{1,0:T(8,128)(2,1)S(1)}, f32[2,128,256]{2,1,0:T(8,128)S(1)}, bf16[2,128,256]{2,1,0:T(8,128)(2,1)S(1)}) custom-call(s32[1]{0:T(128)} %bitcast.13.core_ref, s32[1]{0:T(128)S(6)} %copy.20.length_ref, ...), custom_call_target="tpu_custom_call", output_to_operand_aliasing={{0}: (8, {})} | custom-call | tf_op jit(solution)/shard_map/grads/pallas_call | solution.py:381
  38.9 0.5 collective-permute-start.5
  39.3 0.0 collective-permute-start.6
  39.4 0.5 collective-permute-start.7
  39.8 1.2 collective-permute-done.6.refs_6_
  41.1 0.2 collective-permute-done.7.refs_7_
  41.2 0.0 collective-permute-done.4.refs_2_
  41.3 7.4 %weights.1 = (f32[2,8,64,256]{3,2,1,0:T(8,128)S(1)}, bf16[2,8,64,256]{3,2,1,0:T(8,128)(2,1)S(1)}, f32[2,8,64,256]{3,2,1,0:T(8,128)S(1)}, bf16[2,8,64,256]{3,2,1,...) custom-call(s32[8]{0:T(128)S(1)} %stack.71.place_ref, ...), custom_call_target="tpu_custom_call" | custom-call | tf_op jit(solution)/shard_map/weights/pallas_call | solution.py:436
  48.7 2.8 %collective-permute-start.20 = (bf16[2,256,1024]{2,1,0:T(8,128)(2,1)}, bf16[2,256,1024]{2,1,0:T(8,128)(2,1)}, u32[]{:S(2)}, u32[]{:S(2)}) collective-permute-start(bf16[2,256,1024]{2,1,0:T(8,128)(2,1)} %collective-permute-done.19.refs_2_), channel_id=1, source_target_pairs={{0,32},{1,225},{2,34},{3,227},{4,36},{5,229},{6,38},{7,231},{8,40}... | collective-permute-start | bytes 3145736 | tf_op jit(solution)/shard_map/ppermute | solution.py:284
  51.5 0.1 collective-permute-start.10
  51.6 2.7 %collective-permute-start.11 = (bf16[2,4,144,256]{3,2,1,0:T(8,128)(2,1)S(1)}, bf16[2,4,144,256]{3,2,1,0:T(8,128)(2,1)S(1)}, u32[]{:S(2)}, u32[]{:S(2)}) collective-permute-start(bf16[2,4,144,256]{3,2,1,0:T(8,128)(2,1)S(1)} %get-tuple-element.76), channel_id=1, source_target_pairs={{0,6},{1,7},{2,4},{3,5},{4,2},{5,3},{6,0},{7,1},{8,14},{9,15},{10,... | collective-permute-start | bytes 1769480 | tf_op jit(solution)/shard_map/ppermute | solution.py:284
  54.3 1.1 collective-permute-start.9
  55.4 12.7 %collective-permute-done.8.refs_4_.refs_2_ = bf16[2,8,64,256]{3,2,1,0:T(8,128)(2,1)S(1)} collective-permute-done((bf16[2,8,64,256]{3,2,1,0:T(8,128)(2,1)S(1)}, bf16[2,8,64,256]{3,2,1,0:T(8,128)(2,1)S(1)}, u32[]{:S(2)}, u32[]{:S(2)}) %collective-permute-start.8) | collective-permute-done | bytes 524320 | tf_op jit(solution)/shard_map/ppermute | solution.py:284
  68.1 1.2 collective-permute-done.9.refs_5_.refs_3_
  69.3 0.3 middle.2
  69.6 0.3 collective-permute-start.21
  69.9 2.0 %collective-permute-start.14 = (bf16[4,144,256]{2,1,0:T(8,128)(2,1)S(1)}, bf16[4,144,256]{2,1,0:T(8,128)(2,1)S(1)}, u32[]{:S(2)}, u32[]{:S(2)}) collective-permute-start(bf16[4,144,256]{2,1,0:T(8,128)(2,1)S(1)} %get-tuple-element.85), channel_id=1, source_target_pairs={{0,6},{1,7},{2,4},{3,5},{4,2},{5,3},{6,0},{7,1},{8,14},{9,15},{10,... | collective-permute-start | bytes 884744 | tf_op jit(solution)/shard_map/ppermute | solution.py:284
  71.9 1.1 collective-permute-start.12
  73.0 8.3 %collective-permute-done.12.refs_4_ = bf16[8,64,256]{2,1,0:T(8,128)(2,1)S(1)} collective-permute-done((bf16[8,64,256]{2,1,0:T(8,128)(2,1)S(1)}, bf16[8,64,256]{2,1,0:T(8,128)(2,1)S(1)}, u32[]{:S(2)}, u32[]{:S(2)}) %collective-permute-start.12) | collective-permute-done | bytes 262176 | tf_op jit(solution)/shard_map/ppermute | solution.py:284
  81.3 1.2 %second.1 = (f32[2,8,16,512]{3,2,1,0:T(8,128)S(1)}, bf16[2,8,16,512]{3,2,1,0:T(8,128)(2,1)S(1)}, f32[2,8,16,512]{3,2,1,0:T(8,128)S(1)}, bf16[2,8,16,512]{3,2,1,0:T(8,128)(2,1)S(1)}, f32[4,16,512]{2,1,0:T(8,128)S(1)}) custom-call(s32[8]{0:T(128)S(1)} %stack.71.place_ref, f32[2,8,64,256]{3,2,1,0:T(8,128)S(1)} %get-tuple-element.71.refs_0_, ...), custom_call_target="tpu_custom_call" | custom-call | tf_op jit(solution)/shard_map/second/pallas_call | solution.py:465
  82.5 1.4 %collective-permute-done.21.refs_4_ = bf16[2,256,1024]{2,1,0:T(8,128)(2,1)} collective-permute-done((bf16[2,256,1024]{2,1,0:T(8,128)(2,1)}, bf16[2,256,1024]{2,1,0:T(8,128)(2,1)}, u32[]{:S(2)}, u32[]{:S(2)}) %collective-permute-start.21) | collective-permute-done | bytes 1048608 | tf_op jit(solution)/shard_map/ppermute | solution.py:284
  83.9 1.2 collective-permute-start.26
  85.1 0.6 collective-permute-start.22
  85.7 0.2 collective-permute-start.23
  85.9 5.7 %collective-permute-done.22.refs_2_.refs_1_ = bf16[2,8,16,512]{3,2,1,0:T(8,128)(2,1)S(1)} collective-permute-done((bf16[2,8,16,512]{3,2,1,0:T(8,128)(2,1)S(1)}, bf16[2,8,16,512]{3,2,1,0:T(8,128)(2,1)S(1)}, u32[]{:S(2)}, u32[]{:S(2)}) %collective-permute-start.22) | collective-permute-done | bytes 262176 | tf_op jit(solution)/shard_map/ppermute | solution.py:284
  91.5 0.1 middle.3
  91.6 3.4 %collective-permute-start.24 = (bf16[8,16,512]{2,1,0:T(8,128)(2,1)S(1)}, bf16[8,16,512]{2,1,0:T(8,128)(2,1)S(1)}, u32[]{:S(2)}, u32[]{:S(2)}) collective-permute-start(bf16[8,16,512]{2,1,0:T(8,128)(2,1)S(1)} %get-tuple-element.106), channel_id=1, source_target_pairs={{0,6},{1,7},{2,4},{3,5},{4,2},{5,3},{6,0},{7,1},{8,14},{9,15},{10,... | collective-permute-start | bytes 393224 | tf_op jit(solution)/shard_map/ppermute | solution.py:284
  95.0 1.1 collective-permute-start.25
  96.1 1.6 %collective-permute-done.24.refs_2_ = bf16[8,16,512]{2,1,0:T(8,128)(2,1)S(1)} collective-permute-done((bf16[8,16,512]{2,1,0:T(8,128)(2,1)S(1)}, bf16[8,16,512]{2,1,0:T(8,128)(2,1)S(1)}, u32[]{:S(2)}, u32[]{:S(2)}) %collective-permute-start.24) | collective-permute-done | bytes 131104 | tf_op jit(solution)/shard_map/ppermute | solution.py:284
  97.6 2.7 %collective-permute-done.25.refs_5_ = bf16[8,16,512]{2,1,0:T(8,128)(2,1)S(1)} collective-permute-done((bf16[8,16,512]{2,1,0:T(8,128)(2,1)S(1)}, bf16[8,16,512]{2,1,0:T(8,128)(2,1)S(1)}, u32[]{:S(2)}, u32[]{:S(2)}) %collective-permute-start.25) | collective-permute-done | bytes 131104 | tf_op jit(solution)/shard_map/ppermute | solution.py:284
  100.3 1.0 last.1
  101.3 0.2 copy-done.10
  101.5 2.4 %collective-permute-start.27 = (bf16[2,256,1024]{2,1,0:T(8,128)(2,1)}, bf16[2,256,1024]{2,1,0:T(8,128)(2,1)}, u32[]{:S(2)}, u32[]{:S(2)}) collective-permute-start(bf16[2,256,1024]{2,1,0:T(8,128)(2,1)} %collective-permute-done.19.refs_2_), channel_id=1, source_target_pairs={{0,1},{1,0},{2,3},{3,2},{4,5},{5,4},{6,7},{7,6},{8,9},{9,8},{10,11... | collective-permute-start | bytes 3145736 | tf_op jit(solution)/shard_map/ppermute | solution.py:46
  103.9 0.5 collective-permute-start.29
  104.4 5.9 %all-to-all-start = ((bf16[16,8,1024]{2,1,0:T(8,128)(2,1)}), bf16[16,8,1024]{2,1,0:T(8,128)(2,1)S(1)}, u32[]{:S(2)}, u32[]{:S(2)}) async-start(bf16[16,8,1024]{2,1,0:T(8,128)(2,1)} %bitcast.29), calls=%async_computation | async-start | bytes 524288 | tf_op jit(solution)/shard_map/all_to_all | solution.py:489
  110.2 0.1 stack.80.order_ref
  110.4 0.7 copy.15
  111.1 1.2 copy-done.11
  112.4 8.3 %encoded.1 = bf16[512,2048]{1,0:T(8,128)(2,1)} custom-call(s32[8]{0:T(128)S(1)} %stack.80.order_ref, bf16[2,512,1024]{2,1,0:T(8,128)(2,1)S(1)} %copy-done.7, bf16[2,256,1024]{2,1,0:T(8,128)(2,1)S(1)} %copy-done.9, bf16[2,256,1024]{2,1,0:T(8,128)(2,1)} %collective-permute-done.19.refs_2_, bf16[2,256,1024]{2,1,0:T(8,128)(2,1)} %collective-permute-done.20.refs_3_, ...), custom_call_target="tpu_custom_call" | custom-call | flops 4294967296 | bytes 14680064 | tf_op jit(solution)/shard_map/encoded/pallas_call | solution.py:501
  120.6 1.3 %all-to-all-done = bf16[16,8,1024]{2,1,0:T(8,128)(2,1)S(1)} async-done(((bf16[16,8,1024]{2,1,0:T(8,128)(2,1)}), bf16[16,8,1024]{2,1,0:T(8,128)(2,1)S(1)}, u32[]{:S(2)}, u32[]{:S(2)}) %all-to-all-start) | async-done | bytes 262176 | tf_op jit(solution)/shard_map/all_to_all | solution.py:489
  122.0 0.6 slice_bitcast_fusion
  (42 shorter events, 0.2 us)
Async XLA Ops:
  0.6 21.0 %copy-start.3 = (bf16[1,256,1024]{2,1,0:T(8,128)(2,1)S(1)}, bf16[1,256,1024]{2,1,0:T(8,128)(2,1)}, u32[]{:S(2)}) copy-start(bf16[1,256,1024]{2,1,0:T(8,128)(2,1)} %param.8) | copy-start | bytes 1572868
  0.6 21.0 %copy-start = (bf16[1,512,1024]{2,1,0:T(8,128)(2,1)S(1)}, bf16[1,512,1024]{2,1,0:T(8,128)(2,1)}, u32[]{:S(2)}) copy-start(bf16[1,512,1024]{2,1,0:T(8,128)(2,1)} %param.9) | copy-start | bytes 3145732
  0.7 16.4 %collective-permute-start.2 = (bf16[512,2048]{1,0:T(8,128)(2,1)}, bf16[512,2048]{1,0:T(8,128)(2,1)}, u32[]{:S(2)}, u32[]{:S(2)}) collective-permute-start(bf16[512,2048]{1,0:T(8,128)(2,1)} %bitcast.55), channel_id=1, source_target_pairs={{0,1},{1,0},{2,3},{3,2},{4,5},{5,4},{6,7},{7,6},{8,9},{9,8},{10,11... | collective-permute-start | bytes 6291464 | tf_op jit(solution)/shard_map/ppermute | solution.py:46
  5.0 8.1 %collective-permute-start.16 = (bf16[2,64,1024]{2,1,0:T(8,128)(2,1)S(1)}, bf16[2,64,1024]{2,1,0:T(8,128)(2,1)}, u32[]{:S(2)}, u32[]{:S(2)}) collective-permute-start(bf16[2,64,1024]{2,1,0:T(8,128)(2,1)S(1)} %pad_maximum_fusion.refs_0_), channel_id=1, source_target_pairs={{0,8},{1,9},{2,10},{3,11},{4,12},{5,13},{6,14},{7,15},{8,0},{9,1},... | collective-permute-start | bytes 786440 | tf_op jit(solution)/shard_map/ppermute | solution.py:284
  10.8 1.8 %collective-permute-start = (f32[24,512]{1,0:T(8,128)S(1)}, f32[24,512]{1,0:T(8,128)S(1)}, u32[]{:S(2)}, u32[]{:S(2)}) collective-permute-start(f32[24,512]{1,0:T(8,128)S(1)} %stats.1.left_ref), channel_id=1, source_target_pairs={{0,1},{1,0},{2,3},{3,2},{4,5},{5,4},{6,7},{7,6},{8,9},{9,8},{10,11... | collective-permute-start | bytes 147464 | tf_op jit(solution)/shard_map/ppermute | solution.py:284
  11.0 17.0 %collective-permute-start.17 = (bf16[2,64,1024]{2,1,0:T(8,128)(2,1)S(1)}, bf16[2,64,1024]{2,1,0:T(8,128)(2,1)S(1)}, u32[]{:S(2)}, u32[]{:S(2)}) collective-permute-start(bf16[2,64,1024]{2,1,0:T(8,128)(2,1)S(1)} %pad_maximum_fusion.refs_0_), channel_id=1, source_target_pairs={{0,24},{1,25},{2,26},{3,27},{4,28},{5,29},{6,30},{7,31},{8,16},{9,... | collective-permute-start | bytes 786440 | tf_op jit(solution)/shard_map/ppermute | solution.py:284
  13.1 15.0 %collective-permute-start.18 = (bf16[2,64,1024]{2,1,0:T(8,128)(2,1)}, bf16[2,64,1024]{2,1,0:T(8,128)(2,1)S(1)}, u32[]{:S(2)}, u32[]{:S(2)}) collective-permute-start(bf16[2,64,1024]{2,1,0:T(8,128)(2,1)} %collective-permute-done.16.refs_1_), channel_id=1, source_target_pairs={{0,24},{1,25},{2,26},{3,27},{4,28},{5,29},{6,30},{7,31},{8,16},{9,... | collective-permute-start | bytes 786440 | tf_op jit(solution)/shard_map/ppermute | solution.py:284
  13.8 3.2 %collective-permute-start.1 = (f32[24,512]{1,0:T(8,128)S(1)}, f32[24,512]{1,0:T(8,128)S(1)}, u32[]{:S(2)}, u32[]{:S(2)}) collective-permute-start(f32[24,512]{1,0:T(8,128)S(1)} %merge.2.left_ref), channel_id=1, source_target_pairs={{0,2},{1,3},{2,0},{3,1},{4,6},{5,7},{6,4},{7,5},{8,10},{9,11},{10,... | collective-permute-start | bytes 147464 | tf_op jit(solution)/shard_map/ppermute | solution.py:284
  17.1 4.6 %collective-permute-start.3 = (f32[24,512]{1,0:T(8,128)S(1)}, f32[24,512]{1,0:T(8,128)S(1)}, u32[]{:S(2)}, u32[]{:S(2)}) collective-permute-start(f32[24,512]{1,0:T(8,128)S(1)} %merge.3.refs_0_), channel_id=1, source_target_pairs={{0,6},{1,7},{2,4},{3,5},{4,2},{5,3},{6,0},{7,1},{8,14},{9,15},{10,... | collective-permute-start | bytes 147464 | tf_op jit(solution)/shard_map/ppermute | solution.py:284
  21.7 1.2 %copy-start.1 = (bf16[1,512,1024]{2,1,0:T(8,128)(2,1)S(1)}, bf16[1,512,1024]{2,1,0:T(8,128)(2,1)}, u32[]{:S(2)}) copy-start(bf16[1,512,1024]{2,1,0:T(8,128)(2,1)} %param.10) | copy-start | bytes 3145732
  22.9 1.0 copy-start.4
  23.9 10.8 %copy-start.2 = (bf16[1,512,1024]{2,1,0:T(8,128)(2,1)S(1)}, bf16[1,512,1024]{2,1,0:T(8,128)(2,1)}, u32[]{:S(2)}) copy-start(bf16[1,512,1024]{2,1,0:T(8,128)(2,1)} %param.10) | copy-start | bytes 3145732
  23.9 10.8 %copy-start.5 = (bf16[1,256,1024]{2,1,0:T(8,128)(2,1)S(1)}, bf16[1,256,1024]{2,1,0:T(8,128)(2,1)}, u32[]{:S(2)}) copy-start(bf16[1,256,1024]{2,1,0:T(8,128)(2,1)} %param.14) | copy-start | bytes 1572868
  29.0 9.8 %copy-start.8 = (bf16[2,256,1024]{2,1,0:T(8,128)(2,1)}, bf16[2,256,1024]{2,1,0:T(8,128)(2,1)S(1)}, u32[]{:S(2)}) copy-start(bf16[2,256,1024]{2,1,0:T(8,128)(2,1)S(1)} %arrange.1.refs_1_) | copy-start | bytes 3145732
  29.1 19.6 %collective-permute-start.19 = (bf16[2,256,1024]{2,1,0:T(8,128)(2,1)S(1)}, bf16[2,256,1024]{2,1,0:T(8,128)(2,1)}, u32[]{:S(2)}, u32[]{:S(2)}) collective-permute-start(bf16[2,256,1024]{2,1,0:T(8,128)(2,1)S(1)} %arrange.1.refs_1_), channel_id=1, source_target_pairs={{0,32},{1,225},{2,34},{3,227},{4,36},{5,229},{6,38},{7,231},{8,40}... | collective-permute-start | bytes 3145736 | tf_op jit(solution)/shard_map/ppermute | solution.py:284
  34.7 6.5 %collective-permute-start.4 = (bf16[512,512]{1,0:T(8,128)(2,1)S(1)}, bf16[512,512]{1,0:T(8,128)(2,1)S(1)}, u32[]{:S(2)}, u32[]{:S(2)}) collective-permute-start(bf16[512,512]{1,0:T(8,128)(2,1)S(1)} %get-tuple-element.65), channel_id=1, source_target_pairs={{0,1},{1,0},{2,3},{3,2},{4,5},{5,4},{6,7},{7,6},{8,9},{9,8},{10,11... | collective-permute-start | bytes 1572872 | tf_op jit(solution)/shard_map/ppermute | solution.py:46
  34.7 6.5 %copy-start.6 = (bf16[1,512,2048]{2,1,0:T(8,128)(2,1)S(1)}, bf16[1,512,2048]{2,1,0:T(8,128)(2,1)}, u32[]{:S(2)}) copy-start(bf16[1,512,2048]{2,1,0:T(8,128)(2,1)} %param.11) | copy-start | bytes 6291460
  38.9 2.4 %collective-permute-start.5 = (bf16[512,512]{1,0:T(8,128)(2,1)S(1)}, bf16[512,512]{1,0:T(8,128)(2,1)S(1)}, u32[]{:S(2)}, u32[]{:S(2)}) collective-permute-start(bf16[512,512]{1,0:T(8,128)(2,1)S(1)} %get-tuple-element.66), channel_id=1, source_target_pairs={{0,1},{1,0},{2,3},{3,2},{4,5},{5,4},{6,7},{7,6},{8,9},{9,8},{10,11... | collective-permute-start | bytes 1572872 | tf_op jit(solution)/shard_map/ppermute | solution.py:46
  39.3 1.7 %collective-permute-start.6 = (bf16[2,128,256]{2,1,0:T(8,128)(2,1)S(1)}, bf16[2,128,256]{2,1,0:T(8,128)(2,1)S(1)}, u32[]{:S(2)}, u32[]{:S(2)}) collective-permute-start(bf16[2,128,256]{2,1,0:T(8,128)(2,1)S(1)} %get-tuple-element.69), channel_id=1, source_target_pairs={{0,1},{1,0},{2,3},{3,2},{4,5},{5,4},{6,7},{7,6},{8,9},{9,8},{10,11... | collective-permute-start | bytes 393224 | tf_op jit(solution)/shard_map/ppermute | solution.py:46
  39.4 1.9 %collective-permute-start.7 = (bf16[2,128,256]{2,1,0:T(8,128)(2,1)S(1)}, bf16[2,128,256]{2,1,0:T(8,128)(2,1)S(1)}, u32[]{:S(2)}, u32[]{:S(2)}) collective-permute-start(bf16[2,128,256]{2,1,0:T(8,128)(2,1)S(1)} %get-tuple-element.70), channel_id=1, source_target_pairs={{0,1},{1,0},{2,3},{3,2},{4,5},{5,4},{6,7},{7,6},{8,9},{9,8},{10,11... | collective-permute-start | bytes 393224 | tf_op jit(solution)/shard_map/ppermute | solution.py:46
  48.7 20.9 %collective-permute-start.20 = (bf16[2,256,1024]{2,1,0:T(8,128)(2,1)}, bf16[2,256,1024]{2,1,0:T(8,128)(2,1)}, u32[]{:S(2)}, u32[]{:S(2)}) collective-permute-start(bf16[2,256,1024]{2,1,0:T(8,128)(2,1)} %collective-permute-done.19.refs_2_), channel_id=1, source_target_pairs={{0,32},{1,225},{2,34},{3,227},{4,36},{5,229},{6,38},{7,231},{8,40}... | collective-permute-start | bytes 3145736 | tf_op jit(solution)/shard_map/ppermute | solution.py:284
  51.5 17.8 %collective-permute-start.10 = (bf16[2,4,144,256]{3,2,1,0:T(8,128)(2,1)S(1)}, bf16[2,4,144,256]{3,2,1,0:T(8,128)(2,1)S(1)}, u32[]{:S(2)}, u32[]{:S(2)}) collective-permute-start(bf16[2,4,144,256]{3,2,1,0:T(8,128)(2,1)S(1)} %get-tuple-element.75), channel_id=1, source_target_pairs={{0,2},{1,3},{2,0},{3,1},{4,6},{5,7},{6,4},{7,5},{8,10},{9,11},{10,... | collective-permute-start | bytes 1769480 | tf_op jit(solution)/shard_map/ppermute | solution.py:284
  51.6 17.7 %collective-permute-start.11 = (bf16[2,4,144,256]{3,2,1,0:T(8,128)(2,1)S(1)}, bf16[2,4,144,256]{3,2,1,0:T(8,128)(2,1)S(1)}, u32[]{:S(2)}, u32[]{:S(2)}) collective-permute-start(bf16[2,4,144,256]{3,2,1,0:T(8,128)(2,1)S(1)} %get-tuple-element.76), channel_id=1, source_target_pairs={{0,6},{1,7},{2,4},{3,5},{4,2},{5,3},{6,0},{7,1},{8,14},{9,15},{10,... | collective-permute-start | bytes 1769480 | tf_op jit(solution)/shard_map/ppermute | solution.py:284
  54.3 13.8 %collective-permute-start.8 = (bf16[2,8,64,256]{3,2,1,0:T(8,128)(2,1)S(1)}, bf16[2,8,64,256]{3,2,1,0:T(8,128)(2,1)S(1)}, u32[]{:S(2)}, u32[]{:S(2)}) collective-permute-start(bf16[2,8,64,256]{3,2,1,0:T(8,128)(2,1)S(1)} %get-tuple-element.73), channel_id=1, source_target_pairs={{0,8},{1,9},{2,10},{3,11},{4,12},{5,13},{6,14},{7,15},{8,0},{9,1},... | collective-permute-start | bytes 1572872 | tf_op jit(solution)/shard_map/ppermute | solution.py:284
  54.3 15.0 %collective-permute-start.9 = (bf16[2,8,64,256]{3,2,1,0:T(8,128)(2,1)S(1)}, bf16[2,8,64,256]{3,2,1,0:T(8,128)(2,1)S(1)}, u32[]{:S(2)}, u32[]{:S(2)}) collective-permute-start(bf16[2,8,64,256]{3,2,1,0:T(8,128)(2,1)S(1)} %get-tuple-element.74), channel_id=1, source_target_pairs={{0,24},{1,25},{2,26},{3,27},{4,28},{5,29},{6,30},{7,31},{8,16},{9,... | collective-permute-start | bytes 1572872 | tf_op jit(solution)/shard_map/ppermute | solution.py:284
  69.6 14.3 %collective-permute-start.21 = (bf16[2,256,1024]{2,1,0:T(8,128)(2,1)}, bf16[2,256,1024]{2,1,0:T(8,128)(2,1)}, u32[]{:S(2)}, u32[]{:S(2)}) collective-permute-start(bf16[2,256,1024]{2,1,0:T(8,128)(2,1)} %collective-permute-done.20.refs_3_), channel_id=1, source_target_pairs={{0,32},{1,225},{2,34},{3,227},{4,36},{5,229},{6,38},{7,231},{8,40}... | collective-permute-start | bytes 3145736 | tf_op jit(solution)/shard_map/ppermute | solution.py:284
  69.9 11.3 %collective-permute-start.14 = (bf16[4,144,256]{2,1,0:T(8,128)(2,1)S(1)}, bf16[4,144,256]{2,1,0:T(8,128)(2,1)S(1)}, u32[]{:S(2)}, u32[]{:S(2)}) collective-permute-start(bf16[4,144,256]{2,1,0:T(8,128)(2,1)S(1)} %get-tuple-element.85), channel_id=1, source_target_pairs={{0,6},{1,7},{2,4},{3,5},{4,2},{5,3},{6,0},{7,1},{8,14},{9,15},{10,... | collective-permute-start | bytes 884744 | tf_op jit(solution)/shard_map/ppermute | solution.py:284
  71.9 9.4 %collective-permute-start.15 = (bf16[4,144,256]{2,1,0:T(8,128)(2,1)S(1)}, bf16[4,144,256]{2,1,0:T(8,128)(2,1)S(1)}, u32[]{:S(2)}, u32[]{:S(2)}) collective-permute-start(bf16[4,144,256]{2,1,0:T(8,128)(2,1)S(1)} %get-tuple-element.86), channel_id=1, source_target_pairs={{0,2},{1,3},{2,0},{3,1},{4,6},{5,7},{6,4},{7,5},{8,10},{9,11},{10,... | collective-permute-start | bytes 884744 | tf_op jit(solution)/shard_map/ppermute | solution.py:284
  71.9 9.4 %collective-permute-start.12 = (bf16[8,64,256]{2,1,0:T(8,128)(2,1)S(1)}, bf16[8,64,256]{2,1,0:T(8,128)(2,1)S(1)}, u32[]{:S(2)}, u32[]{:S(2)}) collective-permute-start(bf16[8,64,256]{2,1,0:T(8,128)(2,1)S(1)} %get-tuple-element.83), channel_id=1, source_target_pairs={{0,24},{1,25},{2,26},{3,27},{4,28},{5,29},{6,30},{7,31},{8,16},{9,... | collective-permute-start | bytes 786440 | tf_op jit(solution)/shard_map/ppermute | solution.py:284
  73.0 8.3 %collective-permute-start.13 = (bf16[8,64,256]{2,1,0:T(8,128)(2,1)S(1)}, bf16[8,64,256]{2,1,0:T(8,128)(2,1)S(1)}, u32[]{:S(2)}, u32[]{:S(2)}) collective-permute-start(bf16[8,64,256]{2,1,0:T(8,128)(2,1)S(1)} %get-tuple-element.84), channel_id=1, source_target_pairs={{0,8},{1,9},{2,10},{3,11},{4,12},{5,13},{6,14},{7,15},{8,0},{9,1},... | collective-permute-start | bytes 786440 | tf_op jit(solution)/shard_map/ppermute | solution.py:284
  83.9 16.4 %collective-permute-start.26 = (bf16[2,256,1024]{2,1,0:T(8,128)(2,1)}, bf16[2,256,1024]{2,1,0:T(8,128)(2,1)S(1)}, u32[]{:S(2)}, u32[]{:S(2)}) collective-permute-start(bf16[2,256,1024]{2,1,0:T(8,128)(2,1)} %collective-permute-done.21.refs_4_), channel_id=1, source_target_pairs={{0,32},{1,225},{2,34},{3,227},{4,36},{5,229},{6,38},{7,231},{8,40}... | collective-permute-start | bytes 3145736 | tf_op jit(solution)/shard_map/ppermute | solution.py:284
  85.1 6.4 %collective-permute-start.22 = (bf16[2,8,16,512]{3,2,1,0:T(8,128)(2,1)S(1)}, bf16[2,8,16,512]{3,2,1,0:T(8,128)(2,1)S(1)}, u32[]{:S(2)}, u32[]{:S(2)}) collective-permute-start(bf16[2,8,16,512]{3,2,1,0:T(8,128)(2,1)S(1)} %get-tuple-element.101), channel_id=1, source_target_pairs={{0,2},{1,3},{2,0},{3,1},{4,6},{5,7},{6,4},{7,5},{8,10},{9,11},{10,... | collective-permute-start | bytes 786440 | tf_op jit(solution)/shard_map/ppermute | solution.py:284
  85.7 5.8 %collective-permute-start.23 = (bf16[2,8,16,512]{3,2,1,0:T(8,128)(2,1)S(1)}, bf16[2,8,16,512]{3,2,1,0:T(8,128)(2,1)S(1)}, u32[]{:S(2)}, u32[]{:S(2)}) collective-permute-start(bf16[2,8,16,512]{3,2,1,0:T(8,128)(2,1)S(1)} %get-tuple-element.102), channel_id=1, source_target_pairs={{0,8},{1,9},{2,10},{3,11},{4,12},{5,13},{6,14},{7,15},{8,0},{9,1},... | collective-permute-start | bytes 786440 | tf_op jit(solution)/shard_map/ppermute | solution.py:284
  91.5 19.6 %copy-start.7 = (bf16[2,512,1024]{2,1,0:T(8,128)(2,1)S(1)}, bf16[2,512,1024]{2,1,0:T(8,128)(2,1)}, u32[]{:S(2)}) copy-start(bf16[2,512,1024]{2,1,0:T(8,128)(2,1)} %get-tuple-element.92.refs_0_) | copy-start | bytes 6291460
  91.5 19.6 %copy-start.9 = (bf16[2,256,1024]{2,1,0:T(8,128)(2,1)S(1)}, bf16[2,256,1024]{2,1,0:T(8,128)(2,1)}, u32[]{:S(2)}) copy-start(bf16[2,256,1024]{2,1,0:T(8,128)(2,1)} %copy-done.8) | copy-start | bytes 3145732
  91.6 6.0 %collective-permute-start.24 = (bf16[8,16,512]{2,1,0:T(8,128)(2,1)S(1)}, bf16[8,16,512]{2,1,0:T(8,128)(2,1)S(1)}, u32[]{:S(2)}, u32[]{:S(2)}) collective-permute-start(bf16[8,16,512]{2,1,0:T(8,128)(2,1)S(1)} %get-tuple-element.106), channel_id=1, source_target_pairs={{0,6},{1,7},{2,4},{3,5},{4,2},{5,3},{6,0},{7,1},{8,14},{9,15},{10,... | collective-permute-start | bytes 393224 | tf_op jit(solution)/shard_map/ppermute | solution.py:284
  95.0 5.3 %collective-permute-start.25 = (bf16[8,16,512]{2,1,0:T(8,128)(2,1)S(1)}, bf16[8,16,512]{2,1,0:T(8,128)(2,1)S(1)}, u32[]{:S(2)}, u32[]{:S(2)}) collective-permute-start(bf16[8,16,512]{2,1,0:T(8,128)(2,1)S(1)} %get-tuple-element.107), channel_id=1, source_target_pairs={{0,24},{1,25},{2,26},{3,27},{4,28},{5,29},{6,30},{7,31},{8,16},{9,... | collective-permute-start | bytes 393224 | tf_op jit(solution)/shard_map/ppermute | solution.py:284
  100.3 1.1 copy-start.10
  101.5 9.6 %collective-permute-start.27 = (bf16[2,256,1024]{2,1,0:T(8,128)(2,1)}, bf16[2,256,1024]{2,1,0:T(8,128)(2,1)}, u32[]{:S(2)}, u32[]{:S(2)}) collective-permute-start(bf16[2,256,1024]{2,1,0:T(8,128)(2,1)} %collective-permute-done.19.refs_2_), channel_id=1, source_target_pairs={{0,1},{1,0},{2,3},{3,2},{4,5},{5,4},{6,7},{7,6},{8,9},{9,8},{10,11... | collective-permute-start | bytes 3145736 | tf_op jit(solution)/shard_map/ppermute | solution.py:46
  103.9 7.2 %collective-permute-start.28 = (bf16[2,256,1024]{2,1,0:T(8,128)(2,1)}, bf16[2,256,1024]{2,1,0:T(8,128)(2,1)}, u32[]{:S(2)}, u32[]{:S(2)}) collective-permute-start(bf16[2,256,1024]{2,1,0:T(8,128)(2,1)} %collective-permute-done.20.refs_3_), channel_id=1, source_target_pairs={{0,1},{1,0},{2,3},{3,2},{4,5},{5,4},{6,7},{7,6},{8,9},{9,8},{10,11... | collective-permute-start | bytes 3145736 | tf_op jit(solution)/shard_map/ppermute | solution.py:46
  103.9 7.2 %collective-permute-start.29 = (bf16[2,256,1024]{2,1,0:T(8,128)(2,1)}, bf16[2,256,1024]{2,1,0:T(8,128)(2,1)}, u32[]{:S(2)}, u32[]{:S(2)}) collective-permute-start(bf16[2,256,1024]{2,1,0:T(8,128)(2,1)} %collective-permute-done.21.refs_4_), channel_id=1, source_target_pairs={{0,1},{1,0},{2,3},{3,2},{4,5},{5,4},{6,7},{7,6},{8,9},{9,8},{10,11... | collective-permute-start | bytes 3145736 | tf_op jit(solution)/shard_map/ppermute | solution.py:46
  104.4 17.6 %all-to-all-start = ((bf16[16,8,1024]{2,1,0:T(8,128)(2,1)}), bf16[16,8,1024]{2,1,0:T(8,128)(2,1)S(1)}, u32[]{:S(2)}, u32[]{:S(2)}) async-start(bf16[16,8,1024]{2,1,0:T(8,128)(2,1)} %bitcast.29), calls=%async_computation | async-start | bytes 524288 | tf_op jit(solution)/shard_map/all_to_all | solution.py:489
  111.1 1.2 copy-start.11
